TPU v7x, 32 devices: a whole 2x2x4 slice. The times are simulated.
32 devices in a mesh: expert: 8 (over y, x, core), wshard: 4 (over z).
Axes of the slice: x: 2, y: 2, z: 4, core: 2. Of those that a mesh axis runs over, the one named last changes fastest.
Arguments:
- tokens: bfloat16 [8192, 768], P(('expert', 'wshard')), may hold values from -6 to 6
- norm_gain_attn: bfloat16 [768], P('wshard'), may hold values from 0.099609375 to 1.8984375
- w_query: bfloat16 [768, 768], P('wshard'), may hold values from -0.21875 to 0.21875
- w_key: bfloat16 [768, 768], P('wshard'), may hold values from -0.21875 to 0.21875
- w_value: bfloat16 [768, 768], P('wshard'), may hold values from -0.21875 to 0.21875
- w_output: bfloat16 [768, 768], P('wshard'), may hold values from -1.75 to 1.75
- rel_bias: bfloat16 [32, 12], P('wshard'), may hold values from -4 to 4
- norm_gain_ffn: bfloat16 [768], P('wshard'), may hold values from 0.099609375 to 1.8984375
- w_router: bfloat16 [768, 8], P('wshard'), may hold values from -0.109375 to 0.109375
- w_in: bfloat16 [8, 768, 3072], P('expert', None, 'wshard'), may hold values from -0.21875 to 0.21875
- w_out: bfloat16 [8, 3072, 768], P('expert', 'wshard'), may hold values from -1.25 to 1.25
- out_grad: bfloat16 [8192, 768], P(('expert', 'wshard')), may hold values from -6 to 6
- expert_ids: int32 [8192, 1], P(('expert', 'wshard')), may hold values from 0 to 7
- priority: int32 [8192], P(('expert', 'wshard')), may hold values from 0 to 255, as said below
- lengths: int32 [64], replicated, may hold values from 0 to 256, as said below
- seq_order: int32 [64], replicated, may hold values from 0 to 63, as said below
- relpos_table: int32 [511], replicated, may hold values from 0 to 31, as said below
Outputs:
- layer_out: bfloat16 [8192, 768], P(('expert', 'wshard'))
- tokens_grad: float32 [8192, 768], P(('expert', 'wshard'))
- grad_gain_attn: float32 [768], P('wshard')
- grad_query: float32 [768, 768], P('wshard')
- grad_key: float32 [768, 768], P('wshard')
- grad_value: float32 [768, 768], P('wshard')
- grad_output: float32 [768, 768], P('wshard')
- grad_rel_bias: float32 [32, 12], P('wshard')
- grad_gain_ffn: float32 [768], P('wshard')
- grad_router: float32 [768, 8], P('wshard')
- grad_w_in: float32 [8, 768, 3072], P('expert', None, 'wshard')
- grad_w_out: float32 [8, 3072, 768], P('expert', 'wshard')
Inputs may be any that keep to these rules, and one draw needn't show every extreme that they name: `priority`: within each block of 256 rows, the priorities are a permutation of 0 to 255. The two lengths dealt to one device (256 / 8) sum to at most 256; some device holds one sequence of 256 tokens and an empty second one. A permutation of all sequence numbers; device d holds sequences seq_order[2 d] and seq_order[2 d + 1], packed in that order from its first row. `relpos_table`: offsets at or below zero have buckets under 32 / 2, offsets above zero have buckets of 16 or more; buckets never fall as the distance grows.
All inputs are finite; a program needn't handle non-finite values.
Results may differ from a plain program's by a relative error of at most 0.014.
Values may be sent and summed in bfloat16 or wider, within the bound.
A program may use at most 128 MiB of HBM per device.

v0:
```python
import jax
import jax.numpy as jnp
from jax import lax
from jax.sharding import PartitionSpec as P

EPSILON = 1e-06
NEG_FILL = -1e30
ROW_BLOCK = 512


def rms_scale(field):
    return lax.rsqrt(jnp.mean(field * field, axis=-1, keepdims=True) + EPSILON)


def device_layout(lengths, seq_order, device, tok_count):
    first = lengths[seq_order[2 * device]]
    second = lengths[seq_order[2 * device + 1]]
    places = jnp.arange(tok_count, dtype=jnp.int32)
    segment = (places >= first).astype(jnp.int32) + (places >= first + second).astype(jnp.int32)
    valid = (places < first + second).astype(jnp.float32)
    return (segment, valid)


def slot_layout(expert_rows, priority, valid, n_experts, capacity):
    chosen = (expert_rows[:, None] == jnp.arange(n_experts, dtype=jnp.int32)[None, :]).astype(
        jnp.int32
    )
    chosen = chosen * (valid[:, None] > 0).astype(jnp.int32)
    ranked = jnp.zeros_like(chosen).at[priority].set(chosen)
    before = jnp.cumsum(ranked, axis=0, dtype=jnp.int32) - ranked
    slot = jnp.sum(before[priority] * chosen, axis=1, dtype=jnp.int32)
    keep = (jnp.sum(chosen, axis=1, dtype=jnp.int32) > 0) & (slot < capacity)
    flat = jnp.where(keep, expert_rows * capacity + slot, n_experts * capacity)
    return (flat, keep.astype(jnp.float32))


def norm_backward(grad, field, scale, gain):
    gain_grad = jnp.sum(grad * field * scale, axis=0)
    direct = grad * gain
    field_grad = scale * direct - field * scale**3 * jnp.mean(
        direct * field, axis=-1, keepdims=True
    )
    return (field_grad, gain_grad)


def gelu_tanh(field):
    return jax.nn.gelu(field, approximate=True)


def block_offsets(tok_count, begin):
    places = jnp.arange(tok_count, dtype=jnp.int32)
    return places[None, :] - (begin + places)[:, None] + tok_count - 1


def score_block(query_rows, keys, bias_offsets, segment, begin, scale):
    tok_count = keys.shape[0]
    raw = jnp.einsum("qhd,khd->hqk", query_rows, keys, preferred_element_type=jnp.float32) * scale
    offsets = block_offsets(tok_count, begin)
    looked = jnp.take(bias_offsets, offsets, axis=1)
    same = segment[:, None] == segment[None, :]
    return jnp.where(same[None], raw + looked, NEG_FILL)


def fill_buffer(rows, flat, n_experts, capacity):
    width = rows.shape[1]
    buffer = jnp.zeros((n_experts * capacity + 1, width), rows.dtype).at[flat].set(rows)
    return buffer[: n_experts * capacity].reshape(n_experts, capacity, width)


def read_buffer(buffer, flat, keep):
    n_experts, capacity, width = buffer.shape
    picked = buffer.reshape(n_experts * capacity, width)[
        jnp.minimum(flat, n_experts * capacity - 1)
    ]
    return picked.astype(jnp.float32) * keep[:, None]


def to_rows(buffer, source_count, local_experts):
    total, capacity, width = buffer.shape
    shaped = buffer.reshape(source_count, local_experts, capacity, width).transpose(0, 2, 1, 3)
    return shaped.reshape(source_count * capacity, local_experts, width)


def to_buffer(rows, source_count, local_experts):
    total, experts_here, width = rows.shape
    capacity = total // source_count
    shaped = rows.reshape(source_count, capacity, local_experts, width).transpose(0, 2, 1, 3)
    return shaped.reshape(source_count * local_experts, capacity, width)


def local(
    tokens,
    norm_gain_attn,
    w_query,
    w_key,
    w_value,
    w_output,
    rel_bias,
    norm_gain_ffn,
    w_router,
    w_in,
    w_out,
    out_grad,
    expert_ids,
    priority,
    lengths,
    seq_order,
    relpos_table,
):
    tok_count, width = tokens.shape
    shard_count = lax.axis_size("wshard")
    source_count = lax.axis_size("expert")
    n_heads = rel_bias.shape[1]
    head_dim = width // n_heads
    n_buckets = rel_bias.shape[0] * shard_count
    n_experts = w_router.shape[1]
    local_experts = w_in.shape[0]
    capacity = tok_count // n_experts
    scale = head_dim ** (-0.5)
    device = lax.axis_index("expert") * shard_count + lax.axis_index("wshard")
    segment, valid = device_layout(lengths, seq_order, device, tok_count)
    expert_rows = expert_ids[:, 0]
    bucket_range = jnp.arange(n_buckets, dtype=jnp.int32)
    mixer_shards = (
        norm_gain_attn,
        w_query,
        w_key,
        w_value,
        w_output,
        rel_bias,
        norm_gain_ffn,
        w_router,
    )
    gain_attn, full_query, full_key, full_value, full_output, full_bias, gain_ffn, full_router = (
        lax.all_gather(mixer_shards[0], "wshard", axis=0, tiled=True),
        lax.all_gather(mixer_shards[1], "wshard", axis=0, tiled=True),
        lax.all_gather(mixer_shards[2], "wshard", axis=0, tiled=True),
        lax.all_gather(mixer_shards[3], "wshard", axis=0, tiled=True),
        lax.all_gather(mixer_shards[4], "wshard", axis=0, tiled=True),
        lax.all_gather(mixer_shards[5], "wshard", axis=0, tiled=True),
        lax.all_gather(mixer_shards[6], "wshard", axis=0, tiled=True),
        lax.all_gather(mixer_shards[7], "wshard", axis=0, tiled=True),
    )
    table_hot = (relpos_table[:, None] == bucket_range[None, :]).astype(jnp.bfloat16)
    bias_offsets = jnp.dot(table_hot, full_bias, preferred_element_type=jnp.float32).T
    hidden_in = tokens.astype(jnp.float32)
    scale_attn = rms_scale(hidden_in)
    normed = (hidden_in * scale_attn * gain_attn.astype(jnp.float32)).astype(jnp.bfloat16)
    query = (
        jnp.dot(normed, full_query, preferred_element_type=jnp.float32)
        .astype(jnp.bfloat16)
        .reshape(tok_count, n_heads, head_dim)
    )
    keys = (
        jnp.dot(normed, full_key, preferred_element_type=jnp.float32)
        .astype(jnp.bfloat16)
        .reshape(tok_count, n_heads, head_dim)
    )
    values = (
        jnp.dot(normed, full_value, preferred_element_type=jnp.float32)
        .astype(jnp.bfloat16)
        .reshape(tok_count, n_heads, head_dim)
    )
    block_rows = min(ROW_BLOCK, tok_count)
    begin = 0
    scores = score_block(query, keys, bias_offsets, segment, begin, scale)
    top = jnp.max(scores, axis=-1, keepdims=True)
    expo = jnp.exp(scores - top)
    total = jnp.sum(expo, axis=-1, keepdims=True)
    probs_low = (expo / total).astype(jnp.bfloat16)
    mixed_parts = jnp.einsum("hqk,khd->qhd", probs_low, values, preferred_element_type=jnp.float32)
    log_totals = [top + jnp.log(total)]
    mixed = mixed_parts.reshape(tok_count, width).astype(jnp.bfloat16)
    attended = jnp.dot(mixed, full_output, preferred_element_type=jnp.float32) * valid[:, None]
    middle = hidden_in + attended
    scale_ffn = rms_scale(middle)
    normed_ffn = (middle * scale_ffn * gain_ffn.astype(jnp.float32)).astype(jnp.bfloat16)
    logits = jnp.dot(normed_ffn, full_router, preferred_element_type=jnp.float32)
    router = jax.nn.softmax(logits, axis=-1)
    picked = (expert_rows[:, None] == jnp.arange(n_experts, dtype=jnp.int32)[None, :]).astype(
        jnp.float32
    )
    gate = jnp.sum(router * picked, axis=1)
    flat, keep = slot_layout(expert_rows, priority, valid, n_experts, capacity)
    dispatch_buffer = fill_buffer(normed_ffn, flat, n_experts, capacity)
    received = lax.all_to_all(dispatch_buffer, "expert", split_axis=0, concat_axis=0, tiled=True)
    rows_local = to_rows(received, source_count, local_experts)
    rows_all = lax.all_gather(rows_local, "wshard", axis=0, tiled=True)
    inner = jnp.einsum("rxd,xdf->rxf", rows_all, w_in, preferred_element_type=jnp.float32)
    active = gelu_tanh(inner).astype(jnp.bfloat16)
    part = active
    result_rows = lax.psum_scatter(
        jnp.einsum("rxf,xfd->rxd", part, w_out, preferred_element_type=jnp.float32),
        "wshard",
        scatter_dimension=0,
        tiled=True,
    ).astype(jnp.bfloat16)
    returned = lax.all_to_all(
        to_buffer(result_rows, source_count, local_experts),
        "expert",
        split_axis=0,
        concat_axis=0,
        tiled=True,
    )
    result_tok = read_buffer(returned, flat, keep)
    layer_out = (middle + (keep * gate)[:, None] * result_tok).astype(jnp.bfloat16)
    upstream = out_grad.astype(jnp.float32)
    result_grad = ((keep * gate)[:, None] * upstream).astype(jnp.bfloat16)
    gate_grad = keep * jnp.sum(upstream * result_tok, axis=1)
    logit_grad = ((gate * gate_grad)[:, None] * (picked - router)).astype(jnp.bfloat16)
    grad_buffer = fill_buffer(result_grad, flat, n_experts, capacity)
    grad_received = lax.all_to_all(grad_buffer, "expert", split_axis=0, concat_axis=0, tiled=True)
    grad_local = to_rows(grad_received, source_count, local_experts)
    grad_all = lax.all_gather(grad_local, "wshard", axis=0, tiled=True)
    active_grad = jnp.einsum("rxd,xfd->rxf", grad_all, w_out, preferred_element_type=jnp.float32)
    inner_value, gelu_back = jax.vjp(gelu_tanh, inner)
    inner_grad = gelu_back(active_grad)[0].astype(jnp.bfloat16)
    grad_w_out = jnp.einsum("rxf,rxd->xfd", active, grad_all, preferred_element_type=jnp.float32)
    grad_w_in = jnp.einsum("rxd,rxf->xdf", rows_all, inner_grad, preferred_element_type=jnp.float32)
    part = inner_grad
    sent_rows = lax.psum_scatter(
        jnp.einsum("rxf,xdf->rxd", part, w_in, preferred_element_type=jnp.float32),
        "wshard",
        scatter_dimension=0,
        tiled=True,
    ).astype(jnp.bfloat16)
    sent_back = lax.all_to_all(
        to_buffer(sent_rows, source_count, local_experts),
        "expert",
        split_axis=0,
        concat_axis=0,
        tiled=True,
    )
    sent_grad = read_buffer(sent_back, flat, keep)
    gain_attn, full_query, full_key, full_value, full_output, full_bias, gain_ffn, full_router = (
        lax.all_gather(mixer_shards[0], "wshard", axis=0, tiled=True),
        lax.all_gather(mixer_shards[1], "wshard", axis=0, tiled=True),
        lax.all_gather(mixer_shards[2], "wshard", axis=0, tiled=True),
        lax.all_gather(mixer_shards[3], "wshard", axis=0, tiled=True),
        lax.all_gather(mixer_shards[4], "wshard", axis=0, tiled=True),
        lax.all_gather(mixer_shards[5], "wshard", axis=0, tiled=True),
        lax.all_gather(mixer_shards[6], "wshard", axis=0, tiled=True),
        lax.all_gather(mixer_shards[7], "wshard", axis=0, tiled=True),
    )
    grad_router = jnp.dot(normed_ffn.T, logit_grad, preferred_element_type=jnp.float32)
    normed_ffn_grad = (
        jnp.dot(logit_grad, full_router.T, preferred_element_type=jnp.float32) + sent_grad
    )
    middle_norm_grad, grad_gain_ffn = norm_backward(
        normed_ffn_grad, middle, scale_ffn, gain_ffn.astype(jnp.float32)
    )
    middle_grad = upstream + middle_norm_grad
    attended_grad = (middle_grad * valid[:, None]).astype(jnp.bfloat16)
    grad_output = jnp.dot(mixed.T, attended_grad, preferred_element_type=jnp.float32)
    mixed_grad = (
        jnp.dot(attended_grad, full_output.T, preferred_element_type=jnp.float32)
        .astype(jnp.bfloat16)
        .reshape(tok_count, n_heads, head_dim)
    )
    query_parts = []
    keys_grad = jnp.zeros((tok_count, n_heads, head_dim), jnp.float32)
    values_grad = jnp.zeros((tok_count, n_heads, head_dim), jnp.float32)
    bias_grad_heads = jnp.zeros((n_heads, n_buckets), jnp.float32)
    for number, begin in enumerate(range(0, tok_count, block_rows)):
        rows = query.shape[0]
        scores = score_block(query, keys, bias_offsets, segment, begin, scale)
        probs = jnp.exp(scores - log_totals[number])
        prob_grad = jnp.einsum(
            "qhd,khd->hqk", mixed_grad, values, preferred_element_type=jnp.float32
        )
        score_grad = (
            probs * (prob_grad - jnp.sum(probs * prob_grad, axis=-1, keepdims=True))
        ).astype(jnp.bfloat16)
        query_parts.append(
            jnp.einsum("hqk,khd->qhd", score_grad, keys, preferred_element_type=jnp.float32) * scale
        )
        keys_grad = (
            jnp.einsum("hqk,qhd->khd", score_grad, query, preferred_element_type=jnp.float32)
            * scale
        )
        values_grad = jnp.einsum(
            "hqk,qhd->khd",
            probs.astype(jnp.bfloat16),
            mixed_grad,
            preferred_element_type=jnp.float32,
        )
        buckets = relpos_table[block_offsets(tok_count, begin)].reshape(rows * tok_count)
        bucket_hot = (buckets[:, None] == bucket_range[None, :]).astype(jnp.bfloat16)
        bias_grad_heads = jnp.dot(
            score_grad.reshape(n_heads, rows * tok_count),
            bucket_hot,
            preferred_element_type=jnp.float32,
        )
    query_grad = query_parts[0].reshape(tok_count, width).astype(jnp.bfloat16)
    keys_grad = keys_grad.reshape(tok_count, width).astype(jnp.bfloat16)
    values_grad = values_grad.reshape(tok_count, width).astype(jnp.bfloat16)
    grad_rel_bias = bias_grad_heads.T
    grad_query = jnp.dot(normed.T, query_grad, preferred_element_type=jnp.float32)
    grad_key = jnp.dot(normed.T, keys_grad, preferred_element_type=jnp.float32)
    grad_value = jnp.dot(normed.T, values_grad, preferred_element_type=jnp.float32)
    normed_grad = jnp.dot(query_grad, full_query.T, preferred_element_type=jnp.float32)
    normed_grad = normed_grad + jnp.dot(keys_grad, full_key.T, preferred_element_type=jnp.float32)
    normed_grad = normed_grad + jnp.dot(
        values_grad, full_value.T, preferred_element_type=jnp.float32
    )
    input_norm_grad, grad_gain_attn = norm_backward(
        normed_grad, hidden_in, scale_attn, gain_attn.astype(jnp.float32)
    )
    tokens_grad = middle_grad + input_norm_grad
    local_grads = (
        grad_gain_attn,
        grad_query,
        grad_key,
        grad_value,
        grad_output,
        grad_rel_bias,
        grad_gain_ffn,
        grad_router,
    )
    shard_grads = (
        lax.psum_scatter(local_grads[0], "wshard", scatter_dimension=0, tiled=True),
        lax.psum_scatter(local_grads[1], "wshard", scatter_dimension=0, tiled=True),
        lax.psum_scatter(local_grads[2], "wshard", scatter_dimension=0, tiled=True),
        lax.psum_scatter(local_grads[3], "wshard", scatter_dimension=0, tiled=True),
        lax.psum_scatter(local_grads[4], "wshard", scatter_dimension=0, tiled=True),
        lax.psum_scatter(local_grads[5], "wshard", scatter_dimension=0, tiled=True),
        lax.psum_scatter(local_grads[6], "wshard", scatter_dimension=0, tiled=True),
        lax.psum_scatter(local_grads[7], "wshard", scatter_dimension=0, tiled=True),
    )
    total_grads = lax.psum(
        (
            shard_grads[0],
            shard_grads[1],
            shard_grads[2],
            shard_grads[3],
            shard_grads[4],
            shard_grads[5],
            shard_grads[6],
            shard_grads[7],
        ),
        "expert",
    )
    return (
        layer_out,
        tokens_grad,
        total_grads[0],
        total_grads[1],
        total_grads[2],
        total_grads[3],
        total_grads[4],
        total_grads[5],
        total_grads[6],
        total_grads[7],
        grad_w_in,
        grad_w_out,
    )


def solution(mesh):
    placed = (
        P(("expert", "wshard"), None),
        P("wshard"),
        P("wshard", None),
        P("wshard", None),
        P("wshard", None),
        P("wshard", None),
        P("wshard", None),
        P("wshard"),
        P("wshard", None),
        P("expert", None, "wshard"),
        P("expert", "wshard", None),
        P(("expert", "wshard"), None),
        P(("expert", "wshard"), None),
        P(("expert", "wshard")),
        P(),
        P(),
        P(),
    )
    return jax.shard_map(
        local,
        mesh=mesh,
        in_specs=placed,
        out_specs=(
            P(("expert", "wshard"), None),
            P(("expert", "wshard"), None),
            P("wshard"),
            P("wshard", None),
            P("wshard", None),
            P("wshard", None),
            P("wshard", None),
            P("wshard", None),
            P("wshard"),
            P("wshard", None),
            P("expert", None, "wshard"),
            P("expert", "wshard", None),
        ),
        check_vma=False,
    )
```

profile of v0, /device:TPU:0, one launch (start us, length us, event | category | flops | bytes accessed | tf_op | source)
XLA Modules:
  0.0 1384.2 jit_solution(9358420536016094315)
XLA Ops:
  10.0 1.3 fusion.92
  15.3 1.3 fusion.91
  19.2 1.3 fusion.90
  22.9 13.7 all-reduce.8
  36.6 1.2 fusion.41
  38.3 12.0 all_gather.41
  51.6 217.1 %gather_fusion.4 = f32[65536,12]{1,0:T(8,128)} fusion(f32[12,511]{0,1:T(8,128)S(1)} %copy.104, s32[65536]{0:T(1024)S(1)} %broadcast_clamp_fusion.1), kind=kCustom, calls=%fused_computation.clone | custom fusion | bytes 6553600 | tf_op jit(solution)/shard_map/jit(_take)/gather | solution.py:59
  268.7 20.4 %copy.106 = f32[256,256,12]{0,1,2:T(8,128)} copy(f32[256,256,12]{2,1,0:T(8,128)} %bitcast.180) | data formatting | bytes 6291456 | tf_op jit(solution)/shard_map/jit(_take)/gather | solution.py:59
  289.4 13.1 all-gather
  302.8 1.2 scatter_custom_fusion
  306.6 1.8 convolution_convert_fusion.3
  308.6 1.9 convolution_convert_fusion.2
  310.7 1.9 convolution_convert_fusion.1
  312.8 3.0 fusion.93
  316.3 1.1 copy-done.3
  318.2 2.0 multiply_reduce_fusion.3
  323.7 2.6 scatter_custom_fusion.1
  327.3 12.0 all_to_all.20
  339.3 2.6 scatter_custom_fusion.2
  343.0 11.4 all_to_all.21
  354.6 18.2 %all-gather.16.cloned.1.call-done = bf16[1024,1,768]{2,0,1:T(8,128)(2,1)} async-done(((bf16[256,1,768]{2,0,1:T(8,128)(2,1)}), bf16[1024,1,768]{2,0,1:T(8,128)(2,1)}) %all-gather.16.cloned.1.call-update) | async-done | bytes 1572880 | tf_op jit(solution)/shard_map/all_gather | solution.py:188
  372.9 4.5 fusion.25
  377.3 32.9 %all-gather.18.cloned.1.call-done = bf16[1024,1,768]{2,0,1:T(8,128)(2,1)} async-done(((bf16[256,1,768]{2,0,1:T(8,128)(2,1)}), bf16[1024,1,768]{2,0,1:T(8,128)(2,1)}) %all-gather.18.cloned.1.call-update) | async-done | bytes 1572880 | tf_op jit(solution)/shard_map/all_gather | solution.py:214
  410.3 5.5 fusion.8
  415.8 1.1 copy-done.80
  416.9 3.1 convolution_bitcast_fusion
  420.2 1.2 copy-done.78
  421.4 5.6 convolution_bitcast_fusion.1
  427.0 52.4 %reduce-scatter.12.cloned.1.call-done = f32[256,1,768]{2,0,1:T(8,128)} async-done(((f32[1024,1,768]{2,0,1:T(8,128)}), f32[256,1,768]{2,0,1:T(8,128)}) %reduce-scatter.12.cloned.1.call-update) | async-done | bytes 786448 | tf_op jit(solution)/shard_map/reduce_scatter | solution.py:221
  479.4 1.9 convert_element_type.186
  481.3 3.7 all-to-all-start.3
  485.0 57.0 %reduce-scatter.10.cloned.1.call-done = f32[256,1,768]{2,0,1:T(8,128)} async-done(((f32[1024,1,768]{2,0,1:T(8,128)}), f32[256,1,768]{2,0,1:T(8,128)}) %reduce-scatter.10.cloned.1.call-update) | async-done | bytes 786448 | tf_op jit(solution)/shard_map/reduce_scatter | solution.py:192
  542.0 1.9 convert_element_type.177
  543.9 3.7 all-to-all-start.1
  548.0 1.2 gather_fusion.2
  549.2 6.7 all-to-all-done.1
  555.9 1.2 gather_fusion.1
  558.7 2.7 convert_add_fusion.1
  562.2 1.3 convolution_convert_fusion
  563.5 1.9 copy.114
  565.4 2.0 multiply_reduce_fusion
  567.4 1.8 multiply_convert_fusion
  569.2 1.8 fusion.33
  571.8 2.0 fusion.85
  573.9 2.1 fusion.34
  576.8 2.8 fusion.83
  579.6 1.6 fusion.30
  582.0 2.0 fusion.81
  584.1 2.1 fusion.80
  586.5 689.0 %gather_fusion.3 = s32[65536]{0:T(1024)} fusion(s32[511]{0:T(512)S(1)} %copy-done.2, s32[65536]{0:T(1024)S(1)} %broadcast_clamp_fusion), kind=kCustom, calls=%fused_computation.4 | custom fusion | bytes 786432 | tf_op jit(solution)/shard_map/gather | solution.py:287
  1276.8 4.9 convolution_bitcast_fusion.3
  1281.7 3.3 convolution_bitcast_fusion.2
  1287.0 1.8 convolution_add_fusion.2
  1288.8 2.6 copy.118
  1291.4 1.6 pad.5
  1293.0 2.5 copy.137
  1295.6 3.0 fusion
  1299.3 17.9 %all-reduce.7 = (f32[768]{0:T(1024)S(1)}, f32[32,12]{1,0:T(8,128)S(1)}, f32[768]{0:T(1024)S(1)}) all-reduce(f32[768]{0:T(1024)S(1)} %get-tuple-element.15, f32[32,12]{1,0:T(8,128)S(1)} %fusion, f32[768]{0:T(1024)S(1)} %copy-done.61), channel_id=4, replica_groups=mesh['expert'=8,'wshard'=4] {'wshard'}, use_global_device_ids=true, to_apply=%region_21.23.clone | all-reduce | flops 1920 | bytes 15360
  1317.4 1.1 fusion.46
  1319.5 23.2 %all-reduce.5 = (f32[192]{0:T(256)}, f32[8,12]{1,0:T(8,128)}, f32[192]{0:T(256)}, f32[192,8]{0,1:T(8,128)}) all-reduce(f32[192]{0:T(256)S(1)} %dynamic-slice.3, f32[8,12]{1,0:T(8,128)S(1)} %constant_dynamic-slice_fusion, f32[192]{0:T(256)S(1)} %dynamic-slice.7, ...), channel_id=1, replica_groups=mesh['expert'=8,'wshard'=4] {'expert'}, use_global_device_ids=true, to_apply=%region_22.24 | all-reduce | flops 2016 | bytes 16128 | tf_op jit(solution)/shard_map/psum | solution.py:330
  1342.7 27.9 %all-reduce.11.cloned.1.call-done = (f32[192,768]{1,0:T(8,128)}, f32[192,768]{1,0:T(8,128)}, f32[192,768]{1,0:T(8,128)}, f32[192,768]{1,0:T(8,128)}) async-done(((f32[192,768]{1,0:T(8,128)}, f32[192,768]{1,0:T(8,128)}, f32[192,768]{1,0:T(8,128)}, f32[192,768]{1,0:T(8,128)}), (f32[192,768]{1,0:T(8,128)}, f32[192,768]{1,0:T(8,128)}, f32[192,768]{1,0:T(8,128)}, ...) | async-done | bytes 2359312 | tf_op jit(solution)/shard_map/psum | solution.py:330
  1370.6 2.0 copy.147
  1372.6 1.9 copy.148
  1374.5 1.9 copy.149
  (266 shorter events, 28.1 us)
Async XLA Ops:
  7.2 365.7 %copy-start = (bf16[1,768,768]{2,1,0:T(8,128)(2,1)S(1)}, bf16[1,768,768]{2,1,0:T(8,128)(2,1)}, u32[]{:S(2)}) copy-start(bf16[1,768,768]{2,1,0:T(8,128)(2,1)} %param.28) | copy-start | bytes 3538948
  7.2 299.4 %all-gather.8.cloned.1.call-start = ((), (), s32[]{:S(2)}) async-start(), calls=%async_computation.11 | async-start | bytes 1474560 | tf_op jit(solution)/shard_map/all_gather | solution.py:138
  7.9 300.6 %all-gather.10.cloned.1.call-start = ((), (), s32[]{:S(2)}) async-start(), calls=%async_computation.12 | async-start | bytes 1474560 | tf_op jit(solution)/shard_map/all_gather | solution.py:136
  8.7 302.0 %all-gather.12.cloned.1.call-start = ((), (), s32[]{:S(2)}) async-start(), calls=%async_computation.13 | async-start | bytes 1474560 | tf_op jit(solution)/shard_map/all_gather | solution.py:137
  9.4 308.8 %all-gather.14.cloned.1.call-start = ((), (), s32[]{:S(2)}) async-start(), calls=%async_computation.14 | async-start | bytes 1474560 | tf_op jit(solution)/shard_map/all_gather | solution.py:139
  10.0 362.9 %all-gather.16.cloned.1.call-start = ((), (), s32[]{:S(2)}) async-start(), calls=%async_computation.15 | async-start | bytes 1966080 | tf_op jit(solution)/shard_map/all_gather | solution.py:188
  36.6 274.1 %copy-start.33 = (f32[768]{0:T(1024)}, f32[768]{0:T(1024)S(1)}, u32[]{:S(2)}) copy-start(f32[768]{0:T(1024)S(1)} %convert_element_type.161) | copy-start | bytes 9220
  38.3 272.4 %copy-start.45 = (f32[256]{0:T(256)}, f32[256]{0:T(256)S(1)}, u32[]{:S(2)}) copy-start(f32[256]{0:T(256)S(1)} %get-tuple-element.40) | copy-start | bytes 3076
  268.7 20.7 %copy-start.70 = (bf16[192,8]{0,1:T(8,128)(2,1)S(1)}, bf16[192,8]{0,1:T(8,128)(2,1)}, u32[]{:S(2)}) copy-start(bf16[192,8]{0,1:T(8,128)(2,1)} %param.27) | copy-start | bytes 9220
  268.7 34.0 %copy-start.76 = (s32[256]{0:T(256)S(1)}, s32[256]{0:T(256)}, u32[]{:S(2)}) copy-start(s32[256]{0:T(256)} %param.32) | copy-start | bytes 3076
  268.7 34.0 %copy-start.49 = (s32[256,1]{0,1:T(1,128)S(1)}, s32[256,1]{0,1:T(1,128)}, u32[]{:S(2)}) copy-start(s32[256,1]{0,1:T(1,128)} %param.31) | copy-start | bytes 3076
  268.7 37.8 %copy-start.5 = (bf16[256,768]{1,0:T(8,128)(2,1)S(1)}, bf16[256,768]{1,0:T(8,128)(2,1)}, u32[]{:S(2)}) copy-start(bf16[256,768]{1,0:T(8,128)(2,1)} %param.19) | copy-start | bytes 1179652
  289.4 34.3 %copy-start.41 = (f32[768]{0:T(1024)}, f32[768]{0:T(1024)S(1)}, u32[]{:S(2)}) copy-start(f32[768]{0:T(1024)S(1)} %convert_element_type.174) | copy-start | bytes 9220
  302.7 18.4 %copy-start.39 = (bf16[768,8]{0,1:T(8,128)(2,1)}, bf16[768,8]{0,1:T(8,128)(2,1)S(1)}, u32[]{:S(2)}) copy-start(bf16[768,8]{0,1:T(8,128)(2,1)S(1)} %reshape.378) | copy-start | bytes 36868
  308.5 7.8 copy-start.22
  310.6 5.1 copy-start.9
  318.1 5.6 copy-start.27
  318.2 3.8 copy-start.50
  318.2 3.8 copy-start.66
  318.2 3.8 copy-start.71
  318.2 21.1 %copy-start.18 = (bf16[256,768]{1,0:T(8,128)(2,1)S(1)}, bf16[256,768]{1,0:T(8,128)(2,1)}, u32[]{:S(2)}) copy-start(bf16[256,768]{1,0:T(8,128)(2,1)} %param.30) | copy-start | bytes 1179652
  320.2 237.2 %copy-start.6 = (f32[256,768]{1,0:T(8,128)}, f32[256,768]{1,0:T(8,128)S(1)}, u32[]{:S(2)}) copy-start(f32[256,768]{1,0:T(8,128)S(1)} %get-tuple-element.52) | copy-start | bytes 2359300
  321.1 33.3 %copy-start.12 = (bf16[256,768]{1,0:T(8,128)(2,1)}, bf16[256,768]{1,0:T(8,128)(2,1)S(1)}, u32[]{:S(2)}) copy-start(bf16[256,768]{1,0:T(8,128)(2,1)S(1)} %multiply_convert_fusion.2) | copy-start | bytes 1179652
  321.9 55.4 %copy-start.58 = (f32[256]{0:T(256)}, f32[256]{0:T(256)S(1)}, u32[]{:S(2)}) copy-start(f32[256]{0:T(256)S(1)} %fusion.68) | copy-start | bytes 3076
  322.0 55.4 %copy-start.64 = (f32[256]{0:T(256)}, f32[256]{0:T(256)S(1)}, u32[]{:S(2)}) copy-start(f32[256]{0:T(256)S(1)} %select_reduce_fusion) | copy-start | bytes 3076
  322.5 54.8 %copy-start.68 = (f32[256]{0:T(256)}, f32[256]{0:T(256)S(1)}, u32[]{:S(2)}) copy-start(f32[256]{0:T(256)S(1)} %get-tuple-element.32) | copy-start | bytes 3076
  339.3 71.0 %all-gather.18.cloned.1.call-start = ((), (), s32[]{:S(2)}) async-start(), calls=%async_computation.17 | async-start | bytes 1966080 | tf_op jit(solution)/shard_map/all_gather | solution.py:214
  354.4 125.0 %reduce-scatter.12.cloned.1.call-start = ((), (), s32[]{:S(2)}) async-start(), calls=%async_computation.18 | async-start | bytes 3932160 | tf_op jit(solution)/shard_map/reduce_scatter | solution.py:221
  420.1 121.9 %reduce-scatter.10.cloned.1.call-start = ((), (), s32[]{:S(2)}) async-start(), calls=%async_computation.16 | async-start | bytes 3932160 | tf_op jit(solution)/shard_map/reduce_scatter | solution.py:192
  427.0 120.9 %copy-start.75 = (pred[256]{0:T(512)(128)(4,1)S(1)}, pred[256]{0:T(512)(128)(4,1)}, u32[]{:S(2)}) copy-start(pred[256]{0:T(512)(128)(4,1)} %get-tuple-element.33) | copy-start | bytes 772
  427.0 120.9 %copy-start.72 = (s32[256,1]{0,1:T(1,128)S(1)}, s32[256,1]{0,1:T(1,128)}, u32[]{:S(2)}) copy-start(s32[256,1]{0,1:T(1,128)} %get-tuple-element.35) | copy-start | bytes 3076
  427.0 120.9 %copy-start.38 = (f32[12,256]{1,0:T(8,128)S(1)}, f32[12,256]{1,0:T(8,128)}, u32[]{:S(2)}) copy-start(f32[12,256]{1,0:T(8,128)} %copy-done.37) | copy-start | bytes 36868
  427.0 120.9 %copy-start.44 = (f32[12,256]{1,0:T(8,128)S(1)}, f32[12,256]{1,0:T(8,128)}, u32[]{:S(2)}) copy-start(f32[12,256]{1,0:T(8,128)} %copy-done.43) | copy-start | bytes 36868
  481.3 62.6 %all-to-all-start.3 = ((bf16[8,32,768]{2,1,0:T(8,128)(2,1)}), bf16[8,32,768]{2,1,0:T(8,128)(2,1)S(1)}, u32[]{:S(2)}, u32[]{:S(2)}) async-start(bf16[8,32,768]{2,1,0:T(8,128)(2,1)} %bitcast.50), calls=%async_computation.5 | async-start | bytes 786432 | tf_op jit(solution)/shard_map/all_to_all | solution.py:227
  543.9 12.0 all-to-all-start.1
  547.6 747.9 %reduce-scatter.14.cloned.1.call-start = ((), (), s32[]{:S(2)}) async-start(), calls=%async_computation.19 | async-start | bytes 2949120 | tf_op jit(solution)/shard_map/reduce_scatter | solution.py:322
  547.9 9.6 copy-start.67
  548.0 9.5 copy-start.65
  548.0 9.5 copy-start.31
  548.0 9.5 copy-start.40
  548.0 9.5 copy-start.42
  548.0 9.5 copy-start.51
  548.0 9.5 copy-start.54
  548.0 9.5 copy-start.57
  548.0 9.5 copy-start.59
  557.1 5.1 copy-start.25
  557.2 5.1 copy-start.73
  558.7 6.7 copy-start.4
  567.4 4.4 copy-start.34
  567.4 4.4 copy-start.46
  573.9 721.6 %reduce-scatter.16.cloned.1.call-start = ((), (), s32[]{:S(2)}) async-start(), calls=%async_computation.20 | async-start | bytes 2949120 | tf_op jit(solution)/shard_map/reduce_scatter | solution.py:323
  579.6 715.9 %reduce-scatter.18.cloned.1.call-start = ((), (), s32[]{:S(2)}) async-start(), calls=%async_computation.21 | async-start | bytes 2949120 | tf_op jit(solution)/shard_map/reduce_scatter | solution.py:324
  584.0 711.5 %reduce-scatter.20.cloned.1.call-start = ((), (), s32[]{:S(2)}) async-start(), calls=%async_computation.22 | async-start | bytes 2949120 | tf_op jit(solution)/shard_map/reduce_scatter | solution.py:325
  586.2 732.4 %reduce-scatter.22.cloned.1.call-start = ((), (), s32[]{:S(2)}) async-start(), calls=%async_computation.23 | async-start | bytes 491520
  1276.7 4.9 copy-start.77
  1276.8 4.9 copy-start.79
  1281.6 3.3 copy-start.13
  1281.7 4.7 copy-start.15
  1281.7 4.7 copy-start.24
  1286.1 84.5 %all-reduce.11.cloned.1.call-start = ((), (), s32[]{:S(2)}) async-start(), calls=%async_computation.24 | async-start | bytes 4718592 | tf_op jit(solution)/shard_map/psum | solution.py:330
  1295.6 3.7 copy-start.61
  1295.6 21.8 %copy-start.69 = (f32[256]{0:T(256)S(1)}, f32[256]{0:T(256)}, u32[]{:S(2)}) copy-start(f32[256]{0:T(256)} %get-tuple-element.39) | copy-start | bytes 3076
  1317.4 59.8 %copy-start.1 = (bf16[1,768,768]{2,1,0:T(8,128)(2,1)S(1)}, bf16[1,768,768]{2,1,0:T(8,128)(2,1)}, u32[]{:S(2)}) copy-start(bf16[1,768,768]{2,1,0:T(8,128)(2,1)} %param.28) | copy-start | bytes 3538948
  1370.6 5.8 copy-start.26
  (33 other events, 72.7 us)
Sparse Core Ops, SparseCore 0:
  9.6 33.4 all-gather.7
  44.6 29.5 all-gather.9
  75.8 29.5 all-gather.11
  106.9 29.5 all-gather.13
  339.4 33.4 all-gather.15
  374.3 35.9 all-gather.17
  420.2 59.1 reduce-scatter.11
  481.7 60.2 reduce-scatter.9
  574.0 46.2 reduce-scatter.13
  622.4 47.4 reduce-scatter.15
  672.3 47.5 reduce-scatter.17
  722.0 47.5 reduce-scatter.19
  1286.2 18.8 reduce-scatter.21
  1308.9 61.6 all-reduce.10
where the time goes:
time: 1390 us; the launch traced here: 1380 us
  local copies, waits for them, and re-layouts  964 us (69%)
  waiting for transfers between devices  198 us (14%)
  blocking collectives  103 us (7%)
  matrix products  65.1 us (5%)
  between operations  22.7 us (2%)
  other arithmetic  22.4 us (2%)
    gather x1, local copies, waits for them, and re-layouts, local(): relpos_table[block_offsets(tok_count, begin)].reshape(rows * tok_count)  689 us
    gather x2, local copies, waits for them, and re-layouts, score_block(): looked = jnp.take(bias_offsets, offsets, axis=1)  238 us
    reduce_scatter x1, waiting for transfers between devices, local(): lax.psum_scatter(jnp.einsum('rxf,xfd->rxd', part, w_out, preferred_elemen...  57 us
    reduce_scatter x1, waiting for transfers between devices, local(): lax.psum_scatter(jnp.einsum('rxf,xdf->rxd', part, w_in, preferred_element...  52.4 us
    all_gather x1, waiting for transfers between devices, local(): grad_all = lax.all_gather(grad_local, 'wshard', axis=0, tiled=True)  32.9 us
    unnamed x2, blocking collectives  31.6 us
    psum x1, waiting for transfers between devices, local(): lax.psum((shard_grads[0], shard_grads[1], shard_grads[2], shard_grads[3],...  27.9 us
  transfers between devices with their start and end apart: 16, of which 6 were waited for; matrix products, arithmetic and copies ran while one was open for 73% of the time, Pallas kernels for 0%

commit v1 on v0

--- a/solution.py
+++ b/solution.py
@@ -52,11 +52,27 @@
     return places[None, :] - (begin + places)[:, None] + tok_count - 1
 
 
+def skew(table, tok_count):
+    heads = table.shape[0]
+    span = 2 * tok_count
+    padded = jnp.pad(table, ((0, 0), (0, span - table.shape[1])))
+    flat = jnp.broadcast_to(padded[:, None, :], (heads, tok_count, span)).reshape(heads, -1)
+    body = flat[:, tok_count - 1 : tok_count - 1 + tok_count * (span - 1)]
+    return body.reshape(heads, tok_count, span - 1)[:, :, :tok_count]
+
+
+def unskew_sum(field):
+    heads, tok_count, _ = field.shape
+    span = 2 * tok_count
+    wide = jnp.pad(field, ((0, 0), (0, 0), (0, tok_count - 1))).reshape(heads, -1)
+    wide = jnp.pad(wide, ((0, 0), (tok_count - 1, 1))).reshape(heads, tok_count, span)
+    return jnp.sum(wide.astype(jnp.float32), axis=1)[:, : span - 1]
+
+
 def score_block(query_rows, keys, bias_offsets, segment, begin, scale):
     tok_count = keys.shape[0]
     raw = jnp.einsum("qhd,khd->hqk", query_rows, keys, preferred_element_type=jnp.float32) * scale
-    offsets = block_offsets(tok_count, begin)
-    looked = jnp.take(bias_offsets, offsets, axis=1)
+    looked = skew(bias_offsets, tok_count)
     same = segment[:, None] == segment[None, :]
     return jnp.where(same[None], raw + looked, NEG_FILL)
 
@@ -262,7 +278,6 @@
     values_grad = jnp.zeros((tok_count, n_heads, head_dim), jnp.float32)
     bias_grad_heads = jnp.zeros((n_heads, n_buckets), jnp.float32)
     for number, begin in enumerate(range(0, tok_count, block_rows)):
-        rows = query.shape[0]
         scores = score_block(query, keys, bias_offsets, segment, begin, scale)
         probs = jnp.exp(scores - log_totals[number])
         prob_grad = jnp.einsum(
@@ -284,12 +299,10 @@
             mixed_grad,
             preferred_element_type=jnp.float32,
         )
-        buckets = relpos_table[block_offsets(tok_count, begin)].reshape(rows * tok_count)
-        bucket_hot = (buckets[:, None] == bucket_range[None, :]).astype(jnp.bfloat16)
         bias_grad_heads = jnp.dot(
-            score_grad.reshape(n_heads, rows * tok_count),
-            bucket_hot,
-            preferred_element_type=jnp.float32,
+            unskew_sum(score_grad),
+            table_hot.astype(jnp.float32),
+            precision=lax.Precision.HIGHEST,
         )
     query_grad = query_parts[0].reshape(tok_count, width).astype(jnp.bfloat16)
     keys_grad = keys_grad.reshape(tok_count, width).astype(jnp.bfloat16)

time: 1390 us -> 683 us (0.49)
  local copies, waits for them, and re-layouts: 964 us -> 82.6 us
  waiting for transfers between devices: 198 us -> 370 us
    gather x3 -> x0, local copies, waits for them, and re-layouts: 927 us -> none  [the longest x1 689 us: local(): relpos_table[block_offsets(tok_count, begin)].reshape(rows * tok_count)]
    reduce_scatter x1, waiting for transfers between devices: 0.01 us -> 49.9 us  [local(): lax.psum_scatter(local_grads[2], 'wshard', scatter_dimension=0, tiled=True)]
    reduce_scatter x1, waiting for transfers between devices: 0.01 us -> 49.7 us  [local(): lax.psum_scatter(local_grads[1], 'wshard', scatter_dimension=0, tiled=True)]
    reduce_scatter x1, waiting for transfers between devices: 0.01 us -> 37.1 us  [local(): lax.psum_scatter(local_grads[3], 'wshard', scatter_dimension=0, tiled=True)]
    all_gather x1, waiting for transfers between devices: 0.02 us -> 23.8 us  [local(): lax.all_gather(mixer_shards[4], 'wshard', axis=0, tiled=True)]
    reshape x1 -> x3, local copies, waits for them, and re-layouts: 0.06 us -> 18.8 us  [the longest x1 9.56 us: skew(): return body.reshape(heads, tok_count, span - 1)[:, :, :tok_count]]
    unnamed x180 -> x161, local copies, waits for them, and re-layouts: 22.7 us -> 39.7 us
  transfers between devices with their start and end apart: 16 -> 16, of which waited for: 6 -> 11; matrix products, arithmetic and copies ran while one was open for 73% -> 21% of each run, Pallas kernels for 0% -> 0%
where the time goes in v1:
time: 683 us; the launch traced here: 674 us
  waiting for transfers between devices  370 us (54%)
  blocking collectives  104 us (15%)
  local copies, waits for them, and re-layouts  82.6 us (12%)
  matrix products  56.8 us (8%)
  other arithmetic  30.2 us (4%)
  between operations  22.4 us (3%)
  starting transfers between devices  8.34 us (1%)
    reduce_scatter x1, waiting for transfers between devices, local(): lax.psum_scatter(jnp.einsum('rxf,xdf->rxd', part, w_in, preferred_element...  57 us
    reduce_scatter x1, waiting for transfers between devices, local(): lax.psum_scatter(jnp.einsum('rxf,xfd->rxd', part, w_out, preferred_elemen...  51.7 us
    reduce_scatter x1, waiting for transfers between devices, local(): lax.psum_scatter(local_grads[2], 'wshard', scatter_dimension=0, tiled=True)  49.9 us
    reduce_scatter x1, waiting for transfers between devices, local(): lax.psum_scatter(local_grads[1], 'wshard', scatter_dimension=0, tiled=True)  49.7 us
    psum x1, waiting for transfers between devices, local(): lax.psum((shard_grads[0], shard_grads[1], shard_grads[2], shard_grads[3],...  41 us
    unnamed x161, local copies, waits for them, and re-layouts  39.7 us
    reduce_scatter x1, waiting for transfers between devices, local(): lax.psum_scatter(local_grads[3], 'wshard', scatter_dimension=0, tiled=True)  37.1 us
    unnamed x2, blocking collectives  31.5 us
  transfers between devices with their start and end apart: 16, of which 11 were waited for; matrix products, arithmetic and copies ran while one was open for 21% of the time, Pallas kernels for 0%

profile of v1, /device:TPU:0, one launch (start us, length us, event | category | flops | bytes accessed | tf_op | source)
XLA Modules:
  0.0 674.2 jit_solution(2781296741734902018)
XLA Ops:
  10.1 1.3 fusion.89
  15.3 1.3 fusion.88
  21.6 1.3 fusion.87
  25.3 13.7 %all-reduce.11 = (bf16[768]{0:T(1024)(128)(2,1)S(1)}, bf16[768]{0:T(1024)(128)(2,1)S(1)}) all-reduce(bf16[768]{0:T(1024)(128)(2,1)S(1)} %dynamic-update-slice, bf16[768]{0:T(1024)(128)(2,1)S(1)} %dynamic-update-slice.1), channel_id=1, replica_groups=mesh['expert'=8,'wshard'=4] {'wshard'}, use_global_device_ids=true, to_apply=%add.3 | all-reduce | flops 1536 | bytes 6144
  39.0 12.0 %all_gather.41 = bf16[32,12]{1,0:T(8,128)(2,1)S(1)} all-gather(bf16[8,12]{1,0:T(8,128)(2,1)} %param.23), channel_id=1, replica_groups=mesh['expert'=8,'wshard'=4] {'wshard'}, dimensions={0}, use_global_device_ids=true | all-gather | bytes 960 | tf_op jit(solution)/shard_map/all_gather | solution.py:156
  51.0 13.4 %all-gather = bf16[4,192,8]{1,2,0:T(8,128)(2,1)S(1)} all-gather(bf16[1,192,8]{1,2,0:T(8,128)(2,1)} %bitcast.206), channel_id=1, replica_groups=mesh['expert'=8,'wshard'=4] {'wshard'}, dimensions={0}, use_global_device_ids=true | all-gather | bytes 15360 | tf_op jit(solution)/shard_map/all_gather | solution.py:158
  71.9 4.9 copy.106
  76.8 5.5 slice.36
  82.2 9.6 %reshape.266 = f32[12,256,511]{2,1,0:T(8,128)} reshape(f32[12,130816]{1,0:T(8,128)} %slice.36) | data formatting | bytes 12558336 | tf_op jit(solution)/shard_map/reshape | solution.py:61
  91.8 3.8 slice.37
  95.6 3.6 copy.96
  99.2 1.8 convolution_convert_fusion.2
  101.2 1.9 convolution_convert_fusion.1
  103.3 2.3 all-gather.8.cloned.1.call-done
  105.6 1.8 convolution_convert_fusion.3
  107.6 2.8 fusion.90
  112.8 23.8 %all-gather.14.cloned.1.call-done = bf16[768,768]{1,0:T(8,128)(2,1)} async-done(((bf16[192,768]{1,0:T(8,128)(2,1)}), bf16[768,768]{1,0:T(8,128)(2,1)}) %all-gather.14.cloned.1.call-update) | async-done | bytes 1179664 | tf_op jit(solution)/shard_map/all_gather | solution.py:155
  136.7 1.9 multiply_reduce_fusion.3
  143.5 2.6 scatter_custom_fusion.1
  147.1 11.9 %all_to_all.20 = bf16[8,32,768]{2,1,0:T(8,128)(2,1)} all-to-all(bf16[8,32,768]{2,1,0:T(8,128)(2,1)S(1)} %bitcast.195), channel_id=1, replica_groups=mesh['expert'=8,'wshard'=4] {'expert'}, dimensions={0} | all-to-all | bytes 786432 | tf_op jit(solution)/shard_map/all_to_all | solution.py:202
  159.1 2.8 scatter_custom_fusion.2
  162.9 11.4 %all_to_all.21 = bf16[8,32,768]{2,1,0:T(8,128)(2,1)} all-to-all(bf16[8,32,768]{2,1,0:T(8,128)(2,1)S(1)} %bitcast.196), channel_id=1, replica_groups=mesh['expert'=8,'wshard'=4] {'expert'}, dimensions={0} | all-to-all | bytes 786432 | tf_op jit(solution)/shard_map/all_to_all | solution.py:228
  174.4 19.2 %all-gather.16.cloned.1.call-done = bf16[1024,1,768]{2,0,1:T(8,128)(2,1)} async-done(((bf16[256,1,768]{2,0,1:T(8,128)(2,1)}), bf16[1024,1,768]{2,0,1:T(8,128)(2,1)}) %all-gather.16.cloned.1.call-update) | async-done | bytes 1572880 | tf_op jit(solution)/shard_map/all_gather | solution.py:204
  193.6 3.1 fusion.22
  196.7 1.7 copy-done.68
  198.4 3.7 convolution_bitcast_fusion.1
  202.2 28.8 %all-gather.18.cloned.1.call-done = bf16[1024,1,768]{2,0,1:T(8,128)(2,1)} async-done(((bf16[256,1,768]{2,0,1:T(8,128)(2,1)}), bf16[1024,1,768]{2,0,1:T(8,128)(2,1)}) %all-gather.18.cloned.1.call-update) | async-done | bytes 1572880 | tf_op jit(solution)/shard_map/all_gather | solution.py:230
  231.0 5.4 fusion.6
  237.6 3.1 convolution_bitcast_fusion
  240.7 51.7 %reduce-scatter.10.cloned.1.call-done = f32[256,1,768]{2,0,1:T(8,128)} async-done(((f32[1024,1,768]{2,0,1:T(8,128)}), f32[256,1,768]{2,0,1:T(8,128)}) %reduce-scatter.10.cloned.1.call-update) | async-done | bytes 786448 | tf_op jit(solution)/shard_map/reduce_scatter | solution.py:208
  292.5 1.9 convert_element_type.190
  294.4 3.7 all-to-all-start.1
  298.1 57.0 %reduce-scatter.12.cloned.1.call-done = f32[256,1,768]{2,0,1:T(8,128)} async-done(((f32[1024,1,768]{2,0,1:T(8,128)}), f32[256,1,768]{2,0,1:T(8,128)}) %reduce-scatter.12.cloned.1.call-update) | async-done | bytes 786448 | tf_op jit(solution)/shard_map/reduce_scatter | solution.py:237
  355.1 1.9 convert_element_type.199
  357.0 3.7 all-to-all-start.3
  360.7 1.2 gather_fusion.1
  362.2 6.8 %all-to-all-done.3 = bf16[8,32,768]{2,1,0:T(8,128)(2,1)S(1)} async-done(((bf16[8,32,768]{2,1,0:T(8,128)(2,1)}), bf16[8,32,768]{2,1,0:T(8,128)(2,1)S(1)}, u32[]{:S(2)}, u32[]{:S(2)}) %all-to-all-start.3) | async-done | bytes 393248 | tf_op jit(solution)/shard_map/all_to_all | solution.py:243
  371.4 1.8 convert_add_fusion.1
  374.1 2.0 fusion.77
  377.0 2.8 convolution_convert_fusion
  379.8 2.0 copy.85
  381.8 1.6 fusion.27
  384.3 2.1 fusion.78
  386.7 2.0 multiply_reduce_fusion
  391.9 2.0 fusion.80
  395.2 4.4 convolution_bitcast_fusion.3
  399.6 3.3 convolution_bitcast_fusion.2
  403.6 1.9 pad.14.clone
  405.6 9.2 %reshape.280 = bf16[12,130816]{1,0:T(8,128)(2,1)} reshape(bf16[12,256,511]{2,1,0:T(8,128)(2,1)} %pad.14.clone) | data formatting | bytes 6279168 | tf_op jit(solution)/shard_map/reshape | solution.py:67
  415.2 2.0 fusion.82
  417.5 3.4 pad_convert_fusion
  420.9 8.1 %copy.107 = f32[2,8,256,512]{3,2,1,0:T(8,128)} copy(f32[2,8,256,512]{3,1,2,0:T(8,128)S(1)} %bitcast.174) | data formatting | bytes 16777216
  430.2 4.2 slice_reduce_fusion
  435.1 37.1 %reduce-scatter.18.cloned.1.call-done = f32[192,768]{1,0:T(8,128)} async-done(((f32[768,768]{1,0:T(8,128)}), f32[192,768]{1,0:T(8,128)}) %reduce-scatter.18.cloned.1.call-update) | async-done | bytes 589840 | tf_op jit(solution)/shard_map/reduce_scatter | solution.py:337
  472.2 49.9 %reduce-scatter.16.cloned.1.call-done = f32[192,768]{1,0:T(8,128)} async-done(((f32[768,768]{1,0:T(8,128)}), f32[192,768]{1,0:T(8,128)}) %reduce-scatter.16.cloned.1.call-update) | async-done | bytes 589840 | tf_op jit(solution)/shard_map/reduce_scatter | solution.py:336
  522.1 49.7 %reduce-scatter.14.cloned.1.call-done = f32[192,768]{1,0:T(8,128)} async-done(((f32[768,768]{1,0:T(8,128)}), f32[192,768]{1,0:T(8,128)}) %reduce-scatter.14.cloned.1.call-update) | async-done | bytes 589840 | tf_op jit(solution)/shard_map/reduce_scatter | solution.py:335
  571.9 1.9 convolution_add_fusion.2
  574.1 1.9 fusion.46
  576.1 17.8 %all-reduce.10 = (f32[768]{0:T(1024)S(1)}, f32[32,12]{1,0:T(8,128)S(1)}, f32[768]{0:T(1024)S(1)}) all-reduce(f32[768]{0:T(1024)S(1)} %get-tuple-element.14, f32[32,12]{1,0:T(8,128)S(1)} %fusion.56, f32[768]{0:T(1024)S(1)} %copy-done.50), channel_id=4, replica_groups=mesh['expert'=8,'wshard'=4] {'wshard'}, use_global_device_ids=true, to_apply=%region_21.22.clone | all-reduce | flops 1920 | bytes 15360
  596.1 23.5 %all-reduce.8 = (f32[192]{0:T(256)}, f32[8,12]{1,0:T(8,128)}, f32[192]{0:T(256)}, f32[192,8]{0,1:T(8,128)}) all-reduce(f32[192]{0:T(256)S(1)} %dynamic-slice.3, f32[8,12]{1,0:T(8,128)S(1)} %constant_dynamic-slice_fusion, f32[192]{0:T(256)S(1)} %dynamic-slice.7, f32[192,8]{0,1:T(8,128)S(1)} %copy.95), channel_id=1, replica_groups=mesh['expert'=8,'wshard'=4] {'expert'}, use_global_device_ids=true, to_apply=%region_22.23 | all-reduce | flops 2016 | bytes 16128 | tf_op jit(solution)/shard_map/psum | solution.py:343
  619.6 41.0 %all-reduce.14.cloned.1.call-done = (f32[192,768]{1,0:T(8,128)}, f32[192,768]{1,0:T(8,128)}, f32[192,768]{1,0:T(8,128)}, f32[192,768]{1,0:T(8,128)}) async-done(((f32[192,768]{1,0:T(8,128)}, f32[192,768]{1,0:T(8,128)}, f32[192,768]{1,0:T(8,128)}, f32[192,768]{1,0:T(8,128)}), (f32[192,768]{1,0:T(8,128)}, f32[192,768]{1,0:T(8,128)}, f32[192,768]{1,0:T(8,128)}, ...) | async-done | bytes 2359312 | tf_op jit(solution)/shard_map/psum | solution.py:343
  660.6 2.0 copy.117
  662.6 1.9 copy.118
  664.5 1.9 copy.119
  (245 shorter events, 42.1 us)
Async XLA Ops:
  7.2 191.2 %copy-start = (bf16[1,768,768]{2,1,0:T(8,128)(2,1)S(1)}, bf16[1,768,768]{2,1,0:T(8,128)(2,1)}, u32[]{:S(2)}) copy-start(bf16[1,768,768]{2,1,0:T(8,128)(2,1)} %param.27) | copy-start | bytes 3538948
  7.2 62.0 %copy-start.39 = (s32[256,1]{0,1:T(1,128)S(1)}, s32[256,1]{0,1:T(1,128)}, u32[]{:S(2)}) copy-start(s32[256,1]{0,1:T(1,128)} %param.29) | copy-start | bytes 3076
  7.2 62.6 %copy-start.66 = (s32[511]{0:T(512)S(1)}, s32[511]{0:T(512)}, u32[]{:S(2)}) copy-start(s32[511]{0:T(512)} %param.33) | copy-start | bytes 6136
  7.2 92.0 %all-gather.10.cloned.1.call-start = ((), (), s32[]{:S(2)}) async-start(), calls=%async_computation.12 | async-start | bytes 1474560 | tf_op jit(solution)/shard_map/all_gather | solution.py:152
  8.0 93.3 %all-gather.12.cloned.1.call-start = ((), (), s32[]{:S(2)}) async-start(), calls=%async_computation.13 | async-start | bytes 1474560 | tf_op jit(solution)/shard_map/all_gather | solution.py:153
  8.7 96.9 %all-gather.8.cloned.1.call-start = ((), (), s32[]{:S(2)}) async-start(), calls=%async_computation.11 | async-start | bytes 1474560 | tf_op jit(solution)/shard_map/all_gather | solution.py:154
  9.4 127.2 %all-gather.14.cloned.1.call-start = ((), (), s32[]{:S(2)}) async-start(), calls=%async_computation.14 | async-start | bytes 1474560 | tf_op jit(solution)/shard_map/all_gather | solution.py:155
  10.0 183.6 %all-gather.16.cloned.1.call-start = ((), (), s32[]{:S(2)}) async-start(), calls=%async_computation.15 | async-start | bytes 1966080 | tf_op jit(solution)/shard_map/all_gather | solution.py:204
  21.6 84.0 %copy-start.35 = (f32[256]{0:T(256)}, f32[256]{0:T(256)S(1)}, u32[]{:S(2)}) copy-start(f32[256]{0:T(256)S(1)} %get-tuple-element.39) | copy-start | bytes 3076
  39.0 66.6 %copy-start.27 = (f32[768]{0:T(1024)}, f32[768]{0:T(1024)S(1)}, u32[]{:S(2)}) copy-start(f32[768]{0:T(1024)S(1)} %convert_element_type.174) | copy-start | bytes 9220
  101.2 9.2 %copy-start.11 = (bf16[256,768]{0,1:T(8,128)(2,1)}, bf16[256,768]{0,1:T(8,128)(2,1)S(1)}, u32[]{:S(2)}) copy-start(bf16[256,768]{0,1:T(8,128)(2,1)S(1)} %copy.75) | copy-start | bytes 1179652
  103.3 7.1 %copy-start.9 = (bf16[256,768]{0,1:T(8,128)(2,1)}, bf16[256,768]{0,1:T(8,128)(2,1)S(1)}, u32[]{:S(2)}) copy-start(bf16[256,768]{0,1:T(8,128)(2,1)S(1)} %copy.76) | copy-start | bytes 1179652
  112.1 24.6 %copy-start.60 = (f32[256]{0:T(256)S(1)}, f32[256]{0:T(256)}, u32[]{:S(2)}) copy-start(f32[256]{0:T(256)} %compare_convert_fusion.1) | copy-start | bytes 3076
  112.8 30.7 %copy-start.23 = (bf16[12,64,256]{2,1,0:T(8,128)(2,1)}, bf16[12,64,256]{2,1,0:T(8,128)(2,1)S(1)}, u32[]{:S(2)}) copy-start(bf16[12,64,256]{2,1,0:T(8,128)(2,1)S(1)} %fusion.26) | copy-start | bytes 1179652
  136.6 5.2 copy-start.55
  136.6 5.2 copy-start.58
  136.6 22.4 %copy-start.17 = (bf16[256,768]{1,0:T(8,128)(2,1)S(1)}, bf16[256,768]{1,0:T(8,128)(2,1)}, u32[]{:S(2)}) copy-start(bf16[256,768]{1,0:T(8,128)(2,1)} %param.28) | copy-start | bytes 1179652
  139.8 34.5 %copy-start.13 = (bf16[256,768]{1,0:T(8,128)(2,1)}, bf16[256,768]{1,0:T(8,128)(2,1)S(1)}, u32[]{:S(2)}) copy-start(bf16[256,768]{1,0:T(8,128)(2,1)S(1)} %multiply_convert_fusion.2) | copy-start | bytes 1179652
  140.1 230.1 %copy-start.25 = (f32[256,8]{0,1:T(8,128)}, f32[256,8]{0,1:T(8,128)S(1)}, u32[]{:S(2)}) copy-start(f32[256,8]{0,1:T(8,128)S(1)} %get-tuple-element.53) | copy-start | bytes 24580
  159.0 72.0 %all-gather.18.cloned.1.call-start = ((), (), s32[]{:S(2)}) async-start(), calls=%async_computation.17 | async-start | bytes 1966080 | tf_op jit(solution)/shard_map/all_gather | solution.py:230
  174.3 118.1 %reduce-scatter.10.cloned.1.call-start = ((), (), s32[]{:S(2)}) async-start(), calls=%async_computation.16 | async-start | bytes 3932160 | tf_op jit(solution)/shard_map/reduce_scatter | solution.py:208
  202.1 152.9 %reduce-scatter.12.cloned.1.call-start = ((), (), s32[]{:S(2)}) async-start(), calls=%async_computation.18 | async-start | bytes 3932160 | tf_op jit(solution)/shard_map/reduce_scatter | solution.py:237
  231.0 6.6 copy-start.65
  240.7 57.3 %copy-start.62 = (pred[256]{0:T(512)(128)(4,1)S(1)}, pred[256]{0:T(512)(128)(4,1)}, u32[]{:S(2)}) copy-start(pred[256]{0:T(512)(128)(4,1)} %get-tuple-element.32) | copy-start | bytes 772
  240.7 57.4 %copy-start.59 = (s32[256,1]{0,1:T(1,128)S(1)}, s32[256,1]{0,1:T(1,128)}, u32[]{:S(2)}) copy-start(s32[256,1]{0,1:T(1,128)} %get-tuple-element.34) | copy-start | bytes 3076
  294.4 62.6 %all-to-all-start.1 = ((bf16[8,32,768]{2,1,0:T(8,128)(2,1)}), bf16[8,32,768]{2,1,0:T(8,128)(2,1)S(1)}, u32[]{:S(2)}, u32[]{:S(2)}) async-start(bf16[8,32,768]{2,1,0:T(8,128)(2,1)} %bitcast.33), calls=%async_computation.2 | async-start | bytes 786432 | tf_op jit(solution)/shard_map/all_to_all | solution.py:214
  298.1 72.1 %copy-start.56 = (f32[256]{0:T(256)}, f32[256]{0:T(256)S(1)}, u32[]{:S(2)}) copy-start(f32[256]{0:T(256)S(1)} %convert_element_type.192) | copy-start | bytes 3076
  298.1 64.1 %copy-start.54 = (f32[256]{0:T(256)S(1)}, f32[256]{0:T(256)}, u32[]{:S(2)}) copy-start(f32[256]{0:T(256)} %copy-done.53) | copy-start | bytes 3076
  357.0 12.0 %all-to-all-start.3 = ((bf16[8,32,768]{2,1,0:T(8,128)(2,1)}), bf16[8,32,768]{2,1,0:T(8,128)(2,1)S(1)}, u32[]{:S(2)}, u32[]{:S(2)}) async-start(bf16[8,32,768]{2,1,0:T(8,128)(2,1)} %bitcast.48), calls=%async_computation.5 | async-start | bytes 786432 | tf_op jit(solution)/shard_map/all_to_all | solution.py:243
  360.7 74.4 %reduce-scatter.20.cloned.1.call-start = ((), (), s32[]{:S(2)}) async-start(), calls=%async_computation.22 | async-start | bytes 2949120 | tf_op jit(solution)/shard_map/reduce_scatter | solution.py:338
  360.7 9.5 %copy-start.33 = (bf16[768,8]{0,1:T(8,128)(2,1)S(1)}, bf16[768,8]{0,1:T(8,128)(2,1)}, u32[]{:S(2)}) copy-start(bf16[768,8]{0,1:T(8,128)(2,1)} %reshape.339) | copy-start | bytes 36868
  360.7 9.5 %copy-start.43 = (f32[256]{0:T(256)S(1)}, f32[256]{0:T(256)}, u32[]{:S(2)}) copy-start(f32[256]{0:T(256)} %copy-done.42) | copy-start | bytes 3076
  360.7 9.5 %copy-start.46 = (f32[256]{0:T(256)S(1)}, f32[256]{0:T(256)}, u32[]{:S(2)}) copy-start(f32[256]{0:T(256)} %copy-done.45) | copy-start | bytes 3076
  360.7 9.5 %copy-start.48 = (f32[256]{0:T(256)S(1)}, f32[256]{0:T(256)}, u32[]{:S(2)}) copy-start(f32[256]{0:T(256)} %copy-done.47) | copy-start | bytes 3076
  362.2 9.2 %copy-start.51 = (f32[256]{0:T(256)}, f32[256]{0:T(256)S(1)}, u32[]{:S(2)}) copy-start(f32[256]{0:T(256)S(1)} %select_multiply_fusion) | copy-start | bytes 3076
  370.2 3.8 copy-start.24
  376.1 5.8 copy-start.3
  376.1 96.1 %reduce-scatter.18.cloned.1.call-start = ((), (), s32[]{:S(2)}) async-start(), calls=%async_computation.21 | async-start | bytes 2949120 | tf_op jit(solution)/shard_map/reduce_scatter | solution.py:337
  386.4 135.7 %reduce-scatter.16.cloned.1.call-start = ((), (), s32[]{:S(2)}) async-start(), calls=%async_computation.20 | async-start | bytes 2949120 | tf_op jit(solution)/shard_map/reduce_scatter | solution.py:336
  391.1 4.1 copy-start.63
  393.9 177.9 %reduce-scatter.14.cloned.1.call-start = ((), (), s32[]{:S(2)}) async-start(), calls=%async_computation.19 | async-start | bytes 2949120 | tf_op jit(solution)/shard_map/reduce_scatter | solution.py:335
  395.2 4.4 copy-start.64
  395.2 4.4 copy-start.69
  405.5 9.2 %copy-start.10 = (bf16[256,768]{0,1:T(8,128)(2,1)S(1)}, bf16[256,768]{0,1:T(8,128)(2,1)}, u32[]{:S(2)}) copy-start(bf16[256,768]{0,1:T(8,128)(2,1)} %copy-done.9) | copy-start | bytes 1179652
  405.5 9.6 %copy-start.30 = (f32[768]{0:T(1024)S(1)}, f32[768]{0:T(1024)}, u32[]{:S(2)}) copy-start(f32[768]{0:T(1024)} %copy-done.27) | copy-start | bytes 9220
  405.5 9.6 %copy-start.38 = (f32[256]{0:T(256)S(1)}, f32[256]{0:T(256)}, u32[]{:S(2)}) copy-start(f32[256]{0:T(256)} %copy-done.35) | copy-start | bytes 3076
  417.2 177.9 %reduce-scatter.22.cloned.1.call-start = ((), (), s32[]{:S(2)}) async-start(), calls=%async_computation.23 | async-start | bytes 491520
  420.9 8.2 %copy-start.14 = (bf16[256,768]{1,0:T(8,128)(2,1)S(1)}, bf16[256,768]{1,0:T(8,128)(2,1)}, u32[]{:S(2)}) copy-start(bf16[256,768]{1,0:T(8,128)(2,1)} %copy-done.13) | copy-start | bytes 1179652
  420.9 8.2 %copy-start.26 = (f32[256,8]{0,1:T(8,128)S(1)}, f32[256,8]{0,1:T(8,128)}, u32[]{:S(2)}) copy-start(f32[256,8]{0,1:T(8,128)} %copy-done.25) | copy-start | bytes 24580
  420.9 8.2 %copy-start.40 = (s32[256,1]{0,1:T(1,128)S(1)}, s32[256,1]{0,1:T(1,128)}, u32[]{:S(2)}) copy-start(s32[256,1]{0,1:T(1,128)} %param.29) | copy-start | bytes 3076
  420.9 8.2 %copy-start.44 = (f32[256]{0:T(256)S(1)}, f32[256]{0:T(256)}, u32[]{:S(2)}) copy-start(f32[256]{0:T(256)} %copy-done.42) | copy-start | bytes 3076
  420.9 8.2 %copy-start.49 = (f32[256]{0:T(256)S(1)}, f32[256]{0:T(256)}, u32[]{:S(2)}) copy-start(f32[256]{0:T(256)} %copy-done.47) | copy-start | bytes 3076
  420.9 8.2 %copy-start.52 = (f32[256]{0:T(256)S(1)}, f32[256]{0:T(256)}, u32[]{:S(2)}) copy-start(f32[256]{0:T(256)} %copy-done.51) | copy-start | bytes 3076
  430.2 4.3 copy-start.21
  434.4 137.4 %copy-start.16 = (bf16[12,64,256]{2,1,0:T(8,128)(2,1)S(1)}, bf16[12,64,256]{2,1,0:T(8,128)(2,1)}, u32[]{:S(2)}) copy-start(bf16[12,64,256]{2,1,0:T(8,128)(2,1)} %copy-done.15) | copy-start | bytes 1179652
  434.4 226.2 %all-reduce.14.cloned.1.call-start = ((), (), s32[]{:S(2)}) async-start(), calls=%async_computation.24 | async-start | bytes 4718592 | tf_op jit(solution)/shard_map/psum | solution.py:343
  435.0 138.7 %copy-start.41 = (f32[12,512]{1,0:T(8,128)S(1)}, f32[12,512]{1,0:T(8,128)}, u32[]{:S(2)}) copy-start(f32[12,512]{1,0:T(8,128)} %slice_reduce_fusion) | copy-start | bytes 73732
  435.0 138.7 %copy-start.67 = (s32[511]{0:T(512)S(1)}, s32[511]{0:T(512)}, u32[]{:S(2)}) copy-start(s32[511]{0:T(512)} %param.33) | copy-start | bytes 6136
  435.0 139.1 %copy-start.19 = (bf16[12,64,256]{2,1,0:T(8,128)(2,1)S(1)}, bf16[12,64,256]{2,1,0:T(8,128)(2,1)}, u32[]{:S(2)}) copy-start(bf16[12,64,256]{2,1,0:T(8,128)(2,1)} %copy-done.18) | copy-start | bytes 1179652
  571.8 4.2 copy-start.50
  571.9 22.2 %copy-start.8 = (f32[256,768]{1,0:T(8,128)S(1)}, f32[256,768]{1,0:T(8,128)}, u32[]{:S(2)}) copy-start(f32[256,768]{1,0:T(8,128)} %copy-done.7) | copy-start | bytes 2359300
  571.9 22.2 %copy-start.57 = (f32[256]{0:T(256)S(1)}, f32[256]{0:T(256)}, u32[]{:S(2)}) copy-start(f32[256]{0:T(256)} %get-tuple-element.38) | copy-start | bytes 3076
  594.0 73.2 %copy-start.1 = (bf16[1,768,768]{2,1,0:T(8,128)(2,1)S(1)}, bf16[1,768,768]{2,1,0:T(8,128)(2,1)}, u32[]{:S(2)}) copy-start(bf16[1,768,768]{2,1,0:T(8,128)(2,1)} %param.27) | copy-start | bytes 3538948
  660.6 5.8 copy-start.22
  (23 other events, 44.9 us)
Sparse Core Ops, SparseCore 0:
  9.6 33.4 all-gather.9
  44.7 29.3 all-gather.11
  75.6 29.9 all-gather.7
  107.0 29.5 all-gather.13
  159.2 34.3 all-gather.15
  195.0 35.9 all-gather.17
  233.3 59.1 reduce-scatter.9
  294.8 60.2 reduce-scatter.11
  376.2 46.2 reduce-scatter.19
  424.6 47.5 reduce-scatter.17
  474.5 47.5 reduce-scatter.15
  524.2 47.5 reduce-scatter.13
  574.7 20.3 reduce-scatter.21
  598.8 61.7 all-reduce.13

commit v2 on v0

v2 whole, which is shorter than its diff:
```python
import functools
import types

import jax
import jax.numpy as jnp
import numpy as np
from jax import lax
from jax.experimental import pallas as pl
from jax.experimental.pallas import tpu as pltpu
from jax.sharding import PartitionSpec as P

EPSILON = 1e-06
NEG_FILL = -1e30
GELU_A = 0.79788456
GELU_B = 0.044715
LANES = 128
REL_LANE = 64
GAIN_ATTN_LANE = 126
GAIN_FFN_LANE = 127
MESH = pl.DeviceIdType.MESH
BF = jnp.bfloat16
F32 = jnp.float32
I32 = jnp.int32


def up16(count):
    return -(-count // 16) * 16


def dot(a, b):
    return jnp.dot(a, b, preferred_element_type=F32)


def dot_rt(a, b):
    return lax.dot_general(a, b, (((1,), (1,)), ((), ())), preferred_element_type=F32)


def dot_lt(a, b):
    return lax.dot_general(a, b, (((0,), (0,)), ((), ())), preferred_element_type=F32)


def iota(shape, axis):
    return lax.broadcasted_iota(I32, shape, axis)


def flip(index, offset):
    out = index
    bit = 1
    while bit <= offset:
        if offset & bit:
            out = out + bit * (1 - 2 * lax.rem(lax.div(index, bit), 2))
        bit *= 2
    return out


def aligned(value, step):
    return pl.multiple_of(value, step)


def two_parts(value):
    high = value.astype(BF)
    return high, (value - high.astype(F32)).astype(BF)


def plan(expert_size, shard_size, tok_count, width, heads, buckets_here, n_experts, hidden):
    s = types.SimpleNamespace()
    s.E, s.W = expert_size, shard_size
    s.C = expert_size // 2
    s.T, s.D, s.H = tok_count, width, heads
    s.HD = width // heads
    s.F = hidden
    s.NX = n_experts
    s.cap = tok_count // n_experts
    s.cp = s.cap if s.cap % 8 == 0 else up16(s.cap)
    s.dt = BF if s.cp % 16 == 0 else F32
    s.S = n_experts * s.cp
    s.R = s.E * s.cp
    s.SR = width // shard_size
    s.NBH = buckets_here
    s.NBP = up16(buckets_here)
    s.half = width // 2
    team = s.C
    while s.SR % team or (s.SR // team) % 16:
        team //= 2
    s.team = team
    s.pw = s.SR // team
    s.pr = up16(s.SR // s.C)
    s.CP = s.C * s.pr
    s.Dp = s.W * s.CP
    s.padded = s.CP != s.SR
    s.tile = LANES
    s.slots = 2 if s.padded else max(width, hidden) // s.tile
    return s


def pieces_shape(s):
    return (4, s.C - 1, s.W * s.pr, s.half)


def arrivals(s):
    return (("Ga", s.D), ("Na", s.D), ("Ta", LANES)) if s.dt == F32 else ()


def scratch_list(s):
    V = pltpu.VMEM
    dma = pltpu.SemaphoreType.DMA
    return [
        ("wfull", V((4, s.D, s.D), BF)),
        ("smg", V((s.W, s.SR + s.NBP, LANES), BF)),
        ("xb", V((s.T, s.D), BF)),
        ("og", V((s.T, s.D), BF)),
        ("wi", V((s.D, s.F), BF)),
        ("wo", V((s.F, s.D), BF)),
        ("pm", V((s.S, s.T), BF)),
        ("pt", V((s.T, s.S), BF)),
        ("gsend", V((s.NX, s.cp, s.D), s.dt)),
        ("nsend", V((s.NX, s.cp, s.D), s.dt)),
        ("tsend", V((s.NX, s.cp, LANES), s.dt)),
        ("Gr", V((s.W * s.R, s.D), BF)),
        ("Nr", V((s.W * s.R, s.D), BF)),
        ("Tr", V((s.W * s.R, LANES), BF)),
        ("agr", V((s.W * s.R, s.F), BF)),
        ("act", V((s.W * s.R, s.F), BF)),
        ("ig", V((s.W * s.R, s.F), BF)),
        ("SS", V((s.W, s.R, s.D + LANES), BF)),
        ("Sr", V((s.W - 1, s.R, s.D + LANES), BF)),
        ("Sb", V((s.R, s.D + LANES), s.dt)),
        ("Sk", V((s.S, s.D + LANES), s.dt)),
        ("Rb", V((s.R, s.D), s.dt)),
        ("Rk", V((s.S, s.D), s.dt)),
        ("tb", V((LANES, 2 * s.T), F32)),
        ("oh", V((s.W * s.NBP, 2 * s.T), BF)),
        ("ohm", V((s.W * s.NBP, 2 * s.T), BF)),
        ("rows", V((8, s.D), F32)),
        ("Rw", V((s.D, LANES), BF)),
        ("probs", V((s.H, s.T, s.T), F32)),
        ("q", V((s.T, s.D), BF)),
        ("kk", V((s.T, s.D), BF)),
        ("v", V((s.T, s.D), BF)),
        ("mixed", V((s.T, s.D), BF)),
        ("nf", V((s.T, s.D), BF)),
        ("middle", V((s.T, s.D), F32)),
        ("mg", V((s.T, s.D), F32)),
        ("att", V((s.T, s.D), BF)),
        ("dq", V((s.T, s.D), BF)),
        ("dk", V((s.T, s.D), BF)),
        ("dv", V((s.T, s.D), BF)),
        ("nT", V((s.Dp, 2 * s.T), BF)),
        ("mT", V((s.Dp, 2 * s.T), BF)),
        ("fac", V((4, s.T, s.half), BF)),
        ("GS", V((4, s.C, s.W * s.pr, s.half), BF)),
        ("ZS", V((4, s.W * s.pr, s.half), BF)),
        ("ZR", V((4, s.W - 1, s.pr, s.half), BF)),
        ("FG", V((4, s.CP, s.D), BF)),
        ("smo", V((s.Dp, LANES), BF)),
        ("sms", V((s.Dp, LANES), BF)),
        ("hGS", V((s.C, s.W * s.pr, LANES), BF)),
        ("hGR", V((s.C - 1, s.W * s.pr, LANES), BF)),
        ("hZS", V((s.W * s.pr, LANES), BF)),
        ("hZR", V((s.W - 1, s.pr, LANES), BF)),
        ("hFG", V((s.CP, LANES), BF)),
        ("bt", V((LANES, 2 * s.T), F32)),
        ("gwi", V((s.slots, s.tile, s.F), F32)),
        ("gwo", V((s.slots, s.tile, s.D), F32)),
        ("gwi_sem", dma((s.slots,))),
        ("gwo_sem", dma((s.slots,))),
        ("lsem", dma((9,))),
        ("smr", dma((s.W,))),
        ("wa", dma((4, s.W))),
        ("wb", dma((4,))),
        ("wc", dma((4,))),
        ("g1", dma((s.C,))),
        ("g2", dma((s.W,))),
        ("n1", dma((s.C,))),
        ("n2", dma((s.W,))),
        ("t1", dma((s.C,))),
        ("t2", dma((s.W,))),
        ("s3", dma((s.W,))),
        ("r3", dma((s.W,))),
        ("back", dma((2,))),
        ("sibT", dma((2,))),
        ("sibF", dma((4,))),
        ("ra", dma((5,))),
        ("rb", dma((5,))),
        ("rc", dma((5,))),
        ("rd", dma((5,))),
        ("x_sm", dma),
        ("x_wa", dma((4,))),
        ("x_wb", dma((4,))),
        ("x_wc", dma((4,))),
        ("x_d1", dma((3,))),
        ("x_d2", dma((3,))),
        ("x_s3", dma((s.W,))),
        ("x_r3", dma((s.W,))),
        ("x_back", dma((2,))),
        ("x_sibT", dma((2,))),
        ("x_sibF", dma((4,))),
        ("x_ra", dma((5,))),
        ("x_rb", dma((5,))),
        ("x_rc", dma((5,))),
        ("x_rd", dma((5,))),
        ("credit", pltpu.SemaphoreType.REGULAR),
    ] + (
        [("gst", V((s.W * s.pr, s.half), BF))]
        + [(name, V((s.R, width), F32)) for name, width in arrivals(s)]
        if s.padded
        else [("GR", V(pieces_shape(s), BF))]
    )


IN_NAMES = (
    "lengths", "seq", "small", "ids", "prio", "table",
    "tokens", "out_grad", "w0", "w1", "w2", "w3", "w_in", "w_out",
)
PAD_NAMES = ("unsel",)
OUT_NAMES = ("layer_out", "tokens_grad", "grads", "smalls", "grad_w_in", "grad_w_out")


def kernel(s, names, *refs):
    r = types.SimpleNamespace(**dict(zip(names, refs, strict=True)))
    e = lax.axis_index("expert")
    z = lax.axis_index("wshard")
    c = lax.div(e, 2)
    k = lax.rem(e, 2)
    T, D, E, W, C, R, cp, half = s.T, s.D, s.E, s.W, s.C, s.R, s.cp, s.half
    sib = (flip(e, 1), z)
    here = pl.ds(aligned(k * half, LANES), half)
    there = pl.ds(aligned((1 - k) * half, LANES), half)

    def zpeer(offset):
        return (e, flip(z, offset))

    def cpeer(offset):
        return (flip(c, offset) * 2 + k, z)

    def remote(src, dst, send, recv, device):
        return pltpu.make_async_remote_copy(
            src_ref=src, dst_ref=dst, send_sem=send, recv_sem=recv, device_id=device, device_id_type=MESH
        )

    def got(ref, sem):
        remote(ref, ref, sem, sem, sib).wait_recv()

    def sent(ref, sem):
        remote(ref, ref, sem, sem, sib).wait_send()

    shards = (r.w0, r.w1, r.w2, r.w3)
    own_rows = pl.ds(aligned(z * s.SR, 16), s.SR)
    load_w = [
        pltpu.make_async_copy(shards[m].at[:, here], r.wfull.at[m, own_rows, here], r.lsem.at[m])
        for m in range(4)
    ]
    load_og = pltpu.make_async_copy(r.out_grad, r.og, r.lsem.at[4])
    load_x = pltpu.make_async_copy(r.tokens, r.xb, r.lsem.at[5])
    load_wo = pltpu.make_async_copy(r.w_out.at[0], r.wo, r.lsem.at[6])
    load_wi = pltpu.make_async_copy(r.w_in.at[0], r.wi, r.lsem.at[7])
    for copy in (*load_w, load_og, load_x, load_wo, load_wi):
        copy.start()

    barrier = pltpu.get_barrier_semaphore()
    peers = [(flip(e, o), z) for o in range(1, E)] + [zpeer(o) for o in range(1, W)]
    for peer in peers:
        pl.semaphore_signal(barrier, inc=1, device_id=peer, device_id_type=MESH)
    pl.semaphore_wait(barrier, len(peers))

    team_c = lax.rem(c, s.team)
    r.smg[z] = r.small[...]
    for o in range(1, W):
        remote(r.small, r.smg.at[z], r.x_sm, r.smr.at[o], zpeer(o)).start()
    piece = pl.ds(aligned(z * s.SR + team_c * s.pw, 16), s.pw)
    for m in range(4):
        load_w[m].wait()
        for o in range(1, W):
            part = r.wfull.at[m, piece, here]
            remote(part, part, r.x_wa.at[m], r.wa.at[m, o], zpeer(o)).start()

    device = e * W + z
    first = r.lengths[r.seq[2 * device]]
    both = first + r.lengths[r.seq[2 * device + 1]]
    col = iota((T, 1), 0)
    row = iota((1, T), 1)
    seg_col = (col >= first).astype(I32) + (col >= both).astype(I32)
    seg_row = (row >= first).astype(I32) + (row >= both).astype(I32)
    same = seg_col == seg_row
    valid = (col < both).astype(F32)
    eye = iota((T, T), 0) == iota((T, T), 1)
    id_col = r.ids[...].astype(F32)
    id_row = jnp.sum(jnp.where(eye, id_col, 0.0), axis=0, keepdims=True)
    prio_row = r.prio[...].astype(F32)
    prio_col = jnp.sum(jnp.where(eye, prio_row, 0.0), axis=1, keepdims=True)
    ahead = (id_col == id_row) & (prio_col < prio_row)
    slot_row = jnp.sum(jnp.where(ahead, valid, 0.0), axis=0, keepdims=True)
    kept = (row < both) & (slot_row < s.cap)
    flat_row = jnp.where(kept, id_row * cp + slot_row, -1.0)
    flat_col = jnp.sum(jnp.where(eye, flat_row, 0.0), axis=1, keepdims=True)
    r.pm[...] = (iota((s.S, T), 0).astype(F32) == flat_row).astype(F32).astype(BF)
    r.pt[...] = (iota((T, s.S), 1).astype(F32) == flat_col).astype(F32).astype(BF)

    plane_step = 16 if s.dt == BF else 8

    def dispatch(index, send, rows, first_sem, value):
        width = rows.shape[1]
        buffer = dot(r.pm[...], value)
        send[...] = buffer.astype(s.dt).reshape(s.NX, cp, width)
        mine = pl.ds(aligned(e * cp, plane_step), cp)
        for o in range(1, E):
            x = flip(e, o)
            remote(
                send.at[x], rows.at[mine], r.x_d1.at[index], first_sem.at[o // 2], (x, z)
            ).start()
        rows[mine, :] = send[e]

    def forward(index, rows, arrived, first_sem, second_sem):
        for oc in range(C):
            got(arrived.at[pl.ds(0, (2 if oc else 1) * cp)], first_sem.at[oc])
            at = flip(c, oc) * 2 * cp
            if s.dt != BF:
                block = pl.ds(aligned(at, 16), 2 * cp)
                rows[block, :] = arrived[block, :].astype(BF)
            for o in range(1, W):
                remote(
                    rows.at[pl.ds(aligned(at, 16), 2 * cp)],
                    rows.at[pl.ds(aligned(o * R + at, 16), 2 * cp)],
                    r.x_d2.at[index],
                    second_sem.at[o],
                    zpeer(o),
                ).start()

    Ga, Na, Ta = (r.Gr, r.Nr, r.Tr) if s.dt == BF else (r.Ga, r.Na, r.Ta)
    load_og.wait()
    dispatch(0, r.gsend, Ga, r.g1, r.og[...])

    def pass_on(m):
        for o in range(1, W):
            begin = flip(z, o) * s.SR + team_c * s.pw
            part = r.wfull.at[m, pl.ds(aligned(begin, 16), s.pw), here]
            got(part, r.wa.at[m, o])
            for oc in range(1, s.team):
                remote(part, part, r.x_wb.at[m], r.wb.at[m], cpeer(oc)).start()

    def to_sibling(m):
        if s.team > 1:
            got(r.wfull.at[m, pl.ds(0, (W - 1) * (s.team - 1) * s.pw), here], r.wb.at[m])
        part = r.wfull.at[m, :, here]
        remote(part, part, r.x_wc.at[m], r.wc.at[m], sib).start()

    def weight_ready(m):
        got(r.wfull.at[m, :, there], r.wc.at[m])

    for o in range(1, W):
        got(r.small, r.smr.at[o])
    pass_on(0)
    router_rows = r.smg[:, : s.SR, :].reshape(D, LANES)
    turned = router_rows.astype(F32).T
    r.rows[0:1, :] = turned[GAIN_ATTN_LANE : GAIN_ATTN_LANE + 1, :]
    r.rows[1:2, :] = turned[GAIN_FFN_LANE : GAIN_FFN_LANE + 1, :]
    lane_row = iota((1, LANES), 1)
    r.Rw[...] = router_rows * (lane_row < s.NX).astype(F32).astype(BF)
    bucket = r.table[...]
    shift = s.NBH.bit_length() - 1
    bucket = lax.shift_right_logical(bucket, shift) * s.NBP + lax.bitwise_and(bucket, s.NBH - 1)
    bucket_at = iota((W * s.NBP, 2 * T), 0)
    r.oh[...] = (bucket_at == bucket[0:1]).astype(F32).astype(BF)
    r.ohm[...] = (bucket_at == bucket[1:2]).astype(F32).astype(BF)
    bias_rows = r.smg[:, s.SR :, :].reshape(W * s.NBP, LANES)
    r.tb[...] = dot_lt(bias_rows, r.oh[...])

    def bias_head(h, carry):
        wide = jnp.broadcast_to(r.tb[pl.ds(h, 1), :], (T, 2 * T))
        turned = pltpu.roll(wide, T + 1, 1, stride=1, stride_axis=0)
        r.probs[h] = jnp.where(same, turned[:, :T], NEG_FILL)
        return carry

    third = s.H // 3
    pass_on(1)
    lax.fori_loop(0, third, bias_head, 0)
    pass_on(2)
    to_sibling(0)
    lax.fori_loop(third, 2 * third, bias_head, 0)
    to_sibling(1)
    pass_on(3)
    lax.fori_loop(2 * third, s.H, bias_head, 0)
    to_sibling(2)

    load_x.wait()
    x = r.xb[...].astype(F32)
    scale1 = lax.rsqrt(jnp.mean(x * x, axis=1, keepdims=True) + EPSILON)
    normed = (x * scale1 * r.rows[0:1, :]).astype(BF)

    def spread_rows(value):
        if not s.padded:
            return value
        shards = [value[at : at + s.SR] for at in range(0, D, s.SR)]
        return jnp.concatenate([dot_lt(r.unsel[...], shard) for shard in shards], axis=0).astype(BF)

    def turn_out(index, value, target):
        target[:, :T] = spread_rows(value.T)
        remote(
            target.at[:, pl.ds(0, T)], target.at[:, pl.ds(T, T)], r.x_sibT.at[index], r.sibT.at[index], sib
        ).start()

    turn_out(0, normed, r.nT)
    weight_ready(0)
    r.q[...] = dot(normed, r.wfull[0]).astype(BF)
    weight_ready(1)
    r.kk[...] = dot(normed, r.wfull[1]).astype(BF)
    to_sibling(3)
    weight_ready(2)
    r.v[...] = dot(normed, r.wfull[2]).astype(BF)
    forward(0, r.Gr, Ga, r.g1, r.g2)

    scale = s.HD ** (-0.5)
    low_lane = (lane_row < s.HD).astype(F32)
    lane_masks = (low_lane.astype(BF), (1.0 - low_lane).astype(BF))

    def attend(p, carry):
        cols = pl.ds(aligned(p * LANES, LANES), LANES)
        q, kk, v = r.q[:, cols], r.kk[:, cols], r.v[:, cols]
        outs = []
        for side in range(2):
            h = 2 * p + side
            scores = dot_rt(q * lane_masks[side], kk) * scale + r.probs[h]
            expo = jnp.exp(scores - jnp.max(scores, axis=1, keepdims=True))
            probs = expo * (1.0 / jnp.sum(expo, axis=1, keepdims=True))
            r.probs[h] = probs
            outs.append(dot(probs.astype(BF), v))
        r.mixed[:, cols] = jnp.where(lane_row < s.HD, outs[0], outs[1]).astype(BF)
        return carry

    lax.fori_loop(0, s.H // 2, attend, 0)
    mixed = r.mixed[...]
    weight_ready(3)
    middle = r.xb[...].astype(F32) + dot(mixed, r.wfull[3]) * valid
    r.middle[...] = middle
    scale2 = lax.rsqrt(jnp.mean(middle * middle, axis=1, keepdims=True) + EPSILON)
    nf = (middle * scale2 * r.rows[1:2, :]).astype(BF)
    r.nf[...] = nf
    dispatch(1, r.nsend, Na, r.n1, nf)
    logits = jnp.where(lane_row < s.NX, dot(nf, r.Rw[...]), NEG_FILL)
    raised = jnp.exp(logits - jnp.max(logits, axis=1, keepdims=True))
    router = raised / jnp.sum(raised, axis=1, keepdims=True)
    picked = (lane_row.astype(F32) == id_col).astype(F32)
    gate = jnp.sum(router * picked, axis=1, keepdims=True)
    gate_high, gate_rest = two_parts(gate)
    gate_mid, gate_low = two_parts(gate - gate_high.astype(F32))
    gate_lanes = jnp.where(
        lane_row == 0,
        gate_high.astype(F32),
        jnp.where(lane_row == 1, gate_mid.astype(F32), jnp.where(lane_row == 2, gate_low.astype(F32), 0.0)),
    )
    dispatch(2, r.tsend, Ta, r.t1, gate_lanes.astype(BF))
    forward(1, r.Nr, Na, r.n1, r.n2)
    forward(2, r.Tr, Ta, r.t1, r.t2)
    turn_out(1, mixed, r.mT)

    load_wo.wait()
    for o in range(1, W):
        got(r.Gr.at[pl.ds(0, R)], r.g2.at[o])

    def back_rows(step, carry):
        at = pl.ds(aligned(step * R, 16), R)
        r.agr[at, :] = dot_rt(r.Gr[at, :], r.wo[...]).astype(BF)
        return carry

    lax.fori_loop(0, W, back_rows, 0)
    load_wi.wait()

    def expert(step, carry):
        at = pl.ds(aligned(step * R, 16), R)

        @pl.when(step > 0)
        def _():
            got(r.Nr.at[pl.ds(0, R)], r.n2.at[step])

        inner = dot(r.Nr[at, :], r.wi[...])
        square = inner * inner
        tanh = jnp.tanh(GELU_A * inner * (1.0 + GELU_B * square))
        active = (0.5 * inner * (1.0 + tanh)).astype(BF)
        slope = 0.5 * (1.0 + tanh) + (0.5 * GELU_A) * inner * (1.0 - tanh * tanh) * (
            1.0 + (3.0 * GELU_B) * square
        )
        back = r.agr[at, :].astype(F32)
        inner_grad = (back * slope).astype(BF)
        r.act[at, :] = active
        r.ig[at, :] = inner_grad
        r.SS[step, :, :D] = dot_rt(inner_grad, r.wi[...]).astype(BF)
        high, rest = two_parts(jnp.sum(active.astype(F32) * back, axis=1, keepdims=True))
        r.SS[step, :, D:] = jnp.where(
            lane_row == 0, high.astype(F32), jnp.where(lane_row == 1, rest.astype(F32), 0.0)
        ).astype(BF)
        for o in range(1, W):

            @pl.when(step == o)
            def _():
                remote(r.SS.at[o], r.Sr.at[o - 1], r.x_s3.at[o], r.s3.at[o], zpeer(o)).start()

        return carry

    lax.fori_loop(0, W, expert, 0)

    sent(r.Gr.at[pl.ds(0, (W - 1) * R)], r.x_d2.at[0])
    sent(r.Nr.at[pl.ds(0, (W - 1) * R)], r.x_d2.at[1])
    for o in range(1, W):
        got(r.Tr.at[pl.ds(0, R)], r.t2.at[o])

    def scale_rows(step, carry):
        at = pl.ds(aligned(step * R, 16), R)
        gates = jnp.sum(r.Tr[at, :].astype(F32), axis=1, keepdims=True)
        r.Gr[at, :] = (r.Gr[at, :].astype(F32) * gates).astype(BF)
        r.ig[at, :] = (r.ig[at, :].astype(F32) * gates).astype(BF)
        return carry

    lax.fori_loop(0, W, scale_rows, 0)
    tile, slots = s.tile, s.slots

    def save_out(step):
        slot = lax.rem(step, slots)
        at = pl.ds(aligned(step * tile, LANES), tile)
        return pltpu.make_async_copy(r.gwo.at[slot], r.grad_w_out.at[0, at], r.gwo_sem.at[slot])

    def save_in(step):
        slot = lax.rem(step, slots)
        at = pl.ds(aligned(step * tile, LANES), tile)
        return pltpu.make_async_copy(r.gwi.at[slot], r.grad_w_in.at[0, at], r.gwi_sem.at[slot])

    def grad_out_tile(step, carry):
        @pl.when(step >= slots)
        def _():
            save_out(step - slots).wait()

        at = pl.ds(aligned(step * tile, LANES), tile)
        r.gwo[lax.rem(step, slots)] = dot_lt(r.act[:, at], r.Gr[...])
        save_out(step).start()
        return carry

    def grad_in_tile(step, carry):
        @pl.when(step >= slots)
        def _():
            save_in(step - slots).wait()

        at = pl.ds(aligned(step * tile, LANES), tile)
        r.gwi[lax.rem(step, slots)] = dot_lt(r.Nr[:, at], r.ig[...])
        save_in(step).start()
        return carry

    lax.fori_loop(0, s.F // tile, grad_out_tile, 0)
    lax.fori_loop(0, D // tile, grad_in_tile, 0)

    def plane_back(index, source, target):
        mine = pl.ds(aligned(e * cp, plane_step), cp)
        for o in range(1, E):
            x = flip(e, o)
            remote(
                source.at[pl.ds(aligned(x * cp, plane_step), cp)],
                target.at[mine],
                r.x_back.at[index],
                r.back.at[index],
                (x, z),
            ).start()
        target[mine, :] = source[mine, :]

    total = r.SS[0].astype(F32)
    for o in range(1, W):
        got(r.Sr.at[o - 1], r.s3.at[o])
        total = total + r.Sr[o - 1].astype(F32)
    high, rest = two_parts(jnp.sum(total[:, D:], axis=1, keepdims=True))
    r.Sb[:, :D] = total[:, :D].astype(BF).astype(s.dt)
    r.Sb[:, D:] = jnp.where(
        lane_row == 0, high.astype(F32), jnp.where(lane_row == 1, rest.astype(F32), 0.0)
    ).astype(s.dt)
    for o in range(1, W):
        pl.semaphore_signal(r.credit, inc=1, device_id=zpeer(o), device_id_type=MESH)
    plane_back(0, r.Sb, r.Sk)

    for o in range(1, W):
        sent(r.SS.at[o], r.x_s3.at[o])
    pl.semaphore_wait(r.credit, W - 1)

    def results(step, carry):
        at = pl.ds(aligned(step * R, 16), R)
        r.SS[step, :, :D] = dot(r.act[at, :], r.wo[...]).astype(BF)
        for o in range(1, W):

            @pl.when(step == o)
            def _():
                remote(
                    r.SS.at[o, :, pl.ds(0, D)],
                    r.Sr.at[o - 1, :, pl.ds(0, D)],
                    r.x_r3.at[o],
                    r.r3.at[o],
                    zpeer(o),
                ).start()

        return carry

    lax.fori_loop(0, W, results, 0)

    got(r.Sk.at[pl.ds(0, (E - 1) * cp)], r.back.at[0])
    returned = dot(r.pt[...], r.Sk[...].astype(BF))
    gate_grad = jnp.sum(returned[:, D:], axis=1, keepdims=True)
    logit_grad = (gate * gate_grad * (picked - router)).astype(BF)
    nf_grad = dot_rt(logit_grad, r.Rw[...]) + gate * returned[:, :D]
    middle = r.middle[...]
    along = nf_grad * r.rows[1:2, :]
    middle_grad = (
        r.og[...].astype(F32)
        + scale2 * along
        - middle * (scale2 * scale2 * scale2 * jnp.mean(along * middle, axis=1, keepdims=True))
    )
    r.mg[...] = middle_grad
    r.rows[2:3, :] = jnp.sum(nf_grad * middle * scale2, axis=0, keepdims=True)
    r.att[...] = (middle_grad * valid).astype(BF)
    attended_grad = r.att[...]

    def share(m, source):
        remote(source.at[:, there], r.fac.at[m], r.x_sibF.at[m], r.sibF.at[m], sib).start()

    share(3, r.att)
    r.mixed[...] = dot_rt(attended_grad, r.wfull[3]).astype(BF)
    router_grad = dot_lt(logit_grad, r.nf[...])

    def plane_sum(m, left, source):
        got(r.fac.at[m], r.sibF.at[m])

        def block(step, carry):
            at = pl.ds(aligned(step * s.CP, 16), s.CP)
            part = dot(left[at, :T], source[:, here]) + dot(left[at, T:], r.fac[m])
            part = part.astype(BF)
            for chip in range(C):
                r.GS[m, chip, pl.ds(aligned(step * s.pr, 16), s.pr), :] = part[
                    chip * s.pr : (chip + 1) * s.pr
                ]
            return carry

        lax.fori_loop(0, W, block, 0)
        for oc in range(1, C):
            remote(
                r.GS.at[m, flip(c, oc)], r.GR.at[m, oc - 1], r.x_ra.at[m], r.ra.at[m], cpeer(oc)
            ).start()

    got(r.mT.at[:, pl.ds(T, T)], r.sibT.at[1])
    plane_sum(3, r.mT, r.att)

    def attend_back(p, carry):
        cols = pl.ds(aligned(p * LANES, LANES), LANES)
        q, kk, v, mixg = r.q[:, cols], r.kk[:, cols], r.v[:, cols], r.mixed[:, cols]
        outs = []
        for side in range(2):
            h = 2 * p + side
            probs = r.probs[h]
            prob_grad = dot_rt(mixg * lane_masks[side], v)
            inside = jnp.sum(probs * prob_grad, axis=1, keepdims=True)
            score_grad = (probs * (prob_grad - inside)).astype(BF)
            r.probs[h] = score_grad.astype(F32)
            outs.append(
                (
                    dot(score_grad, kk) * scale,
                    dot_lt(score_grad, q) * scale,
                    dot_lt(probs.astype(BF), mixg),
                )
            )
        low = lane_row < s.HD
        r.dq[:, cols] = jnp.where(low, outs[0][0], outs[1][0]).astype(BF)
        r.dk[:, cols] = jnp.where(low, outs[0][1], outs[1][1]).astype(BF)
        r.dv[:, cols] = jnp.where(low, outs[0][2], outs[1][2]).astype(BF)
        return carry

    lax.fori_loop(0, s.H // 2, attend_back, 0)
    share(0, r.dq)
    share(1, r.dk)
    share(2, r.dv)
    got(r.nT.at[:, pl.ds(T, T)], r.sibT.at[0])
    plane_sum(0, r.nT, r.dq)
    plane_sum(1, r.nT, r.dk)
    plane_sum(2, r.nT, r.dv)

    def shard_sum(m):
        got(r.GR.at[m], r.ra.at[m])
        total = r.GS[m, c].astype(F32)
        for oc in range(1, C):
            if s.padded:
                fetch = pltpu.make_async_copy(r.GR.at[m, oc - 1], r.gst, r.lsem.at[8])
                fetch.start()
                fetch.wait()
            part = r.gst[...] if s.padded else r.GR[m, oc - 1]
            total = total + part.astype(F32)
        r.ZS[m] = total.astype(BF)
        for o in range(1, W):
            remote(
                r.ZS.at[m, pl.ds(aligned(flip(z, o) * s.pr, 16), s.pr)],
                r.ZR.at[m, o - 1],
                r.x_rb.at[m],
                r.rb.at[m],
                zpeer(o),
            ).start()

    def spread(m):
        got(r.ZR.at[m], r.rb.at[m])
        total = r.ZS[m, pl.ds(aligned(z * s.pr, 16), s.pr), :].astype(F32)
        for o in range(1, W):
            total = total + r.ZR[m, o - 1].astype(F32)
        mine = pl.ds(aligned(c * s.pr, 16), s.pr)
        r.FG[m, mine, here] = total.astype(BF)
        part = r.FG.at[m, mine, here]
        for oc in range(1, C):
            remote(part, part, r.x_rc.at[m], r.rc.at[m], cpeer(oc)).start()

    def share_sum(m):
        got(r.FG.at[m, pl.ds(0, (C - 1) * s.pr), here], r.rc.at[m])
        part = r.FG.at[m, :, here]
        remote(part, part, r.x_rd.at[m], r.rd.at[m], sib).start()

    shard_sum(3)

    normed_grad = (
        dot_rt(r.dq[...], r.wfull[0]) + dot_rt(r.dk[...], r.wfull[1]) + dot_rt(r.dv[...], r.wfull[2])
    )
    x = r.xb[...].astype(F32)
    along = normed_grad * r.rows[0:1, :]
    r.tokens_grad[...] = (
        r.mg[...]
        + scale1 * along
        - x * (scale1 * scale1 * scale1 * jnp.mean(along * x, axis=1, keepdims=True))
    )
    r.rows[3:4, :] = jnp.sum(normed_grad * x * scale1, axis=0, keepdims=True)

    r.bt[...] = jnp.zeros_like(r.bt)
    mirror = (iota((T, T), 0) + iota((T, T), 1) == T - 1).astype(F32).astype(BF)

    def bias_back(h, carry):
        mirrored = dot(r.probs[h].astype(BF), mirror)
        wide = jnp.concatenate([mirrored, jnp.zeros((T, T), F32)], axis=1)
        turned = pltpu.roll(wide, 0, 1, stride=1, stride_axis=0)
        r.bt[pl.ds(REL_LANE + h, 1), :] = jnp.sum(turned, axis=0, keepdims=True)
        return carry

    lax.fori_loop(0, s.H, bias_back, 0)
    high, rest = two_parts(r.bt[...])
    rel_grad = dot_rt(r.ohm[...], high) + dot_rt(r.ohm[...], rest)
    lane_col = iota((LANES, 1), 0)
    small = jnp.where(
        lane_col == GAIN_ATTN_LANE,
        r.rows[3:4, :],
        jnp.where(lane_col == GAIN_FFN_LANE, r.rows[2:3, :], router_grad),
    ).T
    blocks = []
    for block in range(W):
        part = small[block * s.SR : (block + 1) * s.SR]
        head = part[: s.NBP] + rel_grad[block * s.NBP : (block + 1) * s.NBP]
        blocks.append(jnp.concatenate([head, part[s.NBP :]], axis=0))
    small = jnp.concatenate(blocks, axis=0).astype(BF)
    r.smo[...] = spread_rows(small)
    remote(r.smo, r.sms, r.x_rd.at[4], r.rd.at[4], sib).start()
    shard_sum(0)
    shard_sum(1)
    shard_sum(2)
    got(r.sms, r.rd.at[4])
    pair = (r.smo[...].astype(F32) + r.sms[...].astype(F32)).astype(BF)
    for block in range(W):
        for chip in range(C):
            at = block * s.CP + chip * s.pr
            r.hGS[chip, block * s.pr : (block + 1) * s.pr, :] = pair[at : at + s.pr]
    for oc in range(1, C):
        remote(r.hGS.at[flip(c, oc)], r.hGR.at[oc - 1], r.x_ra.at[4], r.ra.at[4], cpeer(oc)).start()
    spread(3)

    total = r.SS[0, :, :D].astype(F32)
    for o in range(1, W):
        got(r.Sr.at[o - 1, :, pl.ds(0, D)], r.r3.at[o])
        total = total + r.Sr[o - 1, :, :D].astype(F32)
    r.Rb[...] = total.astype(BF).astype(s.dt)
    plane_back(1, r.Rb, r.Rk)

    got(r.hGR, r.ra.at[4])
    total = r.hGS[c].astype(F32)
    for oc in range(1, C):
        total = total + r.hGR[oc - 1].astype(F32)
    r.hZS[...] = total.astype(BF)
    for o in range(1, W):
        remote(
            r.hZS.at[pl.ds(aligned(flip(z, o) * s.pr, 16), s.pr)],
            r.hZR.at[o - 1],
            r.x_rb.at[4],
            r.rb.at[4],
            zpeer(o),
        ).start()
    spread(0)
    spread(1)
    spread(2)
    share_sum(3)
    got(r.hZR, r.rb.at[4])
    total = r.hZS[pl.ds(aligned(z * s.pr, 16), s.pr), :].astype(F32)
    for o in range(1, W):
        total = total + r.hZR[o - 1].astype(F32)
    mine = pl.ds(aligned(c * s.pr, 16), s.pr)
    r.hFG[mine, :] = total.astype(BF)
    for oc in range(1, C):
        part = r.hFG.at[mine]
        remote(part, part, r.x_rc.at[4], r.rc.at[4], cpeer(oc)).start()

    got(r.Rk.at[pl.ds(0, (E - 1) * cp)], r.back.at[1])
    r.layer_out[...] = (r.middle[...] + gate * dot(r.pt[...], r.Rk[...].astype(BF))).astype(BF)

    share_sum(0)
    share_sum(1)
    share_sum(2)
    got(r.hFG.at[pl.ds(0, (C - 1) * s.pr)], r.rc.at[4])

    def unpad(value):
        return dot(r.unsel[...], value) if s.padded else value.astype(F32)

    r.smalls[...] = unpad(r.hFG[...])
    for m in (3, 0, 1, 2):
        got(r.FG.at[m, :, there], r.rd.at[m])
        r.grads[m] = unpad(r.FG[m]).astype(r.grads.dtype)

    for step in range(max(0, s.F // tile - slots), s.F // tile):
        save_out(step).wait()
    for step in range(max(0, D // tile - slots), D // tile):
        save_in(step).wait()
    sent(r.smg.at[pl.ds(0, W - 1)], r.x_sm)
    for m in range(4):
        sent(r.wfull.at[m, pl.ds(0, (W - 1) * s.pw), here], r.x_wa.at[m])
        if s.team > 1:
            sent(r.wfull.at[m, pl.ds(0, (W - 1) * (s.team - 1) * s.pw), here], r.x_wb.at[m])
        sent(r.wfull.at[m, :, here], r.x_wc.at[m])
        sent(r.fac.at[m], r.x_sibF.at[m])
        sent(r.GR.at[m], r.x_ra.at[m])
        sent(r.ZR.at[m], r.x_rb.at[m])
        sent(r.FG.at[m, pl.ds(0, (C - 1) * s.pr), here], r.x_rc.at[m])
        sent(r.FG.at[m, :, here], r.x_rd.at[m])
    for index, buffer in enumerate((r.gsend, r.nsend, r.tsend)):
        sent(buffer.at[pl.ds(0, E - 1)], r.x_d1.at[index])
    sent(r.Tr.at[pl.ds(0, (W - 1) * R)], r.x_d2.at[2])
    for o in range(1, W):
        sent(r.SS.at[o, :, pl.ds(0, D)], r.x_r3.at[o])
    sent(r.Sk.at[pl.ds(0, (E - 1) * cp)], r.x_back.at[0])
    sent(r.Rk.at[pl.ds(0, (E - 1) * cp)], r.x_back.at[1])
    sent(r.nT.at[:, pl.ds(0, T)], r.x_sibT.at[0])
    sent(r.mT.at[:, pl.ds(0, T)], r.x_sibT.at[1])
    sent(r.hGR, r.x_ra.at[4])
    sent(r.hZR, r.x_rb.at[4])
    sent(r.hFG.at[pl.ds(0, (C - 1) * s.pr)], r.x_rc.at[4])
    sent(r.smo, r.x_rd.at[4])


def selection(s):
    share = s.SR // s.C
    unsel = np.zeros((s.SR, s.CP), np.float32)
    for chip in range(s.C):
        for at in range(share):
            unsel[chip * share + at, chip * s.pr + at] = 1
    return jnp.asarray(unsel, BF)


def local(
    tokens,
    norm_gain_attn,
    w_query,
    w_key,
    w_value,
    w_output,
    rel_bias,
    norm_gain_ffn,
    w_router,
    w_in,
    w_out,
    out_grad,
    expert_ids,
    priority,
    lengths,
    seq_order,
    relpos_table,
):
    tok_count, width = tokens.shape
    buckets_here, heads = rel_bias.shape
    n_experts = w_router.shape[1]
    s = plan(
        lax.axis_size("expert"),
        lax.axis_size("wshard"),
        tok_count,
        width,
        heads,
        buckets_here,
        n_experts,
        w_in.shape[2],
    )
    gap = jnp.zeros((s.SR, GAIN_ATTN_LANE - n_experts), BF)
    small = jnp.concatenate(
        [w_router, gap, norm_gain_attn[:, None], norm_gain_ffn[:, None]], axis=1
    )
    bias = jnp.pad(rel_bias, ((0, s.NBP - buckets_here), (0, LANES - heads)))
    small = jnp.concatenate([small, bias], axis=0)
    table = jnp.pad(jnp.stack([relpos_table, relpos_table[::-1]]), ((0, 0), (0, 1)))
    operands = [
        lengths, seq_order, small, expert_ids, priority.reshape(1, tok_count), table,
        tokens, out_grad, w_query, w_key, w_value, w_output, w_in, w_out,
    ]
    smem, vmem, anywhere = (
        pl.BlockSpec(memory_space=space) for space in (pltpu.SMEM, pltpu.VMEM, pl.ANY)
    )
    in_specs = [smem] * 2 + [vmem] * 4 + [anywhere] * 8
    names = IN_NAMES
    if s.padded:
        operands.append(selection(s))
        in_specs.append(vmem)
        names = names + PAD_NAMES
    spilled = (jax.ShapeDtypeStruct(pieces_shape(s), BF),) if s.padded else ()
    scratch = scratch_list(s)
    names = names + OUT_NAMES + ("GR",) * len(spilled) + tuple(name for name, _ in scratch)
    outs = pl.pallas_call(
        functools.partial(kernel, s, names),
        name="layer",
        out_shape=(
            jax.ShapeDtypeStruct((s.T, s.D), BF),
            jax.ShapeDtypeStruct((s.T, s.D), F32),
            jax.ShapeDtypeStruct((4, s.SR, s.D), BF),
            jax.ShapeDtypeStruct((s.SR, LANES), F32),
            jax.ShapeDtypeStruct((1, s.D, s.F), F32),
            jax.ShapeDtypeStruct((1, s.F, s.D), F32),
            *spilled,
        ),
        in_specs=in_specs,
        out_specs=(vmem, vmem, vmem, vmem, anywhere, anywhere) + (anywhere,) * len(spilled),
        scratch_shapes=[shape for _, shape in scratch],
        compiler_params=pltpu.CompilerParams(
            collective_id=0, has_side_effects=True, vmem_limit_bytes=62 * 2**20
        ),
    )(*operands)
    layer_out, tokens_grad, grads, smalls, grad_w_in, grad_w_out = outs[:6]
    return (
        layer_out,
        tokens_grad,
        smalls[:, GAIN_ATTN_LANE],
        grads[0].astype(F32),
        grads[1].astype(F32),
        grads[2].astype(F32),
        grads[3].astype(F32),
        smalls[:buckets_here, REL_LANE : REL_LANE + heads],
        smalls[:, GAIN_FFN_LANE],
        smalls[:, :n_experts],
        grad_w_in,
        grad_w_out,
    )


def solution(mesh):
    rows = P(("expert", "wshard"), None)
    shard = P("wshard", None)
    into, outof = P("expert", None, "wshard"), P("expert", "wshard", None)
    return jax.shard_map(
        local,
        mesh=mesh,
        in_specs=(
            rows,
            P("wshard"),
            shard,
            shard,
            shard,
            shard,
            shard,
            P("wshard"),
            shard,
            into,
            outof,
            rows,
            rows,
            P(("expert", "wshard")),
            P(),
            P(),
            P(),
        ),
        out_specs=(
            rows,
            rows,
            P("wshard"),
            shard,
            shard,
            shard,
            shard,
            shard,
            P("wshard"),
            shard,
            into,
            outof,
        ),
        check_vma=False,
    )
```

time: 1390 us -> 232 us (0.17)
  local copies, waits for them, and re-layouts: 964 us -> 15.5 us
  Pallas kernels: 0 us -> 210 us
  waiting for transfers between devices: 198 us -> 0 us
  blocking collectives: 103 us -> 0 us
  matrix products: 65.1 us -> 0 us
  between operations: 22.7 us -> 0.71 us
  other arithmetic: 22.4 us -> 4.93 us
    gather x7 -> x0, local copies, waits for them, and re-layouts: 930 us -> none  [the longest x1 689 us: local(): relpos_table[block_offsets(tok_count, begin)].reshape(rows * tok_count)]
    pallas_call x0 -> x1, Pallas kernels: none -> 210 us  [local(): pl.pallas_call(functools.partial(kernel, s, names), name='layer', out_sha...]
    reduce_scatter x6 -> x0, waiting for transfers between devices: 109 us -> none  [the longest x1 57 us: local(): lax.psum_scatter(jnp.einsum('rxf,xfd->rxd', part, w_out, preferred_elemen...]
    dot_general x28 -> x0, matrix products: 64 us -> none  [the longest x1 5.62 us: local(): jnp.einsum('rxf,xfd->rxd', part, w_out, preferred_element_type=jnp.float32)]
    all_gather x6 -> x0, waiting for transfers between devices: 51.2 us -> none  [the longest x1 32.9 us: local(): grad_all = lax.all_gather(grad_local, 'wshard', axis=0, tiled=True)]
    unnamed x2 -> x0, blocking collectives: 31.6 us -> none
    psum x1 -> x0, waiting for transfers between devices: 27.9 us -> none  [local(): lax.psum((shard_grads[0], shard_grads[1], shard_grads[2], shard_grads[3],...]
    all_gather x2 -> x0, blocking collectives: 25.1 us -> none  [the longest x1 13.1 us: local(): lax.all_gather(mixer_shards[7], 'wshard', axis=0, tiled=True)]
  transfers between devices with their start and end apart: 16 -> 0, of which waited for: 6 -> 0; matrix products, arithmetic and copies ran while one was open for 73% -> 0% of each run, Pallas kernels for 0% -> 0%
where the time goes in v2:
time: 232 us; the launch traced here: 231 us
  Pallas kernels  210 us (91%)
  local copies, waits for them, and re-layouts  15.5 us (7%)
  other arithmetic  4.93 us (2%)
    pallas_call x1, Pallas kernels, local(): pl.pallas_call(functools.partial(kernel, s, names), name='layer', out_sha...  210 us
    unnamed x17, local copies, waits for them, and re-layouts  10.3 us

profile of v2, /device:TPU:0, one launch (start us, length us, event | category | flops | bytes accessed | tf_op | source)
XLA Modules:
  0.0 231.1 jit_solution(1559434312791033861)
XLA Ops:
  0.6 0.8 reverse
  1.4 0.1 slice.38
  1.5 0.7 pad_add_fusion
  2.2 0.6 pad.9.refs_5_
  2.8 0.7 broadcast_in_dim.12
  3.5 0.7 broadcast_in_dim.13
  4.3 0.8 copy.32
  5.1 1.4 fusion.1.refs_2_
  6.5 1.5 copy.35.refs_3_
  8.0 210.0 %layer.1 = (bf16[256,768]{1,0:T(8,128)(2,1)}, f32[256,768]{1,0:T(8,128)}, bf16[4,192,768]{2,1,0:T(8,128)(2,1)}, f32[192,128]{1,0:T(8,128)}, f32[1,768,768]{2,1,0:T(8,128)}, /*index=5*/f32[1,768,768]{2,1,0:T(8,128)}) custom-call(s32[64]{0:T(128)} %refs_0_.1, s32[64]{0:T(128)} %refs_1_.1, bf16[208,128]{1,0:T(8,128)(2,1)} %fusion.1.refs_2_, ...), custom_call_target="tpu_custom_call" | custom-call | tf_op jit(solution)/shard_map/layer/pallas_call | solution.py:911
  218.0 0.0 copy-start.3
  218.0 0.0 copy-start.2
  218.0 1.8 slice_reduce_fusion
  219.9 1.3 slice.29
  221.2 1.6 copy.36
  222.8 0.0 copy-start.1
  222.8 2.8 %bitcast_convert_fusion = (f32[192,768]{1,0:T(8,128)}, f32[192,768]{1,0:T(8,128)}, f32[192,768]{1,0:T(8,128)}, f32[192,768]{1,0:T(8,128)}) fusion(bf16[4,192,768]{2,1,0:T(8,128)(2,1)} %get-tuple-element.21), kind=kLoop, calls=%fused_computation | loop fusion | flops 589824 | bytes 3538944 | tf_op jit(solution)/shard_map/convert_element_type | solution.py:938
  225.6 0.0 copy-done.3
  225.6 0.7 copy.41
  226.3 0.0 copy-done.2
  226.3 0.9 copy.42
  227.2 0.0 copy-done.1
  227.2 0.0 copy-start
  227.2 1.4 copy.43
  228.6 1.1 copy-done
  229.7 1.4 copy.44
  (1 shorter events, 0.0 us)
Async XLA Ops:
  218.0 7.6 %copy-start.3 = (bf16[256,768]{1,0:T(8,128)(2,1)S(1)}, bf16[256,768]{1,0:T(8,128)(2,1)}, u32[]{:S(2)}) copy-start(bf16[256,768]{1,0:T(8,128)(2,1)} %get-tuple-element.66) | copy-start | bytes 1179652
  218.0 8.3 %copy-start.2 = (f32[256,768]{1,0:T(8,128)S(1)}, f32[256,768]{1,0:T(8,128)}, u32[]{:S(2)}) copy-start(f32[256,768]{1,0:T(8,128)} %get-tuple-element.67) | copy-start | bytes 2359300
  222.8 4.5 %copy-start.1 = (f32[1,768,768]{2,1,0:T(8,128)S(1)}, f32[1,768,768]{2,1,0:T(8,128)}, u32[]{:S(2)}) copy-start(f32[1,768,768]{2,1,0:T(8,128)} %get-tuple-element.76) | copy-start | bytes 7077892
  227.2 2.5 %copy-start = (f32[1,768,768]{2,1,0:T(8,128)S(1)}, f32[1,768,768]{2,1,0:T(8,128)}, u32[]{:S(2)}) copy-start(f32[1,768,768]{2,1,0:T(8,128)} %get-tuple-element.77) | copy-start | bytes 7077892

commit v3 on v2

--- a/solution.py
+++ b/solution.py
@@ -123,7 +123,7 @@
         ("act", V((s.W * s.R, s.F), BF)),
         ("ig", V((s.W * s.R, s.F), BF)),
         ("SS", V((s.W, s.R, s.D + LANES), BF)),
-        ("Sr", V((s.W - 1, s.R, s.D + LANES), BF)),
+        ("Sin", V((s.W + 1, s.R, s.D + LANES), BF)),
         ("Sb", V((s.R, s.D + LANES), s.dt)),
         ("Sk", V((s.S, s.D + LANES), s.dt)),
         ("Rb", V((s.R, s.D), s.dt)),
@@ -170,12 +170,15 @@
         ("wb", dma((4,))),
         ("wc", dma((4,))),
         ("g1", dma((s.C,))),
-        ("g2", dma((s.W,))),
+        ("gu", dma((s.W, s.C))),
+        ("gd", dma((s.W, s.C))),
         ("n1", dma((s.C,))),
-        ("n2", dma((s.W,))),
+        ("nu", dma((s.W, s.C))),
+        ("nd", dma((s.W, s.C))),
         ("t1", dma((s.C,))),
         ("t2", dma((s.W,))),
-        ("s3", dma((s.W,))),
+        ("su", dma((s.W, s.C))),
+        ("sd", dma((s.W, s.C))),
         ("r3", dma((s.W,))),
         ("back", dma((2,))),
         ("sibT", dma((2,))),
@@ -189,8 +192,13 @@
         ("x_wb", dma((4,))),
         ("x_wc", dma((4,))),
         ("x_d1", dma((3,))),
-        ("x_d2", dma((3,))),
-        ("x_s3", dma((s.W,))),
+        ("x_t2", dma),
+        ("x_gu", dma((s.W,))),
+        ("x_gd", dma((s.W,))),
+        ("x_nu", dma((s.W,))),
+        ("x_nd", dma((s.W,))),
+        ("x_su", dma((s.W,))),
+        ("x_sd", dma((s.W,))),
         ("x_r3", dma((s.W,))),
         ("x_back", dma((2,))),
         ("x_sibT", dma((2,))),
@@ -268,11 +276,16 @@
     for o in range(1, W):
         remote(r.small, r.smg.at[z], r.x_sm, r.smr.at[o], zpeer(o)).start()
     piece = pl.ds(aligned(z * s.SR + team_c * s.pw, 16), s.pw)
+    share_rows = pl.ds(aligned(team_c * s.pw, 16), s.pw)
     for m in range(4):
-        load_w[m].wait()
         for o in range(1, W):
-            part = r.wfull.at[m, piece, here]
-            remote(part, part, r.x_wa.at[m], r.wa.at[m, o], zpeer(o)).start()
+            remote(
+                shards[m].at[share_rows, here],
+                r.wfull.at[m, piece, here],
+                r.x_wa.at[m],
+                r.wa.at[m, o],
+                zpeer(o),
+            ).start()
 
     device = e * W + z
     first = r.lengths[r.seq[2 * device]]
@@ -297,12 +310,13 @@
     r.pt[...] = (iota((T, s.S), 1).astype(F32) == flat_col).astype(F32).astype(BF)
 
     plane_step = 16 if s.dt == BF else 8
+    plane_rows = z * R if s.dt == BF else 0
 
     def dispatch(index, send, rows, first_sem, value):
         width = rows.shape[1]
         buffer = dot(r.pm[...], value)
         send[...] = buffer.astype(s.dt).reshape(s.NX, cp, width)
-        mine = pl.ds(aligned(e * cp, plane_step), cp)
+        mine = pl.ds(aligned(plane_rows + e * cp, plane_step), cp)
         for o in range(1, E):
             x = flip(e, o)
             remote(
@@ -310,22 +324,53 @@
             ).start()
         rows[mine, :] = send[e]
 
-    def forward(index, rows, arrived, first_sem, second_sem):
+    def block_at(plane, oc):
+        return pl.ds(aligned(plane * R + flip(c, oc) * 2 * cp, 16), 2 * cp)
+
+    def landed(rows, arrived, first_sem, oc):
+        got(arrived.at[pl.ds(0, (2 if oc else 1) * cp)], first_sem.at[oc])
+        if s.dt != BF:
+            rows[block_at(z, oc), :] = arrived[block_at(0, oc), :].astype(BF)
+
+    def move(part, send, recv, to):
+        remote(part, part, send, recv, (e, to)).start()
+
+    def line_own(rows, arrived, first_sem, up, down, x_up, x_down):
         for oc in range(C):
-            got(arrived.at[pl.ds(0, (2 if oc else 1) * cp)], first_sem.at[oc])
-            at = flip(c, oc) * 2 * cp
-            if s.dt != BF:
-                block = pl.ds(aligned(at, 16), 2 * cp)
-                rows[block, :] = arrived[block, :].astype(BF)
-            for o in range(1, W):
-                remote(
-                    rows.at[pl.ds(aligned(at, 16), 2 * cp)],
-                    rows.at[pl.ds(aligned(o * R + at, 16), 2 * cp)],
-                    r.x_d2.at[index],
-                    second_sem.at[o],
-                    zpeer(o),
-                ).start()
-
+            landed(rows, arrived, first_sem, oc)
+            part = rows.at[block_at(z, oc)]
+            pl.when(z < W - 1)(functools.partial(move, part, x_up.at[0], up.at[1, oc], z + 1))
+            pl.when(z > 0)(functools.partial(move, part, x_down.at[0], down.at[1, oc], z - 1))
+
+    def line_pass(rows, d, up, down, x_up, x_down):
+        for oc in range(C):
+
+            @pl.when(z >= d)
+            def _():
+                part = rows.at[block_at(z - d, oc)]
+                got(part, up.at[d, oc])
+                if d < W - 1:
+                    pl.when(z < W - 1)(
+                        functools.partial(move, part, x_up.at[d], up.at[d + 1, oc], z + 1)
+                    )
+
+            @pl.when(z + d <= W - 1)
+            def _():
+                part = rows.at[block_at(z + d, oc)]
+                got(part, down.at[d, oc])
+                if d < W - 1:
+                    pl.when(z > 0)(
+                        functools.partial(move, part, x_down.at[d], down.at[d + 1, oc], z - 1)
+                    )
+
+    def line_sent(rows, x_up, x_down):
+        for d in range(W - 1):
+            whole = rows.at[pl.ds(0, R)]
+            pl.when((z >= d) & (z < W - 1))(functools.partial(sent, whole, x_up.at[d]))
+            pl.when((z + d <= W - 1) & (z > 0))(functools.partial(sent, whole, x_down.at[d]))
+
+    g_line = (r.gu, r.gd, r.x_gu, r.x_gd)
+    n_line = (r.nu, r.nd, r.x_nu, r.x_nd)
     Ga, Na, Ta = (r.Gr, r.Nr, r.Tr) if s.dt == BF else (r.Ga, r.Na, r.Ta)
     load_og.wait()
     dispatch(0, r.gsend, Ga, r.g1, r.og[...])
@@ -341,6 +386,7 @@
     def to_sibling(m):
         if s.team > 1:
             got(r.wfull.at[m, pl.ds(0, (W - 1) * (s.team - 1) * s.pw), here], r.wb.at[m])
+        load_w[m].wait()
         part = r.wfull.at[m, :, here]
         remote(part, part, r.x_wc.at[m], r.wc.at[m], sib).start()
 
@@ -378,6 +424,7 @@
     to_sibling(0)
     lax.fori_loop(third, 2 * third, bias_head, 0)
     to_sibling(1)
+    line_own(r.Gr, Ga, r.g1, *g_line)
     pass_on(3)
     lax.fori_loop(2 * third, s.H, bias_head, 0)
     to_sibling(2)
@@ -407,7 +454,7 @@
     to_sibling(3)
     weight_ready(2)
     r.v[...] = dot(normed, r.wfull[2]).astype(BF)
-    forward(0, r.Gr, Ga, r.g1, r.g2)
+    line_pass(r.Gr, 1, *g_line)
 
     scale = s.HD ** (-0.5)
     low_lane = (lane_row < s.HD).astype(F32)
@@ -429,6 +476,8 @@
 
     lax.fori_loop(0, s.H // 2, attend, 0)
     mixed = r.mixed[...]
+    if W > 2:
+        line_pass(r.Gr, 2, *g_line)
     weight_ready(3)
     middle = r.xb[...].astype(F32) + dot(mixed, r.wfull[3]) * valid
     r.middle[...] = middle
@@ -449,13 +498,17 @@
         jnp.where(lane_row == 1, gate_mid.astype(F32), jnp.where(lane_row == 2, gate_low.astype(F32), 0.0)),
     )
     dispatch(2, r.tsend, Ta, r.t1, gate_lanes.astype(BF))
-    forward(1, r.Nr, Na, r.n1, r.n2)
-    forward(2, r.Tr, Ta, r.t1, r.t2)
+    line_own(r.Nr, Na, r.n1, *n_line)
+    for oc in range(C):
+        landed(r.Tr, Ta, r.t1, oc)
+        for o in range(1, W):
+            part = r.Tr.at[block_at(z, oc)]
+            remote(part, part, r.x_t2, r.t2.at[o], zpeer(o)).start()
     turn_out(1, mixed, r.mT)
 
     load_wo.wait()
-    for o in range(1, W):
-        got(r.Gr.at[pl.ds(0, R)], r.g2.at[o])
+    for d in range(3, W):
+        line_pass(r.Gr, d, *g_line)
 
     def back_rows(step, carry):
         at = pl.ds(aligned(step * R, 16), R)
@@ -465,13 +518,14 @@
     lax.fori_loop(0, W, back_rows, 0)
     load_wi.wait()
 
-    def expert(step, carry):
-        at = pl.ds(aligned(step * R, 16), R)
-
-        @pl.when(step > 0)
-        def _():
-            got(r.Nr.at[pl.ds(0, R)], r.n2.at[step])
-
+    def lanes_of(value):
+        high, rest = two_parts(value)
+        return jnp.where(
+            lane_row == 0, high.astype(F32), jnp.where(lane_row == 1, rest.astype(F32), 0.0)
+        )
+
+    def expert(plane):
+        at = pl.ds(aligned(plane * R, 16), R)
         inner = dot(r.Nr[at, :], r.wi[...])
         square = inner * inner
         tanh = jnp.tanh(GELU_A * inner * (1.0 + GELU_B * square))
@@ -483,72 +537,24 @@
         inner_grad = (back * slope).astype(BF)
         r.act[at, :] = active
         r.ig[at, :] = inner_grad
-        r.SS[step, :, :D] = dot_rt(inner_grad, r.wi[...]).astype(BF)
-        high, rest = two_parts(jnp.sum(active.astype(F32) * back, axis=1, keepdims=True))
-        r.SS[step, :, D:] = jnp.where(
-            lane_row == 0, high.astype(F32), jnp.where(lane_row == 1, rest.astype(F32), 0.0)
+        r.SS[plane, :, :D] = dot_rt(inner_grad, r.wi[...]).astype(BF)
+        r.SS[plane, :, D:] = lanes_of(
+            jnp.sum(active.astype(F32) * back, axis=1, keepdims=True)
         ).astype(BF)
-        for o in range(1, W):
-
-            @pl.when(step == o)
-            def _():
-                remote(r.SS.at[o], r.Sr.at[o - 1], r.x_s3.at[o], r.s3.at[o], zpeer(o)).start()
-
-        return carry
-
-    lax.fori_loop(0, W, expert, 0)
-
-    sent(r.Gr.at[pl.ds(0, (W - 1) * R)], r.x_d2.at[0])
-    sent(r.Nr.at[pl.ds(0, (W - 1) * R)], r.x_d2.at[1])
-    for o in range(1, W):
-        got(r.Tr.at[pl.ds(0, R)], r.t2.at[o])
-
-    def scale_rows(step, carry):
-        at = pl.ds(aligned(step * R, 16), R)
-        gates = jnp.sum(r.Tr[at, :].astype(F32), axis=1, keepdims=True)
-        r.Gr[at, :] = (r.Gr[at, :].astype(F32) * gates).astype(BF)
-        r.ig[at, :] = (r.ig[at, :].astype(F32) * gates).astype(BF)
-        return carry
-
-    lax.fori_loop(0, W, scale_rows, 0)
-    tile, slots = s.tile, s.slots
-
-    def save_out(step):
-        slot = lax.rem(step, slots)
-        at = pl.ds(aligned(step * tile, LANES), tile)
-        return pltpu.make_async_copy(r.gwo.at[slot], r.grad_w_out.at[0, at], r.gwo_sem.at[slot])
-
-    def save_in(step):
-        slot = lax.rem(step, slots)
-        at = pl.ds(aligned(step * tile, LANES), tile)
-        return pltpu.make_async_copy(r.gwi.at[slot], r.grad_w_in.at[0, at], r.gwi_sem.at[slot])
-
-    def grad_out_tile(step, carry):
-        @pl.when(step >= slots)
-        def _():
-            save_out(step - slots).wait()
-
-        at = pl.ds(aligned(step * tile, LANES), tile)
-        r.gwo[lax.rem(step, slots)] = dot_lt(r.act[:, at], r.Gr[...])
-        save_out(step).start()
-        return carry
-
-    def grad_in_tile(step, carry):
-        @pl.when(step >= slots)
-        def _():
-            save_in(step - slots).wait()
-
-        at = pl.ds(aligned(step * tile, LANES), tile)
-        r.gwi[lax.rem(step, slots)] = dot_lt(r.Nr[:, at], r.ig[...])
-        save_in(step).start()
-        return carry
-
-    lax.fori_loop(0, s.F // tile, grad_out_tile, 0)
-    lax.fori_loop(0, D // tile, grad_in_tile, 0)
-
-    def plane_back(index, source, target):
+
+    def merge(plane, slot, block):
+        own, other = r.SS[plane, block, :].astype(F32), r.Sin[slot, block, :].astype(F32)
+        r.SS[plane, block, :D] = (own[:, :D] + other[:, :D]).astype(BF)
+        r.SS[plane, block, D:] = lanes_of(
+            jnp.sum(own[:, D:] + other[:, D:], axis=1, keepdims=True)
+        ).astype(BF)
+
+    def plane_back(index, source, target, offsets):
         mine = pl.ds(aligned(e * cp, plane_step), cp)
-        for o in range(1, E):
+        for o in offsets:
+            if o == 0:
+                target[mine, :] = source[mine, :]
+                continue
             x = flip(e, o)
             remote(
                 source.at[pl.ds(aligned(x * cp, plane_step), cp)],
@@ -557,43 +563,144 @@
                 r.back.at[index],
                 (x, z),
             ).start()
-        target[mine, :] = source[mine, :]
-
-    total = r.SS[0].astype(F32)
+
+    expert(z)
+    for step in range(1, 2 * W - 2):
+        if step < W:
+            line_pass(r.Nr, step, *n_line)
+
+            def sides(side, carry, step=step):
+                plane = z + (2 * side - 1) * step
+                pl.when((plane >= 0) & (plane < W))(functools.partial(expert, plane))
+                return carry
+
+            lax.fori_loop(0, 2, sides, 0)
+
+        plane_down = 2 * W - 2 - z - step
+        gap_down = z - plane_down
+        plane_up = step - z
+        gap_up = plane_up - z
+
+        @pl.when((plane_down >= 0) & (gap_down >= 1))
+        def _():
+            for oc in range(C):
+                block = block_at(0, oc)
+
+                @pl.when(z < W - 1)
+                def _():
+                    got(r.Sin.at[plane_down, block], r.sd.at[gap_down, oc])
+                    merge(plane_down, plane_down, block)
+
+                remote(
+                    r.SS.at[plane_down, block],
+                    r.Sin.at[plane_down, block],
+                    r.x_sd.at[gap_down],
+                    r.sd.at[gap_down - 1, oc],
+                    (e, z - 1),
+                ).start()
+
+        @pl.when((plane_up <= W - 1) & (gap_up >= 1))
+        def _():
+            for oc in range(C):
+                block = block_at(0, oc)
+
+                @pl.when(z > 0)
+                def _():
+                    got(r.Sin.at[plane_up + 1, block], r.su.at[gap_up, oc])
+                    merge(plane_up, plane_up + 1, block)
+
+                remote(
+                    r.SS.at[plane_up, block],
+                    r.Sin.at[plane_up + 1, block],
+                    r.x_su.at[gap_up],
+                    r.su.at[gap_up - 1, oc],
+                    (e, z + 1),
+                ).start()
+
+    for oc in range(C):
+        block = block_at(0, oc)
+
+        @pl.when(z < W - 1)
+        def _():
+            got(r.Sin.at[z, block], r.sd.at[0, oc])
+            merge(z, z, block)
+
+        @pl.when(z > 0)
+        def _():
+            got(r.Sin.at[z + 1, block], r.su.at[0, oc])
+            merge(z, z + 1, block)
+
+        r.Sb[block, :] = r.SS[z, block, :].astype(s.dt)
+        plane_back(0, r.Sb, r.Sk, (2 * oc, 2 * oc + 1))
+
+    line_sent(r.Gr, r.x_gu, r.x_gd)
     for o in range(1, W):
-        got(r.Sr.at[o - 1], r.s3.at[o])
-        total = total + r.Sr[o - 1].astype(F32)
-    high, rest = two_parts(jnp.sum(total[:, D:], axis=1, keepdims=True))
-    r.Sb[:, :D] = total[:, :D].astype(BF).astype(s.dt)
-    r.Sb[:, D:] = jnp.where(
-        lane_row == 0, high.astype(F32), jnp.where(lane_row == 1, rest.astype(F32), 0.0)
-    ).astype(s.dt)
+        got(r.Tr.at[pl.ds(0, R)], r.t2.at[o])
+
+    def scale_rows(step, carry):
+        at = pl.ds(aligned(step * R, 16), R)
+        gates = jnp.sum(r.Tr[at, :].astype(F32), axis=1, keepdims=True)
+        r.Gr[at, :] = (r.Gr[at, :].astype(F32) * gates).astype(BF)
+        r.ig[at, :] = (r.ig[at, :].astype(F32) * gates).astype(BF)
+        return carry
+
+    lax.fori_loop(0, W, scale_rows, 0)
+    tile, slots = s.tile, s.slots
+
+    def save_out(step):
+        slot = lax.rem(step, slots)
+        at = pl.ds(aligned(step * tile, LANES), tile)
+        return pltpu.make_async_copy(r.gwo.at[slot], r.grad_w_out.at[0, at], r.gwo_sem.at[slot])
+
+    def save_in(step):
+        slot = lax.rem(step, slots)
+        at = pl.ds(aligned(step * tile, LANES), tile)
+        return pltpu.make_async_copy(r.gwi.at[slot], r.grad_w_in.at[0, at], r.gwi_sem.at[slot])
+
+    def grad_out_tile(step, carry):
+        @pl.when(step >= slots)
+        def _():
+            save_out(step - slots).wait()
+
+        at = pl.ds(aligned(step * tile, LANES), tile)
+        r.gwo[lax.rem(step, slots)] = dot_lt(r.act[:, at], r.Gr[...])
+        save_out(step).start()
+        return carry
+
+    def grad_in_tile(step, carry):
+        @pl.when(step >= slots)
+        def _():
+            save_in(step - slots).wait()
+
+        at = pl.ds(aligned(step * tile, LANES), tile)
+        r.gwi[lax.rem(step, slots)] = dot_lt(r.Nr[:, at], r.ig[...])
+        save_in(step).start()
+        return carry
+
+    lax.fori_loop(0, s.F // tile, grad_out_tile, 0)
+    lax.fori_loop(0, D // tile, grad_in_tile, 0)
+
     for o in range(1, W):
         pl.semaphore_signal(r.credit, inc=1, device_id=zpeer(o), device_id_type=MESH)
-    plane_back(0, r.Sb, r.Sk)
-
-    for o in range(1, W):
-        sent(r.SS.at[o], r.x_s3.at[o])
+    for d in range(1, W):
+        pl.when(z >= d)(functools.partial(sent, r.SS.at[0], r.x_sd.at[d]))
+        pl.when(z + d <= W - 1)(functools.partial(sent, r.SS.at[0], r.x_su.at[d]))
     pl.semaphore_wait(r.credit, W - 1)
 
     def results(step, carry):
         at = pl.ds(aligned(step * R, 16), R)
         r.SS[step, :, :D] = dot(r.act[at, :], r.wo[...]).astype(BF)
-        for o in range(1, W):
-
-            @pl.when(step == o)
-            def _():
-                remote(
-                    r.SS.at[o, :, pl.ds(0, D)],
-                    r.Sr.at[o - 1, :, pl.ds(0, D)],
-                    r.x_r3.at[o],
-                    r.r3.at[o],
-                    zpeer(o),
-                ).start()
-
         return carry
 
     lax.fori_loop(0, W, results, 0)
+    for o in range(1, W):
+        remote(
+            r.SS.at[flip(z, o), :, pl.ds(0, D)],
+            r.Sin.at[z, :, pl.ds(0, D)],
+            r.x_r3.at[o],
+            r.r3.at[o],
+            zpeer(o),
+        ).start()
 
     got(r.Sk.at[pl.ds(0, (E - 1) * cp)], r.back.at[0])
     returned = dot(r.pt[...], r.Sk[...].astype(BF))
@@ -764,12 +871,12 @@
         remote(r.hGS.at[flip(c, oc)], r.hGR.at[oc - 1], r.x_ra.at[4], r.ra.at[4], cpeer(oc)).start()
     spread(3)
 
-    total = r.SS[0, :, :D].astype(F32)
+    total = r.SS[z, :, :D].astype(F32)
     for o in range(1, W):
-        got(r.Sr.at[o - 1, :, pl.ds(0, D)], r.r3.at[o])
-        total = total + r.Sr[o - 1, :, :D].astype(F32)
+        got(r.Sin.at[flip(z, o), :, pl.ds(0, D)], r.r3.at[o])
+        total = total + r.Sin[flip(z, o), :, :D].astype(F32)
     r.Rb[...] = total.astype(BF).astype(s.dt)
-    plane_back(1, r.Rb, r.Rk)
+    plane_back(1, r.Rb, r.Rk, range(E))
 
     got(r.hGR, r.ra.at[4])
     total = r.hGS[c].astype(F32)
@@ -831,9 +938,10 @@
         sent(r.FG.at[m, :, here], r.x_rd.at[m])
     for index, buffer in enumerate((r.gsend, r.nsend, r.tsend)):
         sent(buffer.at[pl.ds(0, E - 1)], r.x_d1.at[index])
-    sent(r.Tr.at[pl.ds(0, (W - 1) * R)], r.x_d2.at[2])
+    line_sent(r.Nr, r.x_nu, r.x_nd)
+    sent(r.Tr.at[pl.ds(0, (W - 1) * R)], r.x_t2)
     for o in range(1, W):
-        sent(r.SS.at[o, :, pl.ds(0, D)], r.x_r3.at[o])
+        sent(r.SS.at[0, :, pl.ds(0, D)], r.x_r3.at[o])
     sent(r.Sk.at[pl.ds(0, (E - 1) * cp)], r.x_back.at[0])
     sent(r.Rk.at[pl.ds(0, (E - 1) * cp)], r.x_back.at[1])
     sent(r.nT.at[:, pl.ds(0, T)], r.x_sibT.at[0])

time: 232 us -> 196 us (0.84)
  Pallas kernels: 210 us -> 174 us
    pallas_call x1, Pallas kernels: 210 us -> 174 us  [local(): pl.pallas_call(functools.partial(kernel, s, names), name='layer', out_sha...]
where the time goes in v3:
time: 196 us; the launch traced here: 195 us
  Pallas kernels  174 us (89%)
  local copies, waits for them, and re-layouts  15.5 us (8%)
  other arithmetic  4.93 us (3%)
    pallas_call x1, Pallas kernels, local(): pl.pallas_call(functools.partial(kernel, s, names), name='layer', out_sha...  174 us
    unnamed x17, local copies, waits for them, and re-layouts  10.3 us

profile of v3, /device:TPU:0, one launch (start us, length us, event | category | flops | bytes accessed | tf_op | source)
XLA Modules:
  0.0 195.4 jit_solution(15739901676334706449)
XLA Ops:
  0.6 0.8 reverse
  1.4 0.1 slice.38
  1.5 0.7 pad_add_fusion
  2.2 0.6 pad.9.refs_5_
  2.8 0.7 broadcast_in_dim.12
  3.5 0.7 broadcast_in_dim.13
  4.3 0.8 copy.32
  5.1 1.4 fusion.1.refs_2_
  6.5 1.5 copy.35.refs_3_
  8.0 174.2 %layer.1 = (bf16[256,768]{1,0:T(8,128)(2,1)}, f32[256,768]{1,0:T(8,128)}, bf16[4,192,768]{2,1,0:T(8,128)(2,1)}, f32[192,128]{1,0:T(8,128)}, f32[1,768,768]{2,1,0:T(8,128)}, /*index=5*/f32[1,768,768]{2,1,0:T(8,128)}) custom-call(s32[64]{0:T(128)} %refs_0_.1, s32[64]{0:T(128)} %refs_1_.1, bf16[208,128]{1,0:T(8,128)(2,1)} %fusion.1.refs_2_, ...), custom_call_target="tpu_custom_call" | custom-call | tf_op jit(solution)/shard_map/layer/pallas_call | solution.py:1019
  182.2 0.0 copy-start.3
  182.2 0.0 copy-start.2
  182.3 1.8 slice_reduce_fusion
  184.1 1.3 slice.29
  185.4 1.6 copy.36
  187.0 0.0 copy-start.1
  187.0 2.8 %bitcast_convert_fusion = (f32[192,768]{1,0:T(8,128)}, f32[192,768]{1,0:T(8,128)}, f32[192,768]{1,0:T(8,128)}, f32[192,768]{1,0:T(8,128)}) fusion(bf16[4,192,768]{2,1,0:T(8,128)(2,1)} %get-tuple-element.21), kind=kLoop, calls=%fused_computation | loop fusion | flops 589824 | bytes 3538944 | tf_op jit(solution)/shard_map/convert_element_type | solution.py:1046
  189.8 0.0 copy-done.3
  189.8 0.7 copy.41
  190.6 0.0 copy-done.2
  190.6 0.9 copy.42
  191.4 0.0 copy-done.1
  191.4 0.0 copy-start
  191.4 1.4 copy.43
  192.9 1.1 copy-done
  194.0 1.4 copy.44
  (1 shorter events, 0.0 us)
Async XLA Ops:
  182.2 7.6 %copy-start.3 = (bf16[256,768]{1,0:T(8,128)(2,1)S(1)}, bf16[256,768]{1,0:T(8,128)(2,1)}, u32[]{:S(2)}) copy-start(bf16[256,768]{1,0:T(8,128)(2,1)} %get-tuple-element.66) | copy-start | bytes 1179652
  182.2 8.3 %copy-start.2 = (f32[256,768]{1,0:T(8,128)S(1)}, f32[256,768]{1,0:T(8,128)}, u32[]{:S(2)}) copy-start(f32[256,768]{1,0:T(8,128)} %get-tuple-element.67) | copy-start | bytes 2359300
  187.0 4.5 %copy-start.1 = (f32[1,768,768]{2,1,0:T(8,128)S(1)}, f32[1,768,768]{2,1,0:T(8,128)}, u32[]{:S(2)}) copy-start(f32[1,768,768]{2,1,0:T(8,128)} %get-tuple-element.76) | copy-start | bytes 7077892
  191.4 2.5 %copy-start = (f32[1,768,768]{2,1,0:T(8,128)S(1)}, f32[1,768,768]{2,1,0:T(8,128)}, u32[]{:S(2)}) copy-start(f32[1,768,768]{2,1,0:T(8,128)} %get-tuple-element.77) | copy-start | bytes 7077892

commit v4 on v3

--- a/solution.py
+++ b/solution.py
@@ -79,6 +79,8 @@
     s.NBH = buckets_here
     s.NBP = up16(buckets_here)
     s.half = width // 2
+    s.P1 = up16(n_experts + 2)
+    s.LW = -(-s.SR // LANES) * LANES
     team = s.C
     while s.SR % team or (s.SR // team) % 16:
         team //= 2
@@ -106,7 +108,9 @@
     dma = pltpu.SemaphoreType.DMA
     return [
         ("wfull", V((4, s.D, s.D), BF)),
-        ("smg", V((s.W, s.SR + s.NBP, LANES), BF)),
+        ("smf", V((s.P1 + s.NBP, s.LW), F32)),
+        ("smg", V((s.W, s.P1 + s.NBP, s.LW), BF)),
+        ("tab", V((8, 2 * s.T), I32)),
         ("xb", V((s.T, s.D), BF)),
         ("og", V((s.T, s.D), BF)),
         ("wi", V((s.D, s.F), BF)),
@@ -129,10 +133,9 @@
         ("Rb", V((s.R, s.D), s.dt)),
         ("Rk", V((s.S, s.D), s.dt)),
         ("tb", V((LANES, 2 * s.T), F32)),
-        ("oh", V((s.W * s.NBP, 2 * s.T), BF)),
         ("ohm", V((s.W * s.NBP, 2 * s.T), BF)),
         ("rows", V((8, s.D), F32)),
-        ("Rw", V((s.D, LANES), BF)),
+        ("RwT", V((LANES, s.D), BF)),
         ("probs", V((s.H, s.T, s.T), F32)),
         ("q", V((s.T, s.D), BF)),
         ("kk", V((s.T, s.D), BF)),
@@ -160,15 +163,16 @@
         ("hZR", V((s.W - 1, s.pr, LANES), BF)),
         ("hFG", V((s.CP, LANES), BF)),
         ("bt", V((LANES, 2 * s.T), F32)),
-        ("gwi", V((s.slots, s.tile, s.F), F32)),
-        ("gwo", V((s.slots, s.tile, s.D), F32)),
+        ("gwi", V((s.slots, s.tile, s.F), BF)),
+        ("gwo", V((s.slots, s.tile, s.D), BF)),
         ("gwi_sem", dma((s.slots,))),
         ("gwo_sem", dma((s.slots,))),
         ("lsem", dma((9,))),
         ("smr", dma((s.W,))),
-        ("wa", dma((4, s.W))),
-        ("wb", dma((4,))),
-        ("wc", dma((4,))),
+        ("wu", dma((2, s.W))),
+        ("wd", dma((2, s.W))),
+        ("wb", dma((2,))),
+        ("wc", dma((2,))),
         ("g1", dma((s.C,))),
         ("gu", dma((s.W, s.C))),
         ("gd", dma((s.W, s.C))),
@@ -179,7 +183,8 @@
         ("t2", dma((s.W,))),
         ("su", dma((s.W, s.C))),
         ("sd", dma((s.W, s.C))),
-        ("r3", dma((s.W,))),
+        ("ru", dma((s.W,))),
+        ("rdn", dma((s.W,))),
         ("back", dma((2,))),
         ("sibT", dma((2,))),
         ("sibF", dma((4,))),
@@ -188,9 +193,10 @@
         ("rc", dma((5,))),
         ("rd", dma((5,))),
         ("x_sm", dma),
-        ("x_wa", dma((4,))),
-        ("x_wb", dma((4,))),
-        ("x_wc", dma((4,))),
+        ("x_wu", dma((2, s.W))),
+        ("x_wd", dma((2, s.W))),
+        ("x_wb", dma((2,))),
+        ("x_wc", dma((2,))),
         ("x_d1", dma((3,))),
         ("x_t2", dma),
         ("x_gu", dma((s.W,))),
@@ -199,7 +205,8 @@
         ("x_nd", dma((s.W,))),
         ("x_su", dma((s.W,))),
         ("x_sd", dma((s.W,))),
-        ("x_r3", dma((s.W,))),
+        ("x_ru", dma((s.W,))),
+        ("x_rdn", dma((s.W,))),
         ("x_back", dma((2,))),
         ("x_sibT", dma((2,))),
         ("x_sibF", dma((4,))),
@@ -217,7 +224,7 @@
 
 
 IN_NAMES = (
-    "lengths", "seq", "small", "ids", "prio", "table",
+    "lengths", "seq", "ids", "prio", "table", "router", "gain_attn", "gain_ffn", "bias",
     "tokens", "out_grad", "w0", "w1", "w2", "w3", "w_in", "w_out",
 )
 PAD_NAMES = ("unsel",)
@@ -265,6 +272,13 @@
     for copy in (*load_w, load_og, load_x, load_wo, load_wi):
         copy.start()
 
+    r.smf[...] = jnp.zeros_like(r.smf)
+    r.smf[0 : s.NX, 0 : s.SR] = r.router[...].astype(F32)
+    r.smf[s.NX : s.NX + 1, 0 : s.SR] = r.gain_attn[...].astype(F32).reshape(1, s.SR)
+    r.smf[s.NX + 1 : s.NX + 2, 0 : s.SR] = r.gain_ffn[...].astype(F32).reshape(1, s.SR)
+    r.smf[s.P1 : s.P1 + s.NBH, 0 : s.H] = r.bias[...].astype(F32)
+    r.smg[z] = r.smf[...].astype(BF)
+
     barrier = pltpu.get_barrier_semaphore()
     peers = [(flip(e, o), z) for o in range(1, E)] + [zpeer(o) for o in range(1, W)]
     for peer in peers:
@@ -272,21 +286,25 @@
     pl.semaphore_wait(barrier, len(peers))
 
     team_c = lax.rem(c, s.team)
-    r.smg[z] = r.small[...]
     for o in range(1, W):
-        remote(r.small, r.smg.at[z], r.x_sm, r.smr.at[o], zpeer(o)).start()
-    piece = pl.ds(aligned(z * s.SR + team_c * s.pw, 16), s.pw)
+        remote(r.smg.at[z], r.smg.at[z], r.x_sm, r.smr.at[o], zpeer(o)).start()
     share_rows = pl.ds(aligned(team_c * s.pw, 16), s.pw)
-    for m in range(4):
-        for o in range(1, W):
-            remote(
-                shards[m].at[share_rows, here],
-                r.wfull.at[m, piece, here],
-                r.x_wa.at[m],
-                r.wa.at[m, o],
-                zpeer(o),
-            ).start()
-
+    groups = (pl.ds(0, 3), pl.ds(3, 1))
+    members = ((0, 1, 2), (3,))
+
+    def weight_at(plane):
+        return pl.ds(aligned(plane * s.SR + team_c * s.pw, 16), s.pw)
+
+    def weight_own(g):
+        def send(sender, receiver, to):
+            for m in members[g]:
+                source = shards[m].at[share_rows, here]
+                remote(source, r.wfull.at[m, weight_at(z), here], sender, receiver, (e, to)).start()
+
+        pl.when(z < W - 1)(functools.partial(send, r.x_wu.at[g, 0], r.wu.at[g, 1], z + 1))
+        pl.when(z > 0)(functools.partial(send, r.x_wd.at[g, 0], r.wd.at[g, 1], z - 1))
+
+    weight_own(0)
     device = e * W + z
     first = r.lengths[r.seq[2 * device]]
     both = first + r.lengths[r.seq[2 * device + 1]]
@@ -297,8 +315,8 @@
     same = seg_col == seg_row
     valid = (col < both).astype(F32)
     eye = iota((T, T), 0) == iota((T, T), 1)
-    id_col = r.ids[...].astype(F32)
-    id_row = jnp.sum(jnp.where(eye, id_col, 0.0), axis=0, keepdims=True)
+    id_row = r.ids[...].astype(F32)
+    id_col = jnp.sum(jnp.where(eye, id_row, 0.0), axis=1, keepdims=True)
     prio_row = r.prio[...].astype(F32)
     prio_col = jnp.sum(jnp.where(eye, prio_row, 0.0), axis=1, keepdims=True)
     ahead = (id_col == id_row) & (prio_col < prio_row)
@@ -375,41 +393,70 @@
     load_og.wait()
     dispatch(0, r.gsend, Ga, r.g1, r.og[...])
 
-    def pass_on(m):
-        for o in range(1, W):
-            begin = flip(z, o) * s.SR + team_c * s.pw
-            part = r.wfull.at[m, pl.ds(aligned(begin, 16), s.pw), here]
-            got(part, r.wa.at[m, o])
+    def weight_pass(g, d):
+        def handle(plane, arrived, onward, sender, receiver, to):
+            part = r.wfull.at[groups[g], weight_at(plane), here]
+            got(part, arrived)
+            if d < W - 1:
+                pl.when(onward)(functools.partial(move, part, sender, receiver, to))
             for oc in range(1, s.team):
-                remote(part, part, r.x_wb.at[m], r.wb.at[m], cpeer(oc)).start()
-
-    def to_sibling(m):
+                remote(part, part, r.x_wb.at[g], r.wb.at[g], cpeer(oc)).start()
+
+        after = min(d + 1, W - 1)
+        pl.when(z >= d)(
+            functools.partial(
+                handle, z - d, r.wu.at[g, d], z < W - 1, r.x_wu.at[g, d], r.wu.at[g, after], z + 1
+            )
+        )
+        pl.when(z + d <= W - 1)(
+            functools.partial(
+                handle, z + d, r.wd.at[g, d], z > 0, r.x_wd.at[g, d], r.wd.at[g, after], z - 1
+            )
+        )
+
+    team_rows = pl.ds(0, (W - 1) * (s.team - 1) * s.pw)
+
+    def to_sibling(g):
         if s.team > 1:
-            got(r.wfull.at[m, pl.ds(0, (W - 1) * (s.team - 1) * s.pw), here], r.wb.at[m])
-        load_w[m].wait()
-        part = r.wfull.at[m, :, here]
-        remote(part, part, r.x_wc.at[m], r.wc.at[m], sib).start()
-
-    def weight_ready(m):
-        got(r.wfull.at[m, :, there], r.wc.at[m])
-
+            got(r.wfull.at[groups[g], team_rows, here], r.wb.at[g])
+        for m in members[g]:
+            load_w[m].wait()
+        part = r.wfull.at[groups[g], :, here]
+        remote(part, part, r.x_wc.at[g], r.wc.at[g], sib).start()
+
+    def weight_ready(g):
+        got(r.wfull.at[groups[g], :, there], r.wc.at[g])
+
+    for d in range(1, W):
+        weight_pass(0, d)
+        if d == 1:
+            weight_own(1)
+        else:
+            weight_pass(1, d - 1)
+        if d == min(2, W - 1):
+            line_own(r.Gr, Ga, r.g1, *g_line)
+    weight_pass(1, W - 1)
     for o in range(1, W):
-        got(r.small, r.smr.at[o])
-    pass_on(0)
-    router_rows = r.smg[:, : s.SR, :].reshape(D, LANES)
-    turned = router_rows.astype(F32).T
-    r.rows[0:1, :] = turned[GAIN_ATTN_LANE : GAIN_ATTN_LANE + 1, :]
-    r.rows[1:2, :] = turned[GAIN_FFN_LANE : GAIN_FFN_LANE + 1, :]
+        got(r.smg.at[0], r.smr.at[o])
+    gathered = jnp.concatenate(
+        [r.smg[w, : s.P1, : s.SR].astype(F32) for w in range(W)], axis=1
+    )
+    r.rows[0:1, :] = gathered[s.NX : s.NX + 1]
+    r.rows[1:2, :] = gathered[s.NX + 1 : s.NX + 2]
+    r.RwT[...] = jnp.zeros_like(r.RwT)
+    r.RwT[: s.P1, :] = jnp.where(iota((s.P1, D), 0) < s.NX, gathered, 0.0).astype(BF)
     lane_row = iota((1, LANES), 1)
-    r.Rw[...] = router_rows * (lane_row < s.NX).astype(F32).astype(BF)
-    bucket = r.table[...]
+    r.tab[...] = jnp.full(r.tab.shape, -1, I32)
+    r.tab[0:1, 0 : 2 * T - 1] = r.table[...]
+    bucket = r.tab[0:1, :]
     shift = s.NBH.bit_length() - 1
     bucket = lax.shift_right_logical(bucket, shift) * s.NBP + lax.bitwise_and(bucket, s.NBH - 1)
-    bucket_at = iota((W * s.NBP, 2 * T), 0)
-    r.oh[...] = (bucket_at == bucket[0:1]).astype(F32).astype(BF)
-    r.ohm[...] = (bucket_at == bucket[1:2]).astype(F32).astype(BF)
-    bias_rows = r.smg[:, s.SR :, :].reshape(W * s.NBP, LANES)
-    r.tb[...] = dot_lt(bias_rows, r.oh[...])
+    bucket = jnp.where(r.tab[0:1, :] < 0, -1, bucket)
+    hot = (iota((W * s.NBP, 2 * T), 0) == bucket).astype(F32).astype(BF)
+    backwards = (iota((2 * T, 2 * T), 0) + iota((2 * T, 2 * T), 1) == 2 * T - 2).astype(F32)
+    r.ohm[...] = dot(hot, backwards.astype(BF)).astype(BF)
+    bias_rows = r.smg[:, s.P1 :, :LANES].reshape(W * s.NBP, LANES)
+    r.tb[...] = dot_lt(bias_rows, hot)
 
     def bias_head(h, carry):
         wide = jnp.broadcast_to(r.tb[pl.ds(h, 1), :], (T, 2 * T))
@@ -417,18 +464,8 @@
         r.probs[h] = jnp.where(same, turned[:, :T], NEG_FILL)
         return carry
 
-    third = s.H // 3
-    pass_on(1)
-    lax.fori_loop(0, third, bias_head, 0)
-    pass_on(2)
+    lax.fori_loop(0, s.H, bias_head, 0)
     to_sibling(0)
-    lax.fori_loop(third, 2 * third, bias_head, 0)
-    to_sibling(1)
-    line_own(r.Gr, Ga, r.g1, *g_line)
-    pass_on(3)
-    lax.fori_loop(2 * third, s.H, bias_head, 0)
-    to_sibling(2)
-
     load_x.wait()
     x = r.xb[...].astype(F32)
     scale1 = lax.rsqrt(jnp.mean(x * x, axis=1, keepdims=True) + EPSILON)
@@ -449,11 +486,9 @@
     turn_out(0, normed, r.nT)
     weight_ready(0)
     r.q[...] = dot(normed, r.wfull[0]).astype(BF)
-    weight_ready(1)
     r.kk[...] = dot(normed, r.wfull[1]).astype(BF)
-    to_sibling(3)
-    weight_ready(2)
     r.v[...] = dot(normed, r.wfull[2]).astype(BF)
+    to_sibling(1)
     line_pass(r.Gr, 1, *g_line)
 
     scale = s.HD ** (-0.5)
@@ -476,16 +511,14 @@
 
     lax.fori_loop(0, s.H // 2, attend, 0)
     mixed = r.mixed[...]
-    if W > 2:
-        line_pass(r.Gr, 2, *g_line)
-    weight_ready(3)
+    weight_ready(1)
     middle = r.xb[...].astype(F32) + dot(mixed, r.wfull[3]) * valid
     r.middle[...] = middle
     scale2 = lax.rsqrt(jnp.mean(middle * middle, axis=1, keepdims=True) + EPSILON)
     nf = (middle * scale2 * r.rows[1:2, :]).astype(BF)
     r.nf[...] = nf
     dispatch(1, r.nsend, Na, r.n1, nf)
-    logits = jnp.where(lane_row < s.NX, dot(nf, r.Rw[...]), NEG_FILL)
+    logits = jnp.where(lane_row < s.NX, dot_rt(nf, r.RwT[...]), NEG_FILL)
     raised = jnp.exp(logits - jnp.max(logits, axis=1, keepdims=True))
     router = raised / jnp.sum(raised, axis=1, keepdims=True)
     picked = (lane_row.astype(F32) == id_col).astype(F32)
@@ -498,6 +531,8 @@
         jnp.where(lane_row == 1, gate_mid.astype(F32), jnp.where(lane_row == 2, gate_low.astype(F32), 0.0)),
     )
     dispatch(2, r.tsend, Ta, r.t1, gate_lanes.astype(BF))
+    if W > 2:
+        line_pass(r.Gr, 2, *g_line)
     line_own(r.Nr, Na, r.n1, *n_line)
     for oc in range(C):
         landed(r.Tr, Ta, r.t1, oc)
@@ -650,12 +685,12 @@
     def save_out(step):
         slot = lax.rem(step, slots)
         at = pl.ds(aligned(step * tile, LANES), tile)
-        return pltpu.make_async_copy(r.gwo.at[slot], r.grad_w_out.at[0, at], r.gwo_sem.at[slot])
+        return pltpu.make_async_copy(r.gwo.at[slot], r.grad_w_out.at[at], r.gwo_sem.at[slot])
 
     def save_in(step):
         slot = lax.rem(step, slots)
         at = pl.ds(aligned(step * tile, LANES), tile)
-        return pltpu.make_async_copy(r.gwi.at[slot], r.grad_w_in.at[0, at], r.gwi_sem.at[slot])
+        return pltpu.make_async_copy(r.gwi.at[slot], r.grad_w_in.at[at], r.gwi_sem.at[slot])
 
     def grad_out_tile(step, carry):
         @pl.when(step >= slots)
@@ -663,7 +698,7 @@
             save_out(step - slots).wait()
 
         at = pl.ds(aligned(step * tile, LANES), tile)
-        r.gwo[lax.rem(step, slots)] = dot_lt(r.act[:, at], r.Gr[...])
+        r.gwo[lax.rem(step, slots)] = dot_lt(r.act[:, at], r.Gr[...]).astype(BF)
         save_out(step).start()
         return carry
 
@@ -673,7 +708,7 @@
             save_in(step - slots).wait()
 
         at = pl.ds(aligned(step * tile, LANES), tile)
-        r.gwi[lax.rem(step, slots)] = dot_lt(r.Nr[:, at], r.ig[...])
+        r.gwi[lax.rem(step, slots)] = dot_lt(r.Nr[:, at], r.ig[...]).astype(BF)
         save_in(step).start()
         return carry
 
@@ -693,20 +728,65 @@
         return carry
 
     lax.fori_loop(0, W, results, 0)
-    for o in range(1, W):
+    body = pl.ds(0, D)
+
+    def result_down(plane):
         remote(
-            r.SS.at[flip(z, o), :, pl.ds(0, D)],
-            r.Sin.at[z, :, pl.ds(0, D)],
-            r.x_r3.at[o],
-            r.r3.at[o],
-            zpeer(o),
+            r.SS.at[plane, :, body],
+            r.Sin.at[plane, :, body],
+            r.x_rdn.at[z - plane],
+            r.rdn.at[z - plane - 1],
+            (e, z - 1),
         ).start()
 
+    def result_up(plane):
+        remote(
+            r.SS.at[plane, :, body],
+            r.Sin.at[plane + 1, :, body],
+            r.x_ru.at[plane - z],
+            r.ru.at[plane - z - 1],
+            (e, z + 1),
+        ).start()
+
+    def result_merge(plane, slot, sem):
+        got(r.Sin.at[slot, :, body], sem)
+        r.SS[plane, :, :D] = (
+            r.SS[plane, :, :D].astype(F32) + r.Sin[slot, :, :D].astype(F32)
+        ).astype(BF)
+
+    def results_pass(step):
+        if step == 0:
+
+            @pl.when(z == W - 1)
+            def _():
+                for plane in range(W - 1):
+                    result_down(plane)
+
+            @pl.when(z == 0)
+            def _():
+                for plane in range(W - 1, 0, -1):
+                    result_up(plane)
+
+            return
+        below = step - (W - 1 - z)
+        above = W - 1 - step + z
+
+        @pl.when((z < W - 1) & (below >= 0) & (below < z))
+        def _():
+            result_merge(below, below, r.rdn.at[z - below])
+            result_down(below)
+
+        @pl.when((z > 0) & (above <= W - 1) & (above > z))
+        def _():
+            result_merge(above, above + 1, r.ru.at[above - z])
+            result_up(above)
+
+    results_pass(0)
     got(r.Sk.at[pl.ds(0, (E - 1) * cp)], r.back.at[0])
     returned = dot(r.pt[...], r.Sk[...].astype(BF))
     gate_grad = jnp.sum(returned[:, D:], axis=1, keepdims=True)
     logit_grad = (gate * gate_grad * (picked - router)).astype(BF)
-    nf_grad = dot_rt(logit_grad, r.Rw[...]) + gate * returned[:, :D]
+    nf_grad = dot(logit_grad, r.RwT[...]) + gate * returned[:, :D]
     middle = r.middle[...]
     along = nf_grad * r.rows[1:2, :]
     middle_grad = (
@@ -778,8 +858,8 @@
     share(2, r.dv)
     got(r.nT.at[:, pl.ds(T, T)], r.sibT.at[0])
     plane_sum(0, r.nT, r.dq)
-    plane_sum(1, r.nT, r.dk)
-    plane_sum(2, r.nT, r.dv)
+    for step in range(1, W - 2):
+        results_pass(step)
 
     def shard_sum(m):
         got(r.GR.at[m], r.ra.at[m])
@@ -817,8 +897,6 @@
         part = r.FG.at[m, :, here]
         remote(part, part, r.x_rd.at[m], r.rd.at[m], sib).start()
 
-    shard_sum(3)
-
     normed_grad = (
         dot_rt(r.dq[...], r.wfull[0]) + dot_rt(r.dk[...], r.wfull[1]) + dot_rt(r.dv[...], r.wfull[2])
     )
@@ -830,6 +908,8 @@
         - x * (scale1 * scale1 * scale1 * jnp.mean(along * x, axis=1, keepdims=True))
     )
     r.rows[3:4, :] = jnp.sum(normed_grad * x * scale1, axis=0, keepdims=True)
+    shard_sum(3)
+    plane_sum(1, r.nT, r.dk)
 
     r.bt[...] = jnp.zeros_like(r.bt)
     mirror = (iota((T, T), 0) + iota((T, T), 1) == T - 1).astype(F32).astype(BF)
@@ -842,6 +922,8 @@
         return carry
 
     lax.fori_loop(0, s.H, bias_back, 0)
+    shard_sum(0)
+    plane_sum(2, r.nT, r.dv)
     high, rest = two_parts(r.bt[...])
     rel_grad = dot_rt(r.ohm[...], high) + dot_rt(r.ohm[...], rest)
     lane_col = iota((LANES, 1), 0)
@@ -858,9 +940,11 @@
     small = jnp.concatenate(blocks, axis=0).astype(BF)
     r.smo[...] = spread_rows(small)
     remote(r.smo, r.sms, r.x_rd.at[4], r.rd.at[4], sib).start()
-    shard_sum(0)
+    if W > 2:
+        results_pass(W - 2)
+    spread(3)
     shard_sum(1)
-    shard_sum(2)
+    spread(0)
     got(r.sms, r.rd.at[4])
     pair = (r.smo[...].astype(F32) + r.sms[...].astype(F32)).astype(BF)
     for block in range(W):
@@ -869,13 +953,13 @@
             r.hGS[chip, block * s.pr : (block + 1) * s.pr, :] = pair[at : at + s.pr]
     for oc in range(1, C):
         remote(r.hGS.at[flip(c, oc)], r.hGR.at[oc - 1], r.x_ra.at[4], r.ra.at[4], cpeer(oc)).start()
-    spread(3)
-
-    total = r.SS[z, :, :D].astype(F32)
-    for o in range(1, W):
-        got(r.Sin.at[flip(z, o), :, pl.ds(0, D)], r.r3.at[o])
-        total = total + r.Sin[flip(z, o), :, :D].astype(F32)
-    r.Rb[...] = total.astype(BF).astype(s.dt)
+    shard_sum(2)
+    share_sum(3)
+    spread(1)
+    share_sum(0)
+    pl.when(z < W - 1)(functools.partial(result_merge, z, z, r.rdn.at[0]))
+    pl.when(z > 0)(functools.partial(result_merge, z, z + 1, r.ru.at[0]))
+    r.Rb[...] = r.SS[z, :, :D].astype(s.dt)
     plane_back(1, r.Rb, r.Rk, range(E))
 
     got(r.hGR, r.ra.at[4])
@@ -891,10 +975,8 @@
             r.rb.at[4],
             zpeer(o),
         ).start()
-    spread(0)
-    spread(1)
+    share_sum(1)
     spread(2)
-    share_sum(3)
     got(r.hZR, r.rb.at[4])
     total = r.hZS[pl.ds(aligned(z * s.pr, 16), s.pr), :].astype(F32)
     for o in range(1, W):
@@ -908,8 +990,6 @@
     got(r.Rk.at[pl.ds(0, (E - 1) * cp)], r.back.at[1])
     r.layer_out[...] = (r.middle[...] + gate * dot(r.pt[...], r.Rk[...].astype(BF))).astype(BF)
 
-    share_sum(0)
-    share_sum(1)
     share_sum(2)
     got(r.hFG.at[pl.ds(0, (C - 1) * s.pr)], r.rc.at[4])
 
@@ -926,11 +1006,15 @@
     for step in range(max(0, D // tile - slots), D // tile):
         save_in(step).wait()
     sent(r.smg.at[pl.ds(0, W - 1)], r.x_sm)
+    for g in range(2):
+        part = r.wfull.at[groups[g], pl.ds(0, s.pw), here]
+        for d in range(W - 1):
+            pl.when((z >= d) & (z < W - 1))(functools.partial(sent, part, r.x_wu.at[g, d]))
+            pl.when((z + d <= W - 1) & (z > 0))(functools.partial(sent, part, r.x_wd.at[g, d]))
+        if s.team > 1:
+            sent(r.wfull.at[groups[g], team_rows, here], r.x_wb.at[g])
+        sent(r.wfull.at[groups[g], :, here], r.x_wc.at[g])
     for m in range(4):
-        sent(r.wfull.at[m, pl.ds(0, (W - 1) * s.pw), here], r.x_wa.at[m])
-        if s.team > 1:
-            sent(r.wfull.at[m, pl.ds(0, (W - 1) * (s.team - 1) * s.pw), here], r.x_wb.at[m])
-        sent(r.wfull.at[m, :, here], r.x_wc.at[m])
         sent(r.fac.at[m], r.x_sibF.at[m])
         sent(r.GR.at[m], r.x_ra.at[m])
         sent(r.ZR.at[m], r.x_rb.at[m])
@@ -940,8 +1024,9 @@
         sent(buffer.at[pl.ds(0, E - 1)], r.x_d1.at[index])
     line_sent(r.Nr, r.x_nu, r.x_nd)
     sent(r.Tr.at[pl.ds(0, (W - 1) * R)], r.x_t2)
-    for o in range(1, W):
-        sent(r.SS.at[0, :, pl.ds(0, D)], r.x_r3.at[o])
+    for d in range(1, W):
+        pl.when(z >= d)(functools.partial(sent, r.SS.at[0, :, body], r.x_rdn.at[d]))
+        pl.when(z + d <= W - 1)(functools.partial(sent, r.SS.at[0, :, body], r.x_ru.at[d]))
     sent(r.Sk.at[pl.ds(0, (E - 1) * cp)], r.x_back.at[0])
     sent(r.Rk.at[pl.ds(0, (E - 1) * cp)], r.x_back.at[1])
     sent(r.nT.at[:, pl.ds(0, T)], r.x_sibT.at[0])
@@ -959,6 +1044,61 @@
         for at in range(share):
             unsel[chip * share + at, chip * s.pr + at] = 1
     return jnp.asarray(unsel, BF)
+
+
+PARTS = 3
+
+
+def finish(s, *refs):
+    layer_out, tokens_grad, grads, smalls, grad_in, grad_out = refs[:6]
+    out_layer, out_tokens, *out_mixers = refs[6:12]
+    out_in, out_out, out_gain1, out_gain2, out_rel, out_router = refs[12:18]
+    low_mix, low_in, low_out, mix, into, outof, held_layer, held_tokens = refs[18:26]
+    pass_sem, load_sem, save_sem, load2, save2 = refs[26:]
+    through = (
+        (layer_out, held_layer, out_layer),
+        (tokens_grad, held_tokens, out_tokens),
+    )
+    loads = [
+        pltpu.make_async_copy(source, held, pass_sem.at[0, index])
+        for index, (source, held, _) in enumerate(through)
+    ]
+    saves = [
+        pltpu.make_async_copy(held, target, pass_sem.at[1, index])
+        for index, (_, held, target) in enumerate(through)
+    ]
+    for m in range(4):
+        loads.append(pltpu.make_async_copy(grads.at[m], low_mix.at[m], load_sem.at[m]))
+        saves.append(pltpu.make_async_copy(mix.at[m], out_mixers[m], save_sem.at[m]))
+    steps = [None, None] + [(low_mix, mix, m) for m in range(4)]
+    for index, (source, low, high, target) in enumerate(
+        ((grad_in, low_in, into, out_in), (grad_out, low_out, outof, out_out))
+    ):
+        rows = source.shape[0] // PARTS
+        for part in range(PARTS):
+            at = pl.ds(part * rows, rows)
+            loads.append(
+                pltpu.make_async_copy(source.at[at], low.at[at], load2.at[index, part])
+            )
+            saves.append(
+                pltpu.make_async_copy(high.at[at], target.at[0, at], save2.at[index, part])
+            )
+            steps.append((low, high, at))
+    for copy in loads:
+        copy.start()
+    turned = smalls[...].T
+    out_router[...] = turned[: s.NX]
+    out_gain1[...] = turned[GAIN_ATTN_LANE : GAIN_ATTN_LANE + 1]
+    out_gain2[...] = turned[GAIN_FFN_LANE : GAIN_FFN_LANE + 1]
+    out_rel[...] = smalls[: s.NBH, REL_LANE : REL_LANE + s.H]
+    for load, save, step in zip(loads, saves, steps, strict=True):
+        load.wait()
+        if step is not None:
+            low, high, at = step
+            high[at] = low[at].astype(F32)
+        save.start()
+    for copy in saves:
+        copy.wait()
 
 
 def local(
@@ -993,21 +1133,16 @@
         n_experts,
         w_in.shape[2],
     )
-    gap = jnp.zeros((s.SR, GAIN_ATTN_LANE - n_experts), BF)
-    small = jnp.concatenate(
-        [w_router, gap, norm_gain_attn[:, None], norm_gain_ffn[:, None]], axis=1
-    )
-    bias = jnp.pad(rel_bias, ((0, s.NBP - buckets_here), (0, LANES - heads)))
-    small = jnp.concatenate([small, bias], axis=0)
-    table = jnp.pad(jnp.stack([relpos_table, relpos_table[::-1]]), ((0, 0), (0, 1)))
     operands = [
-        lengths, seq_order, small, expert_ids, priority.reshape(1, tok_count), table,
+        lengths, seq_order, expert_ids.reshape(1, tok_count), priority.reshape(1, tok_count),
+        relpos_table.reshape(1, -1), w_router.T, norm_gain_attn,
+        norm_gain_ffn, rel_bias,
         tokens, out_grad, w_query, w_key, w_value, w_output, w_in, w_out,
     ]
     smem, vmem, anywhere = (
         pl.BlockSpec(memory_space=space) for space in (pltpu.SMEM, pltpu.VMEM, pl.ANY)
     )
-    in_specs = [smem] * 2 + [vmem] * 4 + [anywhere] * 8
+    in_specs = [smem] * 2 + [vmem] * 7 + [anywhere] * 8
     names = IN_NAMES
     if s.padded:
         operands.append(selection(s))
@@ -1024,8 +1159,8 @@
             jax.ShapeDtypeStruct((s.T, s.D), F32),
             jax.ShapeDtypeStruct((4, s.SR, s.D), BF),
             jax.ShapeDtypeStruct((s.SR, LANES), F32),
-            jax.ShapeDtypeStruct((1, s.D, s.F), F32),
-            jax.ShapeDtypeStruct((1, s.F, s.D), F32),
+            jax.ShapeDtypeStruct((s.D, s.F), BF),
+            jax.ShapeDtypeStruct((s.F, s.D), BF),
             *spilled,
         ),
         in_specs=in_specs,
@@ -1035,18 +1170,51 @@
             collective_id=0, has_side_effects=True, vmem_limit_bytes=62 * 2**20
         ),
     )(*operands)
-    layer_out, tokens_grad, grads, smalls, grad_w_in, grad_w_out = outs[:6]
+    done = pl.pallas_call(
+        functools.partial(finish, s),
+        name="finish",
+        out_shape=(
+            jax.ShapeDtypeStruct((s.T, s.D), BF),
+            jax.ShapeDtypeStruct((s.T, s.D), F32),
+            *[jax.ShapeDtypeStruct((s.SR, s.D), F32)] * 4,
+            jax.ShapeDtypeStruct((1, s.D, s.F), F32),
+            jax.ShapeDtypeStruct((1, s.F, s.D), F32),
+            jax.ShapeDtypeStruct((1, s.SR), F32),
+            jax.ShapeDtypeStruct((1, s.SR), F32),
+            jax.ShapeDtypeStruct((buckets_here, heads), F32),
+            jax.ShapeDtypeStruct((n_experts, s.SR), F32),
+        ),
+        in_specs=[anywhere, anywhere, anywhere, vmem, anywhere, anywhere],
+        out_specs=(anywhere,) * 8 + (vmem,) * 4,
+        scratch_shapes=[
+            pltpu.VMEM((4, s.SR, s.D), BF),
+            pltpu.VMEM((s.D, s.F), BF),
+            pltpu.VMEM((s.F, s.D), BF),
+            pltpu.VMEM((4, s.SR, s.D), F32),
+            pltpu.VMEM((s.D, s.F), F32),
+            pltpu.VMEM((s.F, s.D), F32),
+            pltpu.VMEM((s.T, s.D), BF),
+            pltpu.VMEM((s.T, s.D), F32),
+            pltpu.SemaphoreType.DMA((2, 2)),
+            pltpu.SemaphoreType.DMA((4,)),
+            pltpu.SemaphoreType.DMA((4,)),
+            pltpu.SemaphoreType.DMA((2, PARTS)),
+            pltpu.SemaphoreType.DMA((2, PARTS)),
+        ],
+        compiler_params=pltpu.CompilerParams(vmem_limit_bytes=62 * 2**20),
+    )(*outs[:6])
+    layer_out, tokens_grad, gq, gk, gv, go, grad_w_in, grad_w_out, gain1, gain2, rel, router = done
     return (
         layer_out,
         tokens_grad,
-        smalls[:, GAIN_ATTN_LANE],
-        grads[0].astype(F32),
-        grads[1].astype(F32),
-        grads[2].astype(F32),
-        grads[3].astype(F32),
-        smalls[:buckets_here, REL_LANE : REL_LANE + heads],
-        smalls[:, GAIN_FFN_LANE],
-        smalls[:, :n_experts],
+        gain1.reshape(s.SR),
+        gq,
+        gk,
+        gv,
+        go,
+        rel,
+        gain2.reshape(s.SR),
+        router.T,
         grad_w_in,
         grad_w_out,
     )

time: 196 us -> 179 us (0.913)
  local copies, waits for them, and re-layouts: 15.5 us -> 0 us
  other arithmetic: 4.93 us -> 0 us
  Pallas kernels: 174 us -> 178 us
    unnamed x17 -> x0, local copies, waits for them, and re-layouts: 10.3 us -> none
    pallas_call x0 -> x1, Pallas kernels: none -> 7.07 us  [local(): pl.pallas_call(functools.partial(finish, s), name='finish', out_shape=(ja...]
    slice x2 -> x0, local copies, waits for them, and re-layouts: 3.18 us -> none  [the longest x1 1.84 us: local(): smalls[:, GAIN_FFN_LANE]]
    pallas_call x1, Pallas kernels: 174 us -> 171 us  [local(): pl.pallas_call(functools.partial(kernel, s, names), name='layer', out_sha...]
    convert_element_type x1 -> x0, other arithmetic: 2.81 us -> none  [local(): grads[3].astype(F32)]
where the time goes in v4:
time: 179 us
  Pallas kernels  178 us (99%)
    pallas_call x1, Pallas kernels, local(): pl.pallas_call(functools.partial(kernel, s, names), name='layer', out_sha...  171 us
    pallas_call x1, Pallas kernels, local(): pl.pallas_call(functools.partial(finish, s), name='finish', out_shape=(ja...  7.07 us

profile of v4, /device:TPU:0, one launch (start us, length us, event | category | flops | bytes accessed | tf_op | source)
XLA Modules:
  0.0 179.1 jit_solution(4852826252872481186)
XLA Ops:
  0.7 171.2 %layer.1 = (bf16[256,768]{1,0:T(8,128)(2,1)}, f32[256,768]{1,0:T(8,128)}, bf16[4,192,768]{2,1,0:T(8,128)(2,1)}, f32[192,128]{1,0:T(8,128)}, bf16[768,768]{1,0:T(8,128)(2,1)}, /*index=5*/bf16[768,768]{1,0:T(8,128)(2,1)}) custom-call(s32[64]{0:T(128)} %refs_0_.1, s32[64]{0:T(128)} %refs_1_.1, s32[1,256]{1,0:T(1,128)} %bitcast.9, s32[1,256]{1,0:T(1,128)} %bitcast.10, ...), custom_call_target="tpu_custom_call" | custom-call | tf_op jit(solution)/shard_map/layer/pallas_call | solution.py:1154
  171.9 7.1 %finish.1 = (bf16[256,768]{1,0:T(8,128)(2,1)}, f32[256,768]{1,0:T(8,128)}, f32[192,768]{1,0:T(8,128)}, f32[192,768]{1,0:T(8,128)}, f32[192,768]{1,0:T(8,128)}, /...) custom-call(bf16[256,768]{1,0:T(8,128)(2,1)} %get-tuple-element.30.r, ...), custom_call_target="tpu_custom_call" | custom-call | tf_op jit(solution)/shard_map/finish/pallas_call | solution.py:1173

commit v5 on v3

--- a/solution.py
+++ b/solution.py
@@ -79,6 +79,8 @@
     s.NBH = buckets_here
     s.NBP = up16(buckets_here)
     s.half = width // 2
+    s.P1 = up16(n_experts + 2)
+    s.LW = -(-s.SR // LANES) * LANES
     team = s.C
     while s.SR % team or (s.SR // team) % 16:
         team //= 2
@@ -106,7 +108,9 @@
     dma = pltpu.SemaphoreType.DMA
     return [
         ("wfull", V((4, s.D, s.D), BF)),
-        ("smg", V((s.W, s.SR + s.NBP, LANES), BF)),
+        ("smf", V((s.P1 + s.NBP, s.LW), F32)),
+        ("smg", V((s.W, s.P1 + s.NBP, s.LW), BF)),
+        ("tab", V((8, 2 * s.T), I32)),
         ("xb", V((s.T, s.D), BF)),
         ("og", V((s.T, s.D), BF)),
         ("wi", V((s.D, s.F), BF)),
@@ -122,17 +126,21 @@
         ("agr", V((s.W * s.R, s.F), BF)),
         ("act", V((s.W * s.R, s.F), BF)),
         ("ig", V((s.W * s.R, s.F), BF)),
-        ("SS", V((s.W, s.R, s.D + LANES), BF)),
-        ("Sin", V((s.W + 1, s.R, s.D + LANES), BF)),
-        ("Sb", V((s.R, s.D + LANES), s.dt)),
-        ("Sk", V((s.S, s.D + LANES), s.dt)),
+        ("SS", V((s.W, s.R, s.D), BF)),
+        ("Sin", V((s.W + 1, s.R, s.D), BF)),
+        ("Sb", V((s.R, s.D), s.dt)),
+        ("Sk", V((s.S, s.D), s.dt)),
+        ("HS", V((s.W, 8, s.R), F32)),
+        ("Hr", V((s.W, 8, s.R), F32)),
+        ("Hb", V((8, s.R), F32)),
+        ("Hk", V((s.E, 8, s.R), F32)),
+        ("Hm", V((LANES, s.R), F32)),
         ("Rb", V((s.R, s.D), s.dt)),
         ("Rk", V((s.S, s.D), s.dt)),
         ("tb", V((LANES, 2 * s.T), F32)),
-        ("oh", V((s.W * s.NBP, 2 * s.T), BF)),
         ("ohm", V((s.W * s.NBP, 2 * s.T), BF)),
         ("rows", V((8, s.D), F32)),
-        ("Rw", V((s.D, LANES), BF)),
+        ("RwT", V((LANES, s.D), BF)),
         ("probs", V((s.H, s.T, s.T), F32)),
         ("q", V((s.T, s.D), BF)),
         ("kk", V((s.T, s.D), BF)),
@@ -160,14 +168,16 @@
         ("hZR", V((s.W - 1, s.pr, LANES), BF)),
         ("hFG", V((s.CP, LANES), BF)),
         ("bt", V((LANES, 2 * s.T), F32)),
-        ("gwi", V((s.slots, s.tile, s.F), F32)),
-        ("gwo", V((s.slots, s.tile, s.D), F32)),
+        ("gwi", V((s.slots, s.tile, s.F), BF)),
+        ("gwo", V((s.slots, s.tile, s.D), BF)),
         ("gwi_sem", dma((s.slots,))),
         ("gwo_sem", dma((s.slots,))),
         ("lsem", dma((9,))),
         ("smr", dma((s.W,))),
-        ("wa", dma((4, s.W))),
-        ("wb", dma((4,))),
+        ("wu", dma((4, s.W))),
+        ("wd", dma((4, s.W))),
+        ("wbu", dma((4, s.W))),
+        ("wbd", dma((4, s.W))),
         ("wc", dma((4,))),
         ("g1", dma((s.C,))),
         ("gu", dma((s.W, s.C))),
@@ -177,9 +187,14 @@
         ("nd", dma((s.W, s.C))),
         ("t1", dma((s.C,))),
         ("t2", dma((s.W,))),
+        ("hz", dma((s.W,))),
+        ("hp", dma),
+        ("x_hz", dma((s.W,))),
+        ("x_hp", dma),
         ("su", dma((s.W, s.C))),
         ("sd", dma((s.W, s.C))),
-        ("r3", dma((s.W,))),
+        ("ru", dma((s.W,))),
+        ("rdn", dma((s.W,))),
         ("back", dma((2,))),
         ("sibT", dma((2,))),
         ("sibF", dma((4,))),
@@ -188,7 +203,8 @@
         ("rc", dma((5,))),
         ("rd", dma((5,))),
         ("x_sm", dma),
-        ("x_wa", dma((4,))),
+        ("x_wu", dma((4, s.W))),
+        ("x_wd", dma((4, s.W))),
         ("x_wb", dma((4,))),
         ("x_wc", dma((4,))),
         ("x_d1", dma((3,))),
@@ -199,7 +215,8 @@
         ("x_nd", dma((s.W,))),
         ("x_su", dma((s.W,))),
         ("x_sd", dma((s.W,))),
-        ("x_r3", dma((s.W,))),
+        ("x_ru", dma((s.W,))),
+        ("x_rdn", dma((s.W,))),
         ("x_back", dma((2,))),
         ("x_sibT", dma((2,))),
         ("x_sibF", dma((4,))),
@@ -212,12 +229,16 @@
         [("gst", V((s.W * s.pr, s.half), BF))]
         + [(name, V((s.R, width), F32)) for name, width in arrivals(s)]
         if s.padded
-        else [("GR", V(pieces_shape(s), BF))]
+        else [
+            ("GR", V(pieces_shape(s), BF)),
+            ("RS", V((s.W, s.R, s.D), BF)),
+            ("Rin", V((s.W + 1, s.R, s.D), BF)),
+        ]
     )
 
 
 IN_NAMES = (
-    "lengths", "seq", "small", "ids", "prio", "table",
+    "lengths", "seq", "ids", "prio", "table", "router", "gain_attn", "gain_ffn", "bias",
     "tokens", "out_grad", "w0", "w1", "w2", "w3", "w_in", "w_out",
 )
 PAD_NAMES = ("unsel",)
@@ -255,15 +276,21 @@
     shards = (r.w0, r.w1, r.w2, r.w3)
     own_rows = pl.ds(aligned(z * s.SR, 16), s.SR)
     load_w = [
-        pltpu.make_async_copy(shards[m].at[:, here], r.wfull.at[m, own_rows, here], r.lsem.at[m])
+        pltpu.make_async_copy(shards[m], r.wfull.at[m, own_rows], r.lsem.at[m])
         for m in range(4)
     ]
     load_og = pltpu.make_async_copy(r.out_grad, r.og, r.lsem.at[4])
     load_x = pltpu.make_async_copy(r.tokens, r.xb, r.lsem.at[5])
     load_wo = pltpu.make_async_copy(r.w_out.at[0], r.wo, r.lsem.at[6])
     load_wi = pltpu.make_async_copy(r.w_in.at[0], r.wi, r.lsem.at[7])
-    for copy in (*load_w, load_og, load_x, load_wo, load_wi):
-        copy.start()
+    load_og.start()
+
+    r.smf[...] = jnp.zeros_like(r.smf)
+    r.smf[0 : s.NX, 0 : s.SR] = r.router[...].astype(F32)
+    r.smf[s.NX : s.NX + 1, 0 : s.SR] = r.gain_attn[...].astype(F32).reshape(1, s.SR)
+    r.smf[s.NX + 1 : s.NX + 2, 0 : s.SR] = r.gain_ffn[...].astype(F32).reshape(1, s.SR)
+    r.smf[s.P1 : s.P1 + s.NBH, 0 : s.H] = r.bias[...].astype(F32)
+    r.smg[z] = r.smf[...].astype(BF)
 
     barrier = pltpu.get_barrier_semaphore()
     peers = [(flip(e, o), z) for o in range(1, E)] + [zpeer(o) for o in range(1, W)]
@@ -272,21 +299,24 @@
     pl.semaphore_wait(barrier, len(peers))
 
     team_c = lax.rem(c, s.team)
-    r.smg[z] = r.small[...]
     for o in range(1, W):
-        remote(r.small, r.smg.at[z], r.x_sm, r.smr.at[o], zpeer(o)).start()
-    piece = pl.ds(aligned(z * s.SR + team_c * s.pw, 16), s.pw)
+        remote(r.smg.at[z], r.smg.at[z], r.x_sm, r.smr.at[o], zpeer(o)).start()
     share_rows = pl.ds(aligned(team_c * s.pw, 16), s.pw)
-    for m in range(4):
-        for o in range(1, W):
-            remote(
-                shards[m].at[share_rows, here],
-                r.wfull.at[m, piece, here],
-                r.x_wa.at[m],
-                r.wa.at[m, o],
-                zpeer(o),
-            ).start()
-
+    def weight_at(plane):
+        return pl.ds(aligned(plane * s.SR + team_c * s.pw, 16), s.pw)
+
+    def weight_own(m):
+        def send(sender, receiver, to):
+            source = shards[m].at[share_rows, here]
+            remote(source, r.wfull.at[m, weight_at(z), here], sender, receiver, (e, to)).start()
+
+        pl.when(z < W - 1)(functools.partial(send, r.x_wu.at[m, 0], r.wu.at[m, 1], z + 1))
+        pl.when(z > 0)(functools.partial(send, r.x_wd.at[m, 0], r.wd.at[m, 1], z - 1))
+
+    for m in range(3):
+        weight_own(m)
+    for copy in (load_x, *load_w, load_wo, load_wi):
+        copy.start()
     device = e * W + z
     first = r.lengths[r.seq[2 * device]]
     both = first + r.lengths[r.seq[2 * device + 1]]
@@ -297,8 +327,8 @@
     same = seg_col == seg_row
     valid = (col < both).astype(F32)
     eye = iota((T, T), 0) == iota((T, T), 1)
-    id_col = r.ids[...].astype(F32)
-    id_row = jnp.sum(jnp.where(eye, id_col, 0.0), axis=0, keepdims=True)
+    id_row = r.ids[...].astype(F32)
+    id_col = jnp.sum(jnp.where(eye, id_row, 0.0), axis=1, keepdims=True)
     prio_row = r.prio[...].astype(F32)
     prio_col = jnp.sum(jnp.where(eye, prio_row, 0.0), axis=1, keepdims=True)
     ahead = (id_col == id_row) & (prio_col < prio_row)
@@ -375,41 +405,78 @@
     load_og.wait()
     dispatch(0, r.gsend, Ga, r.g1, r.og[...])
 
-    def pass_on(m):
-        for o in range(1, W):
-            begin = flip(z, o) * s.SR + team_c * s.pw
-            part = r.wfull.at[m, pl.ds(aligned(begin, 16), s.pw), here]
-            got(part, r.wa.at[m, o])
+    def weight_pass(m, d):
+        def handle(plane, arrived, onward, sender, receiver, to, beside):
+            part = r.wfull.at[m, weight_at(plane), here]
+            got(part, arrived)
+            if d < W - 1:
+                pl.when(onward)(functools.partial(move, part, sender, receiver, to))
             for oc in range(1, s.team):
-                remote(part, part, r.x_wb.at[m], r.wb.at[m], cpeer(oc)).start()
-
-    def to_sibling(m):
-        if s.team > 1:
-            got(r.wfull.at[m, pl.ds(0, (W - 1) * (s.team - 1) * s.pw), here], r.wb.at[m])
+                remote(part, part, r.x_wb.at[m], beside, cpeer(oc)).start()
+
+        up, down, after = (m, d), (m, d), (m, min(d + 1, W - 1))
+        pl.when(z >= d)(
+            functools.partial(
+                handle, z - d, r.wu.at[up], z < W - 1, r.x_wu.at[up], r.wu.at[after], z + 1, r.wbu.at[up]
+            )
+        )
+        pl.when(z + d <= W - 1)(
+            functools.partial(
+                handle, z + d, r.wd.at[down], z > 0, r.x_wd.at[down], r.wd.at[after], z - 1, r.wbd.at[down]
+            )
+        )
+
+    def weight_share(m, d):
+        def handle(plane, beside):
+            if s.team > 1:
+                got(r.wfull.at[m, pl.ds(0, (s.team - 1) * s.pw), here], beside)
+            part = r.wfull.at[m, pl.ds(aligned(plane * s.SR, 16), s.SR), here]
+            remote(part, part, r.x_wc.at[m], r.wc.at[m], sib).start()
+
+        pl.when(z >= d)(functools.partial(handle, z - d, r.wbu.at[m, d]))
+        pl.when(z + d <= W - 1)(functools.partial(handle, z + d, r.wbd.at[m, d]))
+
+    others = pl.ds(0, (W - 1) * s.SR)
+
+    def weight_ready(m):
         load_w[m].wait()
-        part = r.wfull.at[m, :, here]
-        remote(part, part, r.x_wc.at[m], r.wc.at[m], sib).start()
-
-    def weight_ready(m):
-        got(r.wfull.at[m, :, there], r.wc.at[m])
-
+        got(r.wfull.at[m, others, there], r.wc.at[m])
+
+    for d in range(1, W):
+        for m in range(3):
+            weight_pass(m, d)
+        if d == 1:
+            weight_own(3)
+        else:
+            weight_pass(3, d - 1)
+            for m in range(3):
+                weight_share(m, d - 1)
+        if d == min(2, W - 1):
+            line_own(r.Gr, Ga, r.g1, *g_line)
+    weight_pass(3, W - 1)
+    for m in range(3):
+        weight_share(m, W - 1)
     for o in range(1, W):
-        got(r.small, r.smr.at[o])
-    pass_on(0)
-    router_rows = r.smg[:, : s.SR, :].reshape(D, LANES)
-    turned = router_rows.astype(F32).T
-    r.rows[0:1, :] = turned[GAIN_ATTN_LANE : GAIN_ATTN_LANE + 1, :]
-    r.rows[1:2, :] = turned[GAIN_FFN_LANE : GAIN_FFN_LANE + 1, :]
+        got(r.smg.at[0], r.smr.at[o])
+    gathered = jnp.concatenate(
+        [r.smg[w, : s.P1, : s.SR].astype(F32) for w in range(W)], axis=1
+    )
+    r.rows[0:1, :] = gathered[s.NX : s.NX + 1]
+    r.rows[1:2, :] = gathered[s.NX + 1 : s.NX + 2]
+    r.RwT[...] = jnp.zeros_like(r.RwT)
+    r.RwT[: s.P1, :] = jnp.where(iota((s.P1, D), 0) < s.NX, gathered, 0.0).astype(BF)
     lane_row = iota((1, LANES), 1)
-    r.Rw[...] = router_rows * (lane_row < s.NX).astype(F32).astype(BF)
-    bucket = r.table[...]
+    r.tab[...] = jnp.full(r.tab.shape, -1, I32)
+    r.tab[0:1, 0 : 2 * T - 1] = r.table[...]
+    bucket = r.tab[0:1, :]
     shift = s.NBH.bit_length() - 1
     bucket = lax.shift_right_logical(bucket, shift) * s.NBP + lax.bitwise_and(bucket, s.NBH - 1)
-    bucket_at = iota((W * s.NBP, 2 * T), 0)
-    r.oh[...] = (bucket_at == bucket[0:1]).astype(F32).astype(BF)
-    r.ohm[...] = (bucket_at == bucket[1:2]).astype(F32).astype(BF)
-    bias_rows = r.smg[:, s.SR :, :].reshape(W * s.NBP, LANES)
-    r.tb[...] = dot_lt(bias_rows, r.oh[...])
+    bucket = jnp.where(r.tab[0:1, :] < 0, -1, bucket)
+    hot = (iota((W * s.NBP, 2 * T), 0) == bucket).astype(F32).astype(BF)
+    backwards = (iota((2 * T, 2 * T), 0) + iota((2 * T, 2 * T), 1) == 2 * T - 2).astype(F32)
+    r.ohm[...] = dot(hot, backwards.astype(BF)).astype(BF)
+    bias_rows = r.smg[:, s.P1 :, :LANES].reshape(W * s.NBP, LANES)
+    r.tb[...] = dot_lt(bias_rows, hot)
 
     def bias_head(h, carry):
         wide = jnp.broadcast_to(r.tb[pl.ds(h, 1), :], (T, 2 * T))
@@ -417,18 +484,7 @@
         r.probs[h] = jnp.where(same, turned[:, :T], NEG_FILL)
         return carry
 
-    third = s.H // 3
-    pass_on(1)
-    lax.fori_loop(0, third, bias_head, 0)
-    pass_on(2)
-    to_sibling(0)
-    lax.fori_loop(third, 2 * third, bias_head, 0)
-    to_sibling(1)
-    line_own(r.Gr, Ga, r.g1, *g_line)
-    pass_on(3)
-    lax.fori_loop(2 * third, s.H, bias_head, 0)
-    to_sibling(2)
-
+    lax.fori_loop(0, s.H, bias_head, 0)
     load_x.wait()
     x = r.xb[...].astype(F32)
     scale1 = lax.rsqrt(jnp.mean(x * x, axis=1, keepdims=True) + EPSILON)
@@ -451,9 +507,10 @@
     r.q[...] = dot(normed, r.wfull[0]).astype(BF)
     weight_ready(1)
     r.kk[...] = dot(normed, r.wfull[1]).astype(BF)
-    to_sibling(3)
     weight_ready(2)
     r.v[...] = dot(normed, r.wfull[2]).astype(BF)
+    for d in range(1, W):
+        weight_share(3, d)
     line_pass(r.Gr, 1, *g_line)
 
     scale = s.HD ** (-0.5)
@@ -476,8 +533,6 @@
 
     lax.fori_loop(0, s.H // 2, attend, 0)
     mixed = r.mixed[...]
-    if W > 2:
-        line_pass(r.Gr, 2, *g_line)
     weight_ready(3)
     middle = r.xb[...].astype(F32) + dot(mixed, r.wfull[3]) * valid
     r.middle[...] = middle
@@ -485,7 +540,7 @@
     nf = (middle * scale2 * r.rows[1:2, :]).astype(BF)
     r.nf[...] = nf
     dispatch(1, r.nsend, Na, r.n1, nf)
-    logits = jnp.where(lane_row < s.NX, dot(nf, r.Rw[...]), NEG_FILL)
+    logits = jnp.where(lane_row < s.NX, dot_rt(nf, r.RwT[...]), NEG_FILL)
     raised = jnp.exp(logits - jnp.max(logits, axis=1, keepdims=True))
     router = raised / jnp.sum(raised, axis=1, keepdims=True)
     picked = (lane_row.astype(F32) == id_col).astype(F32)
@@ -498,6 +553,8 @@
         jnp.where(lane_row == 1, gate_mid.astype(F32), jnp.where(lane_row == 2, gate_low.astype(F32), 0.0)),
     )
     dispatch(2, r.tsend, Ta, r.t1, gate_lanes.astype(BF))
+    if W > 2:
+        line_pass(r.Gr, 2, *g_line)
     line_own(r.Nr, Na, r.n1, *n_line)
     for oc in range(C):
         landed(r.Tr, Ta, r.t1, oc)
@@ -518,14 +575,7 @@
     lax.fori_loop(0, W, back_rows, 0)
     load_wi.wait()
 
-    def lanes_of(value):
-        high, rest = two_parts(value)
-        return jnp.where(
-            lane_row == 0, high.astype(F32), jnp.where(lane_row == 1, rest.astype(F32), 0.0)
-        )
-
-    def expert(plane):
-        at = pl.ds(aligned(plane * R, 16), R)
+    def expert_rows(plane, at, block):
         inner = dot(r.Nr[at, :], r.wi[...])
         square = inner * inner
         tanh = jnp.tanh(GELU_A * inner * (1.0 + GELU_B * square))
@@ -533,21 +583,52 @@
         slope = 0.5 * (1.0 + tanh) + (0.5 * GELU_A) * inner * (1.0 - tanh * tanh) * (
             1.0 + (3.0 * GELU_B) * square
         )
-        back = r.agr[at, :].astype(F32)
-        inner_grad = (back * slope).astype(BF)
+        inner_grad = (r.agr[at, :].astype(F32) * slope).astype(BF)
         r.act[at, :] = active
         r.ig[at, :] = inner_grad
-        r.SS[plane, :, :D] = dot_rt(inner_grad, r.wi[...]).astype(BF)
-        r.SS[plane, :, D:] = lanes_of(
-            jnp.sum(active.astype(F32) * back, axis=1, keepdims=True)
+        r.SS[plane, block, :] = dot_rt(inner_grad, r.wi[...]).astype(BF)
+
+    def expert(plane):
+        expert_rows(plane, pl.ds(aligned(plane * R, 16), R), pl.ds(0, R))
+
+    def gate_sums(plane, carry):
+        at = pl.ds(aligned(plane * R, 16), R)
+        part = jnp.sum(
+            r.act[at, :].astype(F32) * r.agr[at, :].astype(F32), axis=1, keepdims=True
+        )
+        diagonal = iota((R, R), 0) == iota((R, R), 1)
+        r.HS[plane, 0:1, :] = jnp.sum(jnp.where(diagonal, part, 0.0), axis=0, keepdims=True)
+
+        @pl.when(plane != z)
+        def _():
+            remote(r.HS.at[plane], r.Hr.at[z], r.x_hz.at[plane], r.hz.at[z], (e, plane)).start()
+
+        return carry
+
+    def merge(plane, slot, block):
+        r.SS[plane, block, :] = (
+            r.SS[plane, block, :].astype(F32) + r.Sin[slot, block, :].astype(F32)
         ).astype(BF)
 
-    def merge(plane, slot, block):
-        own, other = r.SS[plane, block, :].astype(F32), r.Sin[slot, block, :].astype(F32)
-        r.SS[plane, block, :D] = (own[:, :D] + other[:, :D]).astype(BF)
-        r.SS[plane, block, D:] = lanes_of(
-            jnp.sum(own[:, D:] + other[:, D:], axis=1, keepdims=True)
-        ).astype(BF)
+    def sum_down(plane, gap, oc):
+        block = block_at(0, oc)
+        remote(
+            r.SS.at[plane, block],
+            r.Sin.at[plane, block],
+            r.x_sd.at[gap],
+            r.sd.at[gap - 1, oc],
+            (e, z - 1),
+        ).start()
+
+    def sum_up(plane, gap, oc):
+        block = block_at(0, oc)
+        remote(
+            r.SS.at[plane, block],
+            r.Sin.at[plane + 1, block],
+            r.x_su.at[gap],
+            r.su.at[gap - 1, oc],
+            (e, z + 1),
+        ).start()
 
     def plane_back(index, source, target, offsets):
         mine = pl.ds(aligned(e * cp, plane_step), cp)
@@ -564,9 +645,69 @@
                 (x, z),
             ).start()
 
+    early = not s.padded
+    RS, Rin = (r.RS, r.Rin) if early else (r.SS, r.Sin)
+
+    def results_begin():
+        if not early:
+            for d in range(1, W):
+                pl.when(z >= d)(functools.partial(sent, r.SS.at[0], r.x_sd.at[d]))
+                pl.when(z + d <= W - 1)(functools.partial(sent, r.SS.at[0], r.x_su.at[d]))
+            pl.semaphore_wait(r.credit, W - 1)
+
+        def results(step, carry):
+            at = pl.ds(aligned(step * R, 16), R)
+            RS[step] = dot(r.act[at, :], r.wo[...]).astype(BF)
+            return carry
+
+        lax.fori_loop(0, W, results, 0)
+
+    def result_merge(plane, slot, sem):
+        got(Rin.at[slot], sem)
+        RS[plane] = (RS[plane].astype(F32) + Rin[slot].astype(F32)).astype(BF)
+
+    def results_pass(step):
+        below = step - (W - 1 - z)
+        above = W - 1 - step + z
+
+        @pl.when((below >= 0) & (below < z))
+        def _():
+            @pl.when(z < W - 1)
+            def _():
+                result_merge(below, below, r.rdn.at[z - below])
+
+            remote(
+                RS.at[below],
+                Rin.at[below],
+                r.x_rdn.at[z - below],
+                r.rdn.at[z - below - 1],
+                (e, z - 1),
+            ).start()
+
+        @pl.when((above <= W - 1) & (above > z))
+        def _():
+            @pl.when(z > 0)
+            def _():
+                result_merge(above, above + 1, r.ru.at[above - z])
+
+            remote(
+                RS.at[above],
+                Rin.at[above + 1],
+                r.x_ru.at[above - z],
+                r.ru.at[above - z - 1],
+                (e, z + 1),
+            ).start()
+
+    passes = iter(range(W - 1))
+
+    def next_pass():
+        for step in passes:
+            results_pass(step)
+            break
+
     expert(z)
     for step in range(1, 2 * W - 2):
-        if step < W:
+        if step < W - 1:
             line_pass(r.Nr, step, *n_line)
 
             def sides(side, carry, step=step):
@@ -576,46 +717,56 @@
 
             lax.fori_loop(0, 2, sides, 0)
 
+        if step == W - 1:
+            @pl.when((z == 0) | (z == W - 1))
+            def _():
+                plane = W - 1 - z
+                for oc in range(C):
+                    at = block_at(plane, oc)
+                    top = functools.partial(got, r.Nr.at[at], r.nu.at[W - 1, oc])
+                    bottom = functools.partial(got, r.Nr.at[at], r.nd.at[W - 1, oc])
+                    pl.when(z > 0)(top)
+                    pl.when(z == 0)(bottom)
+                    expert_rows(plane, at, block_at(0, oc))
+                    pl.when(z > 0)(functools.partial(sum_down, plane, W - 1, oc))
+                    pl.when(z == 0)(functools.partial(sum_up, plane, W - 1, oc))
+
         plane_down = 2 * W - 2 - z - step
         gap_down = z - plane_down
         plane_up = step - z
         gap_up = plane_up - z
-
-        @pl.when((plane_down >= 0) & (gap_down >= 1))
+        inner_down = (plane_down >= 0) & (gap_down >= 1)
+        inner_up = (plane_up <= W - 1) & (gap_up >= 1)
+        if step == W - 1:
+            inner_down, inner_up = inner_down & (z < W - 1), inner_up & (z > 0)
+
+        @pl.when(inner_down)
         def _():
             for oc in range(C):
-                block = block_at(0, oc)
 
                 @pl.when(z < W - 1)
                 def _():
-                    got(r.Sin.at[plane_down, block], r.sd.at[gap_down, oc])
-                    merge(plane_down, plane_down, block)
-
-                remote(
-                    r.SS.at[plane_down, block],
-                    r.Sin.at[plane_down, block],
-                    r.x_sd.at[gap_down],
-                    r.sd.at[gap_down - 1, oc],
-                    (e, z - 1),
-                ).start()
-
-        @pl.when((plane_up <= W - 1) & (gap_up >= 1))
+                    got(r.Sin.at[plane_down, block_at(0, oc)], r.sd.at[gap_down, oc])
+                    merge(plane_down, plane_down, block_at(0, oc))
+
+                sum_down(plane_down, gap_down, oc)
+
+        @pl.when(inner_up)
         def _():
             for oc in range(C):
-                block = block_at(0, oc)
 
                 @pl.when(z > 0)
                 def _():
-                    got(r.Sin.at[plane_up + 1, block], r.su.at[gap_up, oc])
-                    merge(plane_up, plane_up + 1, block)
-
-                remote(
-                    r.SS.at[plane_up, block],
-                    r.Sin.at[plane_up + 1, block],
-                    r.x_su.at[gap_up],
-                    r.su.at[gap_up - 1, oc],
-                    (e, z + 1),
-                ).start()
+                    got(r.Sin.at[plane_up + 1, block_at(0, oc)], r.su.at[gap_up, oc])
+                    merge(plane_up, plane_up + 1, block_at(0, oc))
+
+                sum_up(plane_up, gap_up, oc)
+
+        if step == W - 1:
+            if early:
+                results_begin()
+                next_pass()
+            lax.fori_loop(0, W, gate_sums, 0)
 
     for oc in range(C):
         block = block_at(0, oc)
@@ -633,80 +784,36 @@
         r.Sb[block, :] = r.SS[z, block, :].astype(s.dt)
         plane_back(0, r.Sb, r.Sk, (2 * oc, 2 * oc + 1))
 
-    line_sent(r.Gr, r.x_gu, r.x_gd)
+    total = r.HS[z]
     for o in range(1, W):
-        got(r.Tr.at[pl.ds(0, R)], r.t2.at[o])
-
-    def scale_rows(step, carry):
-        at = pl.ds(aligned(step * R, 16), R)
-        gates = jnp.sum(r.Tr[at, :].astype(F32), axis=1, keepdims=True)
-        r.Gr[at, :] = (r.Gr[at, :].astype(F32) * gates).astype(BF)
-        r.ig[at, :] = (r.ig[at, :].astype(F32) * gates).astype(BF)
-        return carry
-
-    lax.fori_loop(0, W, scale_rows, 0)
-    tile, slots = s.tile, s.slots
-
-    def save_out(step):
-        slot = lax.rem(step, slots)
-        at = pl.ds(aligned(step * tile, LANES), tile)
-        return pltpu.make_async_copy(r.gwo.at[slot], r.grad_w_out.at[0, at], r.gwo_sem.at[slot])
-
-    def save_in(step):
-        slot = lax.rem(step, slots)
-        at = pl.ds(aligned(step * tile, LANES), tile)
-        return pltpu.make_async_copy(r.gwi.at[slot], r.grad_w_in.at[0, at], r.gwi_sem.at[slot])
-
-    def grad_out_tile(step, carry):
-        @pl.when(step >= slots)
-        def _():
-            save_out(step - slots).wait()
-
-        at = pl.ds(aligned(step * tile, LANES), tile)
-        r.gwo[lax.rem(step, slots)] = dot_lt(r.act[:, at], r.Gr[...])
-        save_out(step).start()
-        return carry
-
-    def grad_in_tile(step, carry):
-        @pl.when(step >= slots)
-        def _():
-            save_in(step - slots).wait()
-
-        at = pl.ds(aligned(step * tile, LANES), tile)
-        r.gwi[lax.rem(step, slots)] = dot_lt(r.Nr[:, at], r.ig[...])
-        save_in(step).start()
-        return carry
-
-    lax.fori_loop(0, s.F // tile, grad_out_tile, 0)
-    lax.fori_loop(0, D // tile, grad_in_tile, 0)
-
-    for o in range(1, W):
-        pl.semaphore_signal(r.credit, inc=1, device_id=zpeer(o), device_id_type=MESH)
-    for d in range(1, W):
-        pl.when(z >= d)(functools.partial(sent, r.SS.at[0], r.x_sd.at[d]))
-        pl.when(z + d <= W - 1)(functools.partial(sent, r.SS.at[0], r.x_su.at[d]))
-    pl.semaphore_wait(r.credit, W - 1)
-
-    def results(step, carry):
-        at = pl.ds(aligned(step * R, 16), R)
-        r.SS[step, :, :D] = dot(r.act[at, :], r.wo[...]).astype(BF)
-        return carry
-
-    lax.fori_loop(0, W, results, 0)
-    for o in range(1, W):
-        remote(
-            r.SS.at[flip(z, o), :, pl.ds(0, D)],
-            r.Sin.at[z, :, pl.ds(0, D)],
-            r.x_r3.at[o],
-            r.r3.at[o],
-            zpeer(o),
-        ).start()
-
+        other = flip(z, o)
+        got(r.Hr.at[0], r.hz.at[other])
+        total = total + r.Hr[other]
+    r.Hb[...] = total
+    r.Hk[e] = total
+    for o in range(1, E):
+        remote(r.Hb, r.Hk.at[e], r.x_hp, r.hp, (flip(e, o), z)).start()
+
+    if not early:
+        for o in range(1, W):
+            pl.semaphore_signal(r.credit, inc=1, device_id=zpeer(o), device_id_type=MESH)
+        results_begin()
+    next_pass()
     got(r.Sk.at[pl.ds(0, (E - 1) * cp)], r.back.at[0])
+    got(r.Hk.at[pl.ds(0, E - 1)], r.hp)
+    r.Hm[...] = jnp.zeros_like(r.Hm)
+    for x in range(E):
+        r.Hm[x : x + 1, :] = r.Hk[x, 0:1, :]
+    slot_col = jnp.sum(jnp.where(eye, jnp.where(kept, slot_row, -1.0), 0.0), axis=1, keepdims=True)
+    slot_lane = jnp.where(slot_col < 0, -1.0, slot_col + (e * cp).astype(F32))
+    chosen = (iota((T, R), 1).astype(F32) == slot_lane).astype(F32).astype(BF)
+    high, rest = two_parts(r.Hm[...])
+    gate_grad = jnp.sum(
+        picked * (dot_rt(chosen, high) + dot_rt(chosen, rest)), axis=1, keepdims=True
+    )
     returned = dot(r.pt[...], r.Sk[...].astype(BF))
-    gate_grad = jnp.sum(returned[:, D:], axis=1, keepdims=True)
     logit_grad = (gate * gate_grad * (picked - router)).astype(BF)
-    nf_grad = dot_rt(logit_grad, r.Rw[...]) + gate * returned[:, :D]
+    nf_grad = dot(logit_grad, r.RwT[...]) + gate * returned
     middle = r.middle[...]
     along = nf_grad * r.rows[1:2, :]
     middle_grad = (
@@ -725,7 +832,6 @@
     share(3, r.att)
     r.mixed[...] = dot_rt(attended_grad, r.wfull[3]).astype(BF)
     router_grad = dot_lt(logit_grad, r.nf[...])
-
     def plane_sum(m, left, source):
         got(r.fac.at[m], r.sibF.at[m])
 
@@ -745,8 +851,21 @@
                 r.GS.at[m, flip(c, oc)], r.GR.at[m, oc - 1], r.x_ra.at[m], r.ra.at[m], cpeer(oc)
             ).start()
 
+    low_side = lane_row < s.HD
+
+    def values_back(p, carry):
+        cols = pl.ds(aligned(p * LANES, LANES), LANES)
+        mixg = r.mixed[:, cols]
+        outs = [dot_lt(r.probs[2 * p + side].astype(BF), mixg) for side in range(2)]
+        r.dv[:, cols] = jnp.where(low_side, outs[0], outs[1]).astype(BF)
+        return carry
+
+    lax.fori_loop(0, s.H // 2, values_back, 0)
+    share(2, r.dv)
     got(r.mT.at[:, pl.ds(T, T)], r.sibT.at[1])
     plane_sum(3, r.mT, r.att)
+    got(r.nT.at[:, pl.ds(T, T)], r.sibT.at[0])
+    plane_sum(2, r.nT, r.dv)
 
     def attend_back(p, carry):
         cols = pl.ds(aligned(p * LANES, LANES), LANES)
@@ -759,27 +878,15 @@
             inside = jnp.sum(probs * prob_grad, axis=1, keepdims=True)
             score_grad = (probs * (prob_grad - inside)).astype(BF)
             r.probs[h] = score_grad.astype(F32)
-            outs.append(
-                (
-                    dot(score_grad, kk) * scale,
-                    dot_lt(score_grad, q) * scale,
-                    dot_lt(probs.astype(BF), mixg),
-                )
-            )
-        low = lane_row < s.HD
-        r.dq[:, cols] = jnp.where(low, outs[0][0], outs[1][0]).astype(BF)
-        r.dk[:, cols] = jnp.where(low, outs[0][1], outs[1][1]).astype(BF)
-        r.dv[:, cols] = jnp.where(low, outs[0][2], outs[1][2]).astype(BF)
+            outs.append((dot(score_grad, kk) * scale, dot_lt(score_grad, q) * scale))
+        r.dq[:, cols] = jnp.where(low_side, outs[0][0], outs[1][0]).astype(BF)
+        r.dk[:, cols] = jnp.where(low_side, outs[0][1], outs[1][1]).astype(BF)
         return carry
 
     lax.fori_loop(0, s.H // 2, attend_back, 0)
     share(0, r.dq)
     share(1, r.dk)
-    share(2, r.dv)
-    got(r.nT.at[:, pl.ds(T, T)], r.sibT.at[0])
-    plane_sum(0, r.nT, r.dq)
-    plane_sum(1, r.nT, r.dk)
-    plane_sum(2, r.nT, r.dv)
+    next_pass()
 
     def shard_sum(m):
         got(r.GR.at[m], r.ra.at[m])
@@ -817,11 +924,11 @@
         part = r.FG.at[m, :, here]
         remote(part, part, r.x_rd.at[m], r.rd.at[m], sib).start()
 
-    shard_sum(3)
-
     normed_grad = (
         dot_rt(r.dq[...], r.wfull[0]) + dot_rt(r.dk[...], r.wfull[1]) + dot_rt(r.dv[...], r.wfull[2])
     )
+    plane_sum(0, r.nT, r.dq)
+    shard_sum(3)
     x = r.xb[...].astype(F32)
     along = normed_grad * r.rows[0:1, :]
     r.tokens_grad[...] = (
@@ -830,7 +937,6 @@
         - x * (scale1 * scale1 * scale1 * jnp.mean(along * x, axis=1, keepdims=True))
     )
     r.rows[3:4, :] = jnp.sum(normed_grad * x * scale1, axis=0, keepdims=True)
-
     r.bt[...] = jnp.zeros_like(r.bt)
     mirror = (iota((T, T), 0) + iota((T, T), 1) == T - 1).astype(F32).astype(BF)
 
@@ -842,6 +948,8 @@
         return carry
 
     lax.fori_loop(0, s.H, bias_back, 0)
+    plane_sum(1, r.nT, r.dk)
+    shard_sum(2)
     high, rest = two_parts(r.bt[...])
     rel_grad = dot_rt(r.ohm[...], high) + dot_rt(r.ohm[...], rest)
     lane_col = iota((LANES, 1), 0)
@@ -858,9 +966,7 @@
     small = jnp.concatenate(blocks, axis=0).astype(BF)
     r.smo[...] = spread_rows(small)
     remote(r.smo, r.sms, r.x_rd.at[4], r.rd.at[4], sib).start()
-    shard_sum(0)
-    shard_sum(1)
-    shard_sum(2)
+    spread(3)
     got(r.sms, r.rd.at[4])
     pair = (r.smo[...].astype(F32) + r.sms[...].astype(F32)).astype(BF)
     for block in range(W):
@@ -869,13 +975,64 @@
             r.hGS[chip, block * s.pr : (block + 1) * s.pr, :] = pair[at : at + s.pr]
     for oc in range(1, C):
         remote(r.hGS.at[flip(c, oc)], r.hGR.at[oc - 1], r.x_ra.at[4], r.ra.at[4], cpeer(oc)).start()
-    spread(3)
-
-    total = r.SS[z, :, :D].astype(F32)
+    line_sent(r.Gr, r.x_gu, r.x_gd)
     for o in range(1, W):
-        got(r.Sin.at[flip(z, o), :, pl.ds(0, D)], r.r3.at[o])
-        total = total + r.Sin[flip(z, o), :, :D].astype(F32)
-    r.Rb[...] = total.astype(BF).astype(s.dt)
+        got(r.Tr.at[pl.ds(0, R)], r.t2.at[o])
+
+    def scale_rows(step, carry):
+        at = pl.ds(aligned(step * R, 16), R)
+        gates = jnp.sum(r.Tr[at, :].astype(F32), axis=1, keepdims=True)
+        r.Gr[at, :] = (r.Gr[at, :].astype(F32) * gates).astype(BF)
+        r.ig[at, :] = (r.ig[at, :].astype(F32) * gates).astype(BF)
+        return carry
+
+    lax.fori_loop(0, W, scale_rows, 0)
+    tile, slots = s.tile, s.slots
+
+    def save_out(step):
+        slot = lax.rem(step, slots)
+        at = pl.ds(aligned(step * tile, LANES), tile)
+        return pltpu.make_async_copy(r.gwo.at[slot], r.grad_w_out.at[at], r.gwo_sem.at[slot])
+
+    def save_in(step):
+        slot = lax.rem(step, slots)
+        at = pl.ds(aligned(step * tile, LANES), tile)
+        return pltpu.make_async_copy(r.gwi.at[slot], r.grad_w_in.at[at], r.gwi_sem.at[slot])
+
+    def grad_out_tile(step, carry):
+        @pl.when(step >= slots)
+        def _():
+            save_out(step - slots).wait()
+
+        at = pl.ds(aligned(step * tile, LANES), tile)
+        r.gwo[lax.rem(step, slots)] = dot_lt(r.act[:, at], r.Gr[...]).astype(BF)
+        save_out(step).start()
+        return carry
+
+    def grad_in_tile(step, carry):
+        @pl.when(step >= slots)
+        def _():
+            save_in(step - slots).wait()
+
+        at = pl.ds(aligned(step * tile, LANES), tile)
+        r.gwi[lax.rem(step, slots)] = dot_lt(r.Nr[:, at], r.ig[...]).astype(BF)
+        save_in(step).start()
+        return carry
+
+
+    lax.fori_loop(0, s.F // tile, grad_out_tile, 0)
+    shard_sum(0)
+    spread(2)
+    share_sum(3)
+    lax.fori_loop(0, D // tile, grad_in_tile, 0)
+    shard_sum(1)
+    spread(0)
+    share_sum(2)
+    for step in passes:
+        results_pass(step)
+    pl.when(z < W - 1)(functools.partial(result_merge, z, z, r.rdn.at[0]))
+    pl.when(z > 0)(functools.partial(result_merge, z, z + 1, r.ru.at[0]))
+    r.Rb[...] = RS[z].astype(s.dt)
     plane_back(1, r.Rb, r.Rk, range(E))
 
     got(r.hGR, r.ra.at[4])
@@ -891,10 +1048,8 @@
             r.rb.at[4],
             zpeer(o),
         ).start()
-    spread(0)
     spread(1)
-    spread(2)
-    share_sum(3)
+    share_sum(0)
     got(r.hZR, r.rb.at[4])
     total = r.hZS[pl.ds(aligned(z * s.pr, 16), s.pr), :].astype(F32)
     for o in range(1, W):
@@ -908,9 +1063,7 @@
     got(r.Rk.at[pl.ds(0, (E - 1) * cp)], r.back.at[1])
     r.layer_out[...] = (r.middle[...] + gate * dot(r.pt[...], r.Rk[...].astype(BF))).astype(BF)
 
-    share_sum(0)
     share_sum(1)
-    share_sum(2)
     got(r.hFG.at[pl.ds(0, (C - 1) * s.pr)], r.rc.at[4])
 
     def unpad(value):
@@ -927,10 +1080,13 @@
         save_in(step).wait()
     sent(r.smg.at[pl.ds(0, W - 1)], r.x_sm)
     for m in range(4):
-        sent(r.wfull.at[m, pl.ds(0, (W - 1) * s.pw), here], r.x_wa.at[m])
+        part = r.wfull.at[m, pl.ds(0, s.pw), here]
+        for d in range(W - 1):
+            pl.when((z >= d) & (z < W - 1))(functools.partial(sent, part, r.x_wu.at[m, d]))
+            pl.when((z + d <= W - 1) & (z > 0))(functools.partial(sent, part, r.x_wd.at[m, d]))
         if s.team > 1:
             sent(r.wfull.at[m, pl.ds(0, (W - 1) * (s.team - 1) * s.pw), here], r.x_wb.at[m])
-        sent(r.wfull.at[m, :, here], r.x_wc.at[m])
+        sent(r.wfull.at[m, others, here], r.x_wc.at[m])
         sent(r.fac.at[m], r.x_sibF.at[m])
         sent(r.GR.at[m], r.x_ra.at[m])
         sent(r.ZR.at[m], r.x_rb.at[m])
@@ -940,8 +1096,15 @@
         sent(buffer.at[pl.ds(0, E - 1)], r.x_d1.at[index])
     line_sent(r.Nr, r.x_nu, r.x_nd)
     sent(r.Tr.at[pl.ds(0, (W - 1) * R)], r.x_t2)
-    for o in range(1, W):
-        sent(r.SS.at[0, :, pl.ds(0, D)], r.x_r3.at[o])
+    for d in range(1, W):
+        if early:
+            pl.when(z >= d)(functools.partial(sent, r.SS.at[0], r.x_sd.at[d]))
+            pl.when(z + d <= W - 1)(functools.partial(sent, r.SS.at[0], r.x_su.at[d]))
+        pl.when(z >= d)(functools.partial(sent, r.SS.at[0], r.x_rdn.at[d]))
+        pl.when(z + d <= W - 1)(functools.partial(sent, r.SS.at[0], r.x_ru.at[d]))
+    for plane in range(W):
+        pl.when(z != plane)(functools.partial(sent, r.HS.at[0], r.x_hz.at[plane]))
+    sent(r.Hk.at[pl.ds(0, E - 1)], r.x_hp)
     sent(r.Sk.at[pl.ds(0, (E - 1) * cp)], r.x_back.at[0])
     sent(r.Rk.at[pl.ds(0, (E - 1) * cp)], r.x_back.at[1])
     sent(r.nT.at[:, pl.ds(0, T)], r.x_sibT.at[0])
@@ -959,6 +1122,61 @@
         for at in range(share):
             unsel[chip * share + at, chip * s.pr + at] = 1
     return jnp.asarray(unsel, BF)
+
+
+PARTS = 3
+
+
+def finish(s, *refs):
+    layer_out, tokens_grad, grads, smalls, grad_in, grad_out = refs[:6]
+    out_layer, out_tokens, *out_mixers = refs[6:12]
+    out_in, out_out, out_gain1, out_gain2, out_rel, out_router = refs[12:18]
+    low_mix, low_in, low_out, mix, into, outof, held_layer, held_tokens = refs[18:26]
+    pass_sem, load_sem, save_sem, load2, save2 = refs[26:]
+    through = (
+        (layer_out, held_layer, out_layer),
+        (tokens_grad, held_tokens, out_tokens),
+    )
+    loads = [
+        pltpu.make_async_copy(source, held, pass_sem.at[0, index])
+        for index, (source, held, _) in enumerate(through)
+    ]
+    saves = [
+        pltpu.make_async_copy(held, target, pass_sem.at[1, index])
+        for index, (_, held, target) in enumerate(through)
+    ]
+    for m in range(4):
+        loads.append(pltpu.make_async_copy(grads.at[m], low_mix.at[m], load_sem.at[m]))
+        saves.append(pltpu.make_async_copy(mix.at[m], out_mixers[m], save_sem.at[m]))
+    steps = [None, None] + [(low_mix, mix, m) for m in range(4)]
+    for index, (source, low, high, target) in enumerate(
+        ((grad_in, low_in, into, out_in), (grad_out, low_out, outof, out_out))
+    ):
+        rows = source.shape[0] // PARTS
+        for part in range(PARTS):
+            at = pl.ds(part * rows, rows)
+            loads.append(
+                pltpu.make_async_copy(source.at[at], low.at[at], load2.at[index, part])
+            )
+            saves.append(
+                pltpu.make_async_copy(high.at[at], target.at[0, at], save2.at[index, part])
+            )
+            steps.append((low, high, at))
+    for copy in loads:
+        copy.start()
+    turned = smalls[...].T
+    out_router[...] = turned[: s.NX]
+    out_gain1[...] = turned[GAIN_ATTN_LANE : GAIN_ATTN_LANE + 1]
+    out_gain2[...] = turned[GAIN_FFN_LANE : GAIN_FFN_LANE + 1]
+    out_rel[...] = smalls[: s.NBH, REL_LANE : REL_LANE + s.H]
+    for load, save, step in zip(loads, saves, steps, strict=True):
+        load.wait()
+        if step is not None:
+            low, high, at = step
+            high[at] = low[at].astype(F32)
+        save.start()
+    for copy in saves:
+        copy.wait()
 
 
 def local(
@@ -993,21 +1211,16 @@
         n_experts,
         w_in.shape[2],
     )
-    gap = jnp.zeros((s.SR, GAIN_ATTN_LANE - n_experts), BF)
-    small = jnp.concatenate(
-        [w_router, gap, norm_gain_attn[:, None], norm_gain_ffn[:, None]], axis=1
-    )
-    bias = jnp.pad(rel_bias, ((0, s.NBP - buckets_here), (0, LANES - heads)))
-    small = jnp.concatenate([small, bias], axis=0)
-    table = jnp.pad(jnp.stack([relpos_table, relpos_table[::-1]]), ((0, 0), (0, 1)))
     operands = [
-        lengths, seq_order, small, expert_ids, priority.reshape(1, tok_count), table,
+        lengths, seq_order, expert_ids.reshape(1, tok_count), priority.reshape(1, tok_count),
+        relpos_table.reshape(1, -1), w_router.T, norm_gain_attn,
+        norm_gain_ffn, rel_bias,
         tokens, out_grad, w_query, w_key, w_value, w_output, w_in, w_out,
     ]
     smem, vmem, anywhere = (
         pl.BlockSpec(memory_space=space) for space in (pltpu.SMEM, pltpu.VMEM, pl.ANY)
     )
-    in_specs = [smem] * 2 + [vmem] * 4 + [anywhere] * 8
+    in_specs = [smem] * 2 + [vmem] * 7 + [anywhere] * 8
     names = IN_NAMES
     if s.padded:
         operands.append(selection(s))
@@ -1024,8 +1237,8 @@
             jax.ShapeDtypeStruct((s.T, s.D), F32),
             jax.ShapeDtypeStruct((4, s.SR, s.D), BF),
             jax.ShapeDtypeStruct((s.SR, LANES), F32),
-            jax.ShapeDtypeStruct((1, s.D, s.F), F32),
-            jax.ShapeDtypeStruct((1, s.F, s.D), F32),
+            jax.ShapeDtypeStruct((s.D, s.F), BF),
+            jax.ShapeDtypeStruct((s.F, s.D), BF),
             *spilled,
         ),
         in_specs=in_specs,
@@ -1035,18 +1248,51 @@
             collective_id=0, has_side_effects=True, vmem_limit_bytes=62 * 2**20
         ),
     )(*operands)
-    layer_out, tokens_grad, grads, smalls, grad_w_in, grad_w_out = outs[:6]
+    done = pl.pallas_call(
+        functools.partial(finish, s),
+        name="finish",
+        out_shape=(
+            jax.ShapeDtypeStruct((s.T, s.D), BF),
+            jax.ShapeDtypeStruct((s.T, s.D), F32),
+            *[jax.ShapeDtypeStruct((s.SR, s.D), F32)] * 4,
+            jax.ShapeDtypeStruct((1, s.D, s.F), F32),
+            jax.ShapeDtypeStruct((1, s.F, s.D), F32),
+            jax.ShapeDtypeStruct((1, s.SR), F32),
+            jax.ShapeDtypeStruct((1, s.SR), F32),
+            jax.ShapeDtypeStruct((buckets_here, heads), F32),
+            jax.ShapeDtypeStruct((n_experts, s.SR), F32),
+        ),
+        in_specs=[anywhere, anywhere, anywhere, vmem, anywhere, anywhere],
+        out_specs=(anywhere,) * 8 + (vmem,) * 4,
+        scratch_shapes=[
+            pltpu.VMEM((4, s.SR, s.D), BF),
+            pltpu.VMEM((s.D, s.F), BF),
+            pltpu.VMEM((s.F, s.D), BF),
+            pltpu.VMEM((4, s.SR, s.D), F32),
+            pltpu.VMEM((s.D, s.F), F32),
+            pltpu.VMEM((s.F, s.D), F32),
+            pltpu.VMEM((s.T, s.D), BF),
+            pltpu.VMEM((s.T, s.D), F32),
+            pltpu.SemaphoreType.DMA((2, 2)),
+            pltpu.SemaphoreType.DMA((4,)),
+            pltpu.SemaphoreType.DMA((4,)),
+            pltpu.SemaphoreType.DMA((2, PARTS)),
+            pltpu.SemaphoreType.DMA((2, PARTS)),
+        ],
+        compiler_params=pltpu.CompilerParams(vmem_limit_bytes=62 * 2**20),
+    )(*outs[:6])
+    layer_out, tokens_grad, gq, gk, gv, go, grad_w_in, grad_w_out, gain1, gain2, rel, router = done
     return (
         layer_out,
         tokens_grad,
-        smalls[:, GAIN_ATTN_LANE],
-        grads[0].astype(F32),
-        grads[1].astype(F32),
-        grads[2].astype(F32),
-        grads[3].astype(F32),
-        smalls[:buckets_here, REL_LANE : REL_LANE + heads],
-        smalls[:, GAIN_FFN_LANE],
-        smalls[:, :n_experts],
+        gain1.reshape(s.SR),
+        gq,
+        gk,
+        gv,
+        go,
+        rel,
+        gain2.reshape(s.SR),
+        router.T,
         grad_w_in,
         grad_w_out,
     )

time: 196 us -> 165 us (0.84)
  local copies, waits for them, and re-layouts: 15.5 us -> 0 us
  Pallas kernels: 174 us -> 164 us
  other arithmetic: 4.93 us -> 0 us
    pallas_call x1, Pallas kernels: 174 us -> 157 us  [local(): pl.pallas_call(functools.partial(kernel, s, names), name='layer', out_sha...]
    unnamed x17 -> x0, local copies, waits for them, and re-layouts: 10.3 us -> none
    pallas_call x0 -> x1, Pallas kernels: none -> 7.07 us  [local(): pl.pallas_call(functools.partial(finish, s), name='finish', out_shape=(ja...]
    slice x2 -> x0, local copies, waits for them, and re-layouts: 3.18 us -> none  [the longest x1 1.84 us: local(): smalls[:, GAIN_FFN_LANE]]
    convert_element_type x1 -> x0, other arithmetic: 2.81 us -> none  [local(): grads[3].astype(F32)]
where the time goes in v5:
time: 165 us; the launch traced here: 164 us
  Pallas kernels  164 us (99%)
    pallas_call x1, Pallas kernels, local(): pl.pallas_call(functools.partial(kernel, s, names), name='layer', out_sha...  157 us
    pallas_call x1, Pallas kernels, local(): pl.pallas_call(functools.partial(finish, s), name='finish', out_shape=(ja...  7.07 us

profile of v5, /device:TPU:0, one launch (start us, length us, event | category | flops | bytes accessed | tf_op | source)
XLA Modules:
  0.0 164.5 jit_solution(3321477355190123133)
XLA Ops:
  0.7 156.6 %layer.1 = (bf16[256,768]{1,0:T(8,128)(2,1)}, f32[256,768]{1,0:T(8,128)}, bf16[4,192,768]{2,1,0:T(8,128)(2,1)}, f32[192,128]{1,0:T(8,128)}, bf16[768,768]{1,0:T(8,128)(2,1)}, /*index=5*/bf16[768,768]{1,0:T(8,128)(2,1)}) custom-call(s32[64]{0:T(128)} %refs_0_.1, s32[64]{0:T(128)} %refs_1_.1, s32[1,256]{1,0:T(1,128)} %bitcast.9, s32[1,256]{1,0:T(1,128)} %bitcast.10, ...), custom_call_target="tpu_custom_call" | custom-call | tf_op jit(solution)/shard_map/layer/pallas_call | solution.py:1232
  157.2 7.1 %finish.1 = (bf16[256,768]{1,0:T(8,128)(2,1)}, f32[256,768]{1,0:T(8,128)}, f32[192,768]{1,0:T(8,128)}, f32[192,768]{1,0:T(8,128)}, f32[192,768]{1,0:T(8,128)}, /...) custom-call(bf16[256,768]{1,0:T(8,128)(2,1)} %get-tuple-element.30.r, ...), custom_call_target="tpu_custom_call" | custom-call | tf_op jit(solution)/shard_map/finish/pallas_call | solution.py:1251

commit v6 on v5

--- a/solution.py
+++ b/solution.py
@@ -100,7 +100,7 @@
 
 
 def arrivals(s):
-    return (("Ga", s.D), ("Na", s.D), ("Ta", LANES)) if s.dt == F32 else ()
+    return (("Ga", s.D), ("Na", s.D)) if s.dt == F32 else ()
 
 
 def scratch_list(s):
@@ -119,10 +119,11 @@
         ("pt", V((s.T, s.S), BF)),
         ("gsend", V((s.NX, s.cp, s.D), s.dt)),
         ("nsend", V((s.NX, s.cp, s.D), s.dt)),
-        ("tsend", V((s.NX, s.cp, LANES), s.dt)),
+        ("Qs", V((8, s.S), F32)),
+        ("Qk", V((s.E, 8, s.S), F32)),
+        ("Qr", V((s.W, 8, s.R), F32)),
         ("Gr", V((s.W * s.R, s.D), BF)),
         ("Nr", V((s.W * s.R, s.D), BF)),
-        ("Tr", V((s.W * s.R, LANES), BF)),
         ("agr", V((s.W * s.R, s.F), BF)),
         ("act", V((s.W * s.R, s.F), BF)),
         ("ig", V((s.W * s.R, s.F), BF)),
@@ -173,6 +174,8 @@
         ("gwi_sem", dma((s.slots,))),
         ("gwo_sem", dma((s.slots,))),
         ("lsem", dma((9,))),
+        ("osem", dma((7,))),
+        ("smallest", V((s.SR, LANES), F32)),
         ("smr", dma((s.W,))),
         ("wu", dma((4, s.W))),
         ("wd", dma((4, s.W))),
@@ -185,7 +188,7 @@
         ("n1", dma((s.C,))),
         ("nu", dma((s.W, s.C))),
         ("nd", dma((s.W, s.C))),
-        ("t1", dma((s.C,))),
+        ("t1", dma),
         ("t2", dma((s.W,))),
         ("hz", dma((s.W,))),
         ("hp", dma),
@@ -207,7 +210,8 @@
         ("x_wd", dma((4, s.W))),
         ("x_wb", dma((4,))),
         ("x_wc", dma((4,))),
-        ("x_d1", dma((3,))),
+        ("x_d1", dma((2,))),
+        ("x_t1", dma),
         ("x_t2", dma),
         ("x_gu", dma((s.W,))),
         ("x_gd", dma((s.W,))),
@@ -226,11 +230,17 @@
         ("x_rd", dma((5,))),
         ("credit", pltpu.SemaphoreType.REGULAR),
     ] + (
-        [("gst", V((s.W * s.pr, s.half), BF))]
+        [("gst", V((s.W * s.pr, s.half), BF)), ("unpadded", V((4, s.SR, s.D), BF))]
         + [(name, V((s.R, width), F32)) for name, width in arrivals(s)]
         if s.padded
         else [
             ("GR", V(pieces_shape(s), BF)),
+            ("GX", V((4, 2, 2, s.W * s.pr // 2, s.half), BF)),
+            ("GY", V((4, s.W * s.pr, s.half), BF)),
+            ("gx", dma((4, 2))),
+            ("gy", dma((4, 2))),
+            ("x_gx", dma((4, 2))),
+            ("x_gy", dma((4, 2))),
             ("RS", V((s.W, s.R, s.D), BF)),
             ("Rin", V((s.W + 1, s.R, s.D), BF)),
         ]
@@ -272,6 +282,11 @@
 
     def sent(ref, sem):
         remote(ref, ref, sem, sem, sib).wait_send()
+
+    barrier = pltpu.get_barrier_semaphore()
+    peers = [(flip(e, o), z) for o in range(1, E)] + [zpeer(o) for o in range(1, W)]
+    for peer in peers:
+        pl.semaphore_signal(barrier, inc=1, device_id=peer, device_id_type=MESH)
 
     shards = (r.w0, r.w1, r.w2, r.w3)
     own_rows = pl.ds(aligned(z * s.SR, 16), s.SR)
@@ -291,11 +306,6 @@
     r.smf[s.NX + 1 : s.NX + 2, 0 : s.SR] = r.gain_ffn[...].astype(F32).reshape(1, s.SR)
     r.smf[s.P1 : s.P1 + s.NBH, 0 : s.H] = r.bias[...].astype(F32)
     r.smg[z] = r.smf[...].astype(BF)
-
-    barrier = pltpu.get_barrier_semaphore()
-    peers = [(flip(e, o), z) for o in range(1, E)] + [zpeer(o) for o in range(1, W)]
-    for peer in peers:
-        pl.semaphore_signal(barrier, inc=1, device_id=peer, device_id_type=MESH)
     pl.semaphore_wait(barrier, len(peers))
 
     team_c = lax.rem(c, s.team)
@@ -401,7 +411,7 @@
 
     g_line = (r.gu, r.gd, r.x_gu, r.x_gd)
     n_line = (r.nu, r.nd, r.x_nu, r.x_nd)
-    Ga, Na, Ta = (r.Gr, r.Nr, r.Tr) if s.dt == BF else (r.Ga, r.Na, r.Ta)
+    Ga, Na = (r.Gr, r.Nr) if s.dt == BF else (r.Ga, r.Na)
     load_og.wait()
     dispatch(0, r.gsend, Ga, r.g1, r.og[...])
 
@@ -545,22 +555,27 @@
     router = raised / jnp.sum(raised, axis=1, keepdims=True)
     picked = (lane_row.astype(F32) == id_col).astype(F32)
     gate = jnp.sum(router * picked, axis=1, keepdims=True)
-    gate_high, gate_rest = two_parts(gate)
-    gate_mid, gate_low = two_parts(gate - gate_high.astype(F32))
-    gate_lanes = jnp.where(
-        lane_row == 0,
-        gate_high.astype(F32),
-        jnp.where(lane_row == 1, gate_mid.astype(F32), jnp.where(lane_row == 2, gate_low.astype(F32), 0.0)),
-    )
-    dispatch(2, r.tsend, Ta, r.t1, gate_lanes.astype(BF))
+    slot_gates = jnp.sum(jnp.where(r.pt[...] > 0, gate, 0.0), axis=0, keepdims=True)
+    r.Qs[...] = jnp.broadcast_to(slot_gates, r.Qs.shape)
+    r.Qk[e] = r.Qs[...]
+    for o in range(1, E):
+        remote(r.Qs, r.Qk.at[e], r.x_t1, r.t1, (flip(e, o), z)).start()
     if W > 2:
         line_pass(r.Gr, 2, *g_line)
     line_own(r.Nr, Na, r.n1, *n_line)
-    for oc in range(C):
-        landed(r.Tr, Ta, r.t1, oc)
-        for o in range(1, W):
-            part = r.Tr.at[block_at(z, oc)]
-            remote(part, part, r.x_t2, r.t2.at[o], zpeer(o)).start()
+    got(r.Qk.at[pl.ds(0, E - 1)], r.t1)
+    repeated = jnp.concatenate(
+        [jnp.broadcast_to(r.Qk[x, 0:1, :], (cp, s.S)) for x in range(E)], axis=0
+    )
+    wanted = e * cp + lax.rem(iota((R, s.S), 0), cp)
+    gate_col = jnp.sum(
+        jnp.where(iota((R, s.S), 1) == wanted, repeated, 0.0), axis=1, keepdims=True
+    )
+    diagonal = iota((R, R), 0) == iota((R, R), 1)
+    gate_line = jnp.sum(jnp.where(diagonal, gate_col, 0.0), axis=0, keepdims=True)
+    r.Qr[z] = jnp.broadcast_to(gate_line, (8, R))
+    for o in range(1, W):
+        remote(r.Qr.at[z], r.Qr.at[z], r.x_t2, r.t2.at[o], zpeer(o)).start()
     turn_out(1, mixed, r.mT)
 
     load_wo.wait()
@@ -596,7 +611,6 @@
         part = jnp.sum(
             r.act[at, :].astype(F32) * r.agr[at, :].astype(F32), axis=1, keepdims=True
         )
-        diagonal = iota((R, R), 0) == iota((R, R), 1)
         r.HS[plane, 0:1, :] = jnp.sum(jnp.where(diagonal, part, 0.0), axis=0, keepdims=True)
 
         @pl.when(plane != z)
@@ -832,6 +846,10 @@
     share(3, r.att)
     r.mixed[...] = dot_rt(attended_grad, r.wfull[3]).astype(BF)
     router_grad = dot_lt(logit_grad, r.nf[...])
+    two_step = C == 4 and not s.padded
+    half_rows = W * s.pr // 2
+    row_sides = (pl.ds(0, half_rows), pl.ds(half_rows, half_rows))
+
     def plane_sum(m, left, source):
         got(r.fac.at[m], r.sibF.at[m])
 
@@ -846,10 +864,41 @@
             return carry
 
         lax.fori_loop(0, W, block, 0)
+        if two_step:
+            for side in range(2):
+                near, far = 1 + side, 2 - side
+                for slot, oc in enumerate((near, near + far)):
+                    remote(
+                        r.GS.at[m, flip(c, oc), row_sides[side]],
+                        r.GX.at[m, side, slot],
+                        r.x_gx.at[m, side],
+                        r.gx.at[m, side],
+                        cpeer(near),
+                    ).start()
+            return
         for oc in range(1, C):
             remote(
                 r.GS.at[m, flip(c, oc)], r.GR.at[m, oc - 1], r.x_ra.at[m], r.ra.at[m], cpeer(oc)
             ).start()
+
+    def plane_fold(m):
+        if not two_step:
+            return
+        for side in range(2):
+            far, rows = 2 - side, row_sides[side]
+            got(r.GX.at[m, side], r.gx.at[m, side])
+            for slot, chip in ((1, flip(c, far)), (0, c)):
+                r.GS[m, chip, rows, :] = (
+                    r.GS[m, chip, rows, :].astype(F32) + r.GX[m, side, slot].astype(F32)
+                ).astype(BF)
+                if slot:
+                    remote(
+                        r.GS.at[m, chip, rows],
+                        r.GY.at[m, rows],
+                        r.x_gy.at[m, side],
+                        r.gy.at[m, side],
+                        cpeer(far),
+                    ).start()
 
     low_side = lane_row < s.HD
 
@@ -886,12 +935,19 @@
     lax.fori_loop(0, s.H // 2, attend_back, 0)
     share(0, r.dq)
     share(1, r.dk)
+    plane_fold(3)
+    plane_fold(2)
     next_pass()
 
     def shard_sum(m):
-        got(r.GR.at[m], r.ra.at[m])
         total = r.GS[m, c].astype(F32)
-        for oc in range(1, C):
+        if two_step:
+            for side in range(2):
+                got(r.GY.at[m, row_sides[side]], r.gy.at[m, side])
+            total = total + r.GY[m].astype(F32)
+        else:
+            got(r.GR.at[m], r.ra.at[m])
+        for oc in range(1, 1 if two_step else C):
             if s.padded:
                 fetch = pltpu.make_async_copy(r.GR.at[m, oc - 1], r.gst, r.lsem.at[8])
                 fetch.start()
@@ -931,12 +987,14 @@
     shard_sum(3)
     x = r.xb[...].astype(F32)
     along = normed_grad * r.rows[0:1, :]
-    r.tokens_grad[...] = (
+    r.mg[...] = (
         r.mg[...]
         + scale1 * along
         - x * (scale1 * scale1 * scale1 * jnp.mean(along * x, axis=1, keepdims=True))
     )
     r.rows[3:4, :] = jnp.sum(normed_grad * x * scale1, axis=0, keepdims=True)
+    save_tokens = pltpu.make_async_copy(r.mg, r.tokens_grad, r.osem.at[0])
+    save_tokens.start()
     r.bt[...] = jnp.zeros_like(r.bt)
     mirror = (iota((T, T), 0) + iota((T, T), 1) == T - 1).astype(F32).astype(BF)
 
@@ -950,6 +1008,7 @@
     lax.fori_loop(0, s.H, bias_back, 0)
     plane_sum(1, r.nT, r.dk)
     shard_sum(2)
+    plane_fold(0)
     high, rest = two_parts(r.bt[...])
     rel_grad = dot_rt(r.ohm[...], high) + dot_rt(r.ohm[...], rest)
     lane_col = iota((LANES, 1), 0)
@@ -977,11 +1036,11 @@
         remote(r.hGS.at[flip(c, oc)], r.hGR.at[oc - 1], r.x_ra.at[4], r.ra.at[4], cpeer(oc)).start()
     line_sent(r.Gr, r.x_gu, r.x_gd)
     for o in range(1, W):
-        got(r.Tr.at[pl.ds(0, R)], r.t2.at[o])
+        got(r.Qr.at[0], r.t2.at[o])
 
     def scale_rows(step, carry):
         at = pl.ds(aligned(step * R, 16), R)
-        gates = jnp.sum(r.Tr[at, :].astype(F32), axis=1, keepdims=True)
+        gates = jnp.sum(jnp.where(diagonal, r.Qr[step, 0:1, :], 0.0), axis=1, keepdims=True)
         r.Gr[at, :] = (r.Gr[at, :].astype(F32) * gates).astype(BF)
         r.ig[at, :] = (r.ig[at, :].astype(F32) * gates).astype(BF)
         return carry
@@ -1020,6 +1079,7 @@
         return carry
 
 
+    plane_fold(1)
     lax.fori_loop(0, s.F // tile, grad_out_tile, 0)
     shard_sum(0)
     spread(2)
@@ -1061,7 +1121,9 @@
         remote(part, part, r.x_rc.at[4], r.rc.at[4], cpeer(oc)).start()
 
     got(r.Rk.at[pl.ds(0, (E - 1) * cp)], r.back.at[1])
-    r.layer_out[...] = (r.middle[...] + gate * dot(r.pt[...], r.Rk[...].astype(BF))).astype(BF)
+    r.nf[...] = (r.middle[...] + gate * dot(r.pt[...], r.Rk[...].astype(BF))).astype(BF)
+    save_layer = pltpu.make_async_copy(r.nf, r.layer_out, r.osem.at[1])
+    save_layer.start()
 
     share_sum(1)
     got(r.hFG.at[pl.ds(0, (C - 1) * s.pr)], r.rc.at[4])
@@ -1069,11 +1131,20 @@
     def unpad(value):
         return dot(r.unsel[...], value) if s.padded else value.astype(F32)
 
-    r.smalls[...] = unpad(r.hFG[...])
-    for m in (3, 0, 1, 2):
+    r.smallest[...] = unpad(r.hFG[...])
+    saves = [save_tokens, save_layer, pltpu.make_async_copy(r.smallest, r.smalls, r.osem.at[2])]
+    saves[-1].start()
+    for m in (3, 2, 0, 1):
         got(r.FG.at[m, :, there], r.rd.at[m])
-        r.grads[m] = unpad(r.FG[m]).astype(r.grads.dtype)
-
+        complete = r.FG.at[m]
+        if s.padded:
+            r.unpadded[m] = unpad(r.FG[m]).astype(BF)
+            complete = r.unpadded.at[m]
+        saves.append(pltpu.make_async_copy(complete, r.grads.at[m], r.osem.at[3 + m]))
+        saves[-1].start()
+
+    for save in saves:
+        save.wait()
     for step in range(max(0, s.F // tile - slots), s.F // tile):
         save_out(step).wait()
     for step in range(max(0, D // tile - slots), D // tile):
@@ -1088,14 +1159,20 @@
             sent(r.wfull.at[m, pl.ds(0, (W - 1) * (s.team - 1) * s.pw), here], r.x_wb.at[m])
         sent(r.wfull.at[m, others, here], r.x_wc.at[m])
         sent(r.fac.at[m], r.x_sibF.at[m])
-        sent(r.GR.at[m], r.x_ra.at[m])
+        if two_step:
+            for side in range(2):
+                sent(r.GX.at[m, side], r.x_gx.at[m, side])
+                sent(r.GY.at[m, row_sides[side]], r.x_gy.at[m, side])
+        else:
+            sent(r.GR.at[m], r.x_ra.at[m])
         sent(r.ZR.at[m], r.x_rb.at[m])
         sent(r.FG.at[m, pl.ds(0, (C - 1) * s.pr), here], r.x_rc.at[m])
         sent(r.FG.at[m, :, here], r.x_rd.at[m])
-    for index, buffer in enumerate((r.gsend, r.nsend, r.tsend)):
+    sent(r.Qk.at[pl.ds(0, E - 1)], r.x_t1)
+    for index, buffer in enumerate((r.gsend, r.nsend)):
         sent(buffer.at[pl.ds(0, E - 1)], r.x_d1.at[index])
     line_sent(r.Nr, r.x_nu, r.x_nd)
-    sent(r.Tr.at[pl.ds(0, (W - 1) * R)], r.x_t2)
+    sent(r.Qr.at[pl.ds(0, W - 1)], r.x_t2)
     for d in range(1, W):
         if early:
             pl.when(z >= d)(functools.partial(sent, r.SS.at[0], r.x_sd.at[d]))
@@ -1242,7 +1319,7 @@
             *spilled,
         ),
         in_specs=in_specs,
-        out_specs=(vmem, vmem, vmem, vmem, anywhere, anywhere) + (anywhere,) * len(spilled),
+        out_specs=(anywhere,) * (6 + len(spilled)),
         scratch_shapes=[shape for _, shape in scratch],
         compiler_params=pltpu.CompilerParams(
             collective_id=0, has_side_effects=True, vmem_limit_bytes=62 * 2**20

time: 165 us -> 157 us (0.952)
  Pallas kernels: 164 us -> 156 us
    pallas_call x1, Pallas kernels: 157 us -> 149 us  [local(): pl.pallas_call(functools.partial(kernel, s, names), name='layer', out_sha...]
where the time goes in v6:
time: 157 us
  Pallas kernels  156 us (99%)
    pallas_call x1, Pallas kernels, local(): pl.pallas_call(functools.partial(kernel, s, names), name='layer', out_sha...  149 us
    pallas_call x1, Pallas kernels, local(): pl.pallas_call(functools.partial(finish, s), name='finish', out_shape=(ja...  7.07 us

profile of v6, /device:TPU:0, one launch (start us, length us, event | category | flops | bytes accessed | tf_op | source)
XLA Modules:
  0.0 156.6 jit_solution(1829578407704386618)
XLA Ops:
  0.7 148.7 %layer.1 = (bf16[256,768]{1,0:T(8,128)(2,1)}, f32[256,768]{1,0:T(8,128)}, bf16[4,192,768]{2,1,0:T(8,128)(2,1)}, f32[192,128]{1,0:T(8,128)}, bf16[768,768]{1,0:T(8,128)(2,1)}, /*index=5*/bf16[768,768]{1,0:T(8,128)(2,1)}) custom-call(s32[64]{0:T(128)} %refs_0_.1, s32[64]{0:T(128)} %refs_1_.1, s32[1,256]{1,0:T(1,128)} %bitcast.9, s32[1,256]{1,0:T(1,128)} %bitcast.10, ...), custom_call_target="tpu_custom_call" | custom-call | tf_op jit(solution)/shard_map/layer/pallas_call | solution.py:1309
  149.4 7.1 %finish.1 = (bf16[256,768]{1,0:T(8,128)(2,1)}, f32[256,768]{1,0:T(8,128)}, f32[192,768]{1,0:T(8,128)}, f32[192,768]{1,0:T(8,128)}, f32[192,768]{1,0:T(8,128)}, /...) custom-call(bf16[256,768]{1,0:T(8,128)(2,1)} %get-tuple-element.30.r, ...), custom_call_target="tpu_custom_call" | custom-call | tf_op jit(solution)/shard_map/finish/pallas_call | solution.py:1328

commit v7 on v6

--- a/solution.py
+++ b/solution.py
@@ -306,27 +306,6 @@
     r.smf[s.NX + 1 : s.NX + 2, 0 : s.SR] = r.gain_ffn[...].astype(F32).reshape(1, s.SR)
     r.smf[s.P1 : s.P1 + s.NBH, 0 : s.H] = r.bias[...].astype(F32)
     r.smg[z] = r.smf[...].astype(BF)
-    pl.semaphore_wait(barrier, len(peers))
-
-    team_c = lax.rem(c, s.team)
-    for o in range(1, W):
-        remote(r.smg.at[z], r.smg.at[z], r.x_sm, r.smr.at[o], zpeer(o)).start()
-    share_rows = pl.ds(aligned(team_c * s.pw, 16), s.pw)
-    def weight_at(plane):
-        return pl.ds(aligned(plane * s.SR + team_c * s.pw, 16), s.pw)
-
-    def weight_own(m):
-        def send(sender, receiver, to):
-            source = shards[m].at[share_rows, here]
-            remote(source, r.wfull.at[m, weight_at(z), here], sender, receiver, (e, to)).start()
-
-        pl.when(z < W - 1)(functools.partial(send, r.x_wu.at[m, 0], r.wu.at[m, 1], z + 1))
-        pl.when(z > 0)(functools.partial(send, r.x_wd.at[m, 0], r.wd.at[m, 1], z - 1))
-
-    for m in range(3):
-        weight_own(m)
-    for copy in (load_x, *load_w, load_wo, load_wi):
-        copy.start()
     device = e * W + z
     first = r.lengths[r.seq[2 * device]]
     both = first + r.lengths[r.seq[2 * device + 1]]
@@ -349,13 +328,38 @@
     r.pm[...] = (iota((s.S, T), 0).astype(F32) == flat_row).astype(F32).astype(BF)
     r.pt[...] = (iota((T, s.S), 1).astype(F32) == flat_col).astype(F32).astype(BF)
 
+    def fill(send, value):
+        send[...] = dot(r.pm[...], value).astype(s.dt).reshape(send.shape)
+
+    load_og.wait()
+    fill(r.gsend, r.og[...])
+    pl.semaphore_wait(barrier, len(peers))
+
+    team_c = lax.rem(c, s.team)
+    for o in range(1, W):
+        remote(r.smg.at[z], r.smg.at[z], r.x_sm, r.smr.at[o], zpeer(o)).start()
+    share_rows = pl.ds(aligned(team_c * s.pw, 16), s.pw)
+    def weight_at(plane):
+        return pl.ds(aligned(plane * s.SR + team_c * s.pw, 16), s.pw)
+
+    def weight_own(m):
+        def send(sender, receiver, to):
+            source = shards[m].at[share_rows, here]
+            remote(source, r.wfull.at[m, weight_at(z), here], sender, receiver, (e, to)).start()
+
+        pl.when(z < W - 1)(functools.partial(send, r.x_wu.at[m, 0], r.wu.at[m, 1], z + 1))
+        pl.when(z > 0)(functools.partial(send, r.x_wd.at[m, 0], r.wd.at[m, 1], z - 1))
+
+    for m in range(3):
+        weight_own(m)
+    for copy in (load_x, *load_w, load_wo, load_wi):
+        copy.start()
     plane_step = 16 if s.dt == BF else 8
     plane_rows = z * R if s.dt == BF else 0
 
     def dispatch(index, send, rows, first_sem, value):
-        width = rows.shape[1]
-        buffer = dot(r.pm[...], value)
-        send[...] = buffer.astype(s.dt).reshape(s.NX, cp, width)
+        if value is not None:
+            fill(send, value)
         mine = pl.ds(aligned(plane_rows + e * cp, plane_step), cp)
         for o in range(1, E):
             x = flip(e, o)
@@ -412,8 +416,7 @@
     g_line = (r.gu, r.gd, r.x_gu, r.x_gd)
     n_line = (r.nu, r.nd, r.x_nu, r.x_nd)
     Ga, Na = (r.Gr, r.Nr) if s.dt == BF else (r.Ga, r.Na)
-    load_og.wait()
-    dispatch(0, r.gsend, Ga, r.g1, r.og[...])
+    dispatch(0, r.gsend, Ga, r.g1, None)
 
     def weight_pass(m, d):
         def handle(plane, arrived, onward, sender, receiver, to, beside):
@@ -778,9 +781,11 @@
 
         if step == W - 1:
             if early:
+                pass
+            lax.fori_loop(0, W, gate_sums, 0)
+            if early:
                 results_begin()
                 next_pass()
-            lax.fori_loop(0, W, gate_sums, 0)
 
     for oc in range(C):
         block = block_at(0, oc)
@@ -909,7 +914,7 @@
         r.dv[:, cols] = jnp.where(low_side, outs[0], outs[1]).astype(BF)
         return carry
 
-    lax.fori_loop(0, s.H // 2, values_back, 0)
+    lax.fori_loop(0, s.H // 2, values_back, 0, unroll=2)
     share(2, r.dv)
     got(r.mT.at[:, pl.ds(T, T)], r.sibT.at[1])
     plane_sum(3, r.mT, r.att)
@@ -932,7 +937,7 @@
         r.dk[:, cols] = jnp.where(low_side, outs[0][1], outs[1][1]).astype(BF)
         return carry
 
-    lax.fori_loop(0, s.H // 2, attend_back, 0)
+    lax.fori_loop(0, s.H // 2, attend_back, 0, unroll=2)
     share(0, r.dq)
     share(1, r.dk)
     plane_fold(3)
@@ -1239,6 +1244,8 @@
                 pltpu.make_async_copy(high.at[at], target.at[0, at], save2.at[index, part])
             )
             steps.append((low, high, at))
+    order = [6, 9, 7, 10, 8, 11, 2, 3, 4, 5, 1, 0]
+    loads, saves, steps = ([items[at] for at in order] for items in (loads, saves, steps))
     for copy in loads:
         copy.start()
     turned = smalls[...].T

time: 157 us -> 154 us (0.981)
  Pallas kernels: 156 us -> 153 us
where the time goes in v7:
time: 154 us
  Pallas kernels  153 us (99%)
    pallas_call x1, Pallas kernels, local(): pl.pallas_call(functools.partial(kernel, s, names), name='layer', out_sha...  147 us
    pallas_call x1, Pallas kernels, local(): pl.pallas_call(functools.partial(finish, s), name='finish', out_shape=(ja...  6.01 us

profile of v7, /device:TPU:0, one launch (start us, length us, event | category | flops | bytes accessed | tf_op | source)
XLA Modules:
  0.0 154.3 jit_solution(6091789395432241388)
XLA Ops:
  0.7 147.4 %layer.1 = (bf16[256,768]{1,0:T(8,128)(2,1)}, f32[256,768]{1,0:T(8,128)}, bf16[4,192,768]{2,1,0:T(8,128)(2,1)}, f32[192,128]{1,0:T(8,128)}, bf16[768,768]{1,0:T(8,128)(2,1)}, /*index=5*/bf16[768,768]{1,0:T(8,128)(2,1)}) custom-call(s32[64]{0:T(128)} %refs_0_.1, s32[64]{0:T(128)} %refs_1_.1, s32[1,256]{1,0:T(1,128)} %bitcast.9, s32[1,256]{1,0:T(1,128)} %bitcast.10, ...), custom_call_target="tpu_custom_call" | custom-call | tf_op jit(solution)/shard_map/layer/pallas_call | solution.py:1316
  148.1 6.0 %finish.1 = (bf16[256,768]{1,0:T(8,128)(2,1)}, f32[256,768]{1,0:T(8,128)}, f32[192,768]{1,0:T(8,128)}, f32[192,768]{1,0:T(8,128)}, f32[192,768]{1,0:T(8,128)}, /...) custom-call(bf16[256,768]{1,0:T(8,128)(2,1)} %get-tuple-element.30.r, ...), custom_call_target="tpu_custom_call" | custom-call | tf_op jit(solution)/shard_map/finish/pallas_call | solution.py:1335

commit v8 on v7

--- a/solution.py
+++ b/solution.py
@@ -90,7 +90,7 @@
     s.CP = s.C * s.pr
     s.Dp = s.W * s.CP
     s.padded = s.CP != s.SR
-    s.tile = LANES
+    s.tile = 2 * LANES if hidden % (2 * LANES) == 0 and width % (2 * LANES) == 0 else LANES
     s.slots = 2 if s.padded else max(width, hidden) // s.tile
     return s
 
@@ -868,7 +868,7 @@
                 ]
             return carry
 
-        lax.fori_loop(0, W, block, 0)
+        lax.fori_loop(0, W, block, 0, unroll=2)
         if two_step:
             for side in range(2):
                 near, far = 1 + side, 2 - side

time: 154 us -> 153 us (level)
  no operation moved by 1% of the time
where the time goes in v8:
time: 153 us
  Pallas kernels  152 us (99%)
    pallas_call x1, Pallas kernels, local(): pl.pallas_call(functools.partial(kernel, s, names), name='layer', out_sha...  146 us
    pallas_call x1, Pallas kernels, local(): pl.pallas_call(functools.partial(finish, s), name='finish', out_shape=(ja...  6.01 us

profile of v8, /device:TPU:0, one launch (start us, length us, event | category | flops | bytes accessed | tf_op | source)
XLA Modules:
  0.0 153.0 jit_solution(11563129768130880332)
XLA Ops:
  0.7 146.2 %layer.1 = (bf16[256,768]{1,0:T(8,128)(2,1)}, f32[256,768]{1,0:T(8,128)}, bf16[4,192,768]{2,1,0:T(8,128)(2,1)}, f32[192,128]{1,0:T(8,128)}, bf16[768,768]{1,0:T(8,128)(2,1)}, /*index=5*/bf16[768,768]{1,0:T(8,128)(2,1)}) custom-call(s32[64]{0:T(128)} %refs_0_.1, s32[64]{0:T(128)} %refs_1_.1, s32[1,256]{1,0:T(1,128)} %bitcast.9, s32[1,256]{1,0:T(1,128)} %bitcast.10, ...), custom_call_target="tpu_custom_call" | custom-call | tf_op jit(solution)/shard_map/layer/pallas_call | solution.py:1316
  146.9 6.0 %finish.1 = (bf16[256,768]{1,0:T(8,128)(2,1)}, f32[256,768]{1,0:T(8,128)}, f32[192,768]{1,0:T(8,128)}, f32[192,768]{1,0:T(8,128)}, f32[192,768]{1,0:T(8,128)}, /...) custom-call(bf16[256,768]{1,0:T(8,128)(2,1)} %get-tuple-element.30.r, ...), custom_call_target="tpu_custom_call" | custom-call | tf_op jit(solution)/shard_map/finish/pallas_call | solution.py:1335
